TPU v7x, 1024 devices: a whole 4x4x32 slice. The times are simulated.
1024 devices in a mesh: expert: 64 (over z, core), dp: 16 (over x, y).
Axes of the slice: x: 4, y: 4, z: 32, core: 2. Of those that a mesh axis runs over, the one named last changes fastest.
Arguments:
- tokens: bfloat16 [8192, 2048], P('expert', 'dp'), may hold values from -6 to 6
- expert_ids: int32 [8192, 8], P('expert'), may hold values from 0 to 63, all different within a row; in each aligned block of 128 rows (0 to 127, 128 to 255, ...) at most 32 rows name the same one
- gate_weight: bfloat16 [64, 2048, 384], P('expert', 'dp'), may hold values from -0.125 to 0.125
- up_weight: bfloat16 [64, 2048, 384], P('expert', 'dp'), may hold values from -0.125 to 0.125
- hidden_grad: bfloat16 [64, 2048, 384], P('expert', 'dp'), may hold values from -6 to 6
Outputs:
- hidden: bfloat16 [64, 2048, 384], P('expert', 'dp')
- gate_grad: float32 [64, 2048, 384], P('expert', 'dp')
- up_grad: float32 [64, 2048, 384], P('expert', 'dp')
- token_grad: bfloat16 [8192, 2048], P('expert', 'dp')
Inputs may be any that keep to these rules, and one draw needn't show every extreme that they name: `expert_ids`: each row names 8 different experts; among the 128 rows of one source no expert is named by more than 32 rows, a bound that some block reaches.
All inputs are finite; a program needn't handle non-finite values.
Results may differ from a plain program's by a relative error of at most 0.015.
Values may be sent and summed in bfloat16 or wider, within the bound.
No kernel may reach another device: no remote copies, remote signals or barrier semaphores. Data moves between devices by JAX's collectives and lax.ppermute only.
A program may use at most 32 MiB of HBM per device.

v0:
```python
import jax
import jax.numpy as jnp
from jax import lax
from jax.sharding import PartitionSpec as P


def on_device(tokens, expert_ids, gate_weight, up_weight, hidden_grad):
    n_src = lax.axis_size("expert")
    n_dp = lax.axis_size("dp")
    tok_rows = tokens.shape[0]
    width_part = tokens.shape[1]
    top_k = expert_ids.shape[1]
    share_rows = hidden_grad.shape[1]
    capacity = share_rows * n_dp // n_src
    slot_total = n_src * capacity
    hidden_units = gate_weight.shape[2]
    rows_dev = gate_weight.shape[1]
    flat_ids = expert_ids.reshape(tok_rows * top_k)
    onehot = (flat_ids[:, None] == jnp.arange(n_src, dtype=jnp.int32)[None, :]).astype(jnp.int32)
    ranks = jnp.sum((jnp.cumsum(onehot, axis=0) - onehot) * onehot, axis=1)
    slot_index = (flat_ids * capacity + ranks).reshape(tok_rows, top_k)
    slot_iota = jnp.arange(slot_total, dtype=jnp.int32)[None, :]
    placer = jnp.zeros((tok_rows, slot_total), jnp.bfloat16)
    for choice_k in range(top_k):
        placer = placer + (slot_index[:, choice_k : choice_k + 1] == slot_iota).astype(jnp.bfloat16)
    outgoing = lax.dot_general(
        placer, tokens, (((0,), (0,)), ((), ())), preferred_element_type=jnp.float32
    )
    outgoing = outgoing.astype(jnp.bfloat16).reshape(n_src, capacity, width_part)
    arrived = lax.all_to_all(
        lax.all_to_all(outgoing, "expert", split_axis=0, concat_axis=0, tiled=True),
        "dp",
        split_axis=0,
        concat_axis=2,
        tiled=True,
    )
    width = arrived.shape[2]
    slot_rows = arrived.reshape(share_rows, width)
    gate_full, up_full = (
        lax.all_gather(gate_weight[0], "dp", axis=0, tiled=True),
        lax.all_gather(up_weight[0], "dp", axis=0, tiled=True),
    )
    gate = jnp.dot(slot_rows, gate_full, preferred_element_type=jnp.float32)
    up = jnp.dot(slot_rows, up_full, preferred_element_type=jnp.float32)
    sigmoid_gate = jax.nn.sigmoid(gate)
    silu_gate = gate * sigmoid_gate
    hidden = (silu_gate * up).astype(jnp.bfloat16)
    delta = hidden_grad[0].astype(jnp.float32)
    gate_delta = (delta * up * sigmoid_gate * (1.0 + gate * (1.0 - sigmoid_gate))).astype(
        jnp.bfloat16
    )
    up_delta = (delta * silu_gate).astype(jnp.bfloat16)
    both_delta = jnp.concatenate([gate_delta, up_delta], axis=1)
    summed = lax.psum_scatter(
        lax.dot_general(
            slot_rows, both_delta, (((0,), (0,)), ((), ())), preferred_element_type=jnp.float32
        ).astype(jnp.bfloat16),
        "dp",
        scatter_dimension=0,
        tiled=True,
    ).astype(jnp.float32)
    first = lax.dot_general(
        gate_delta, gate_full, (((1,), (1,)), ((), ())), preferred_element_type=jnp.float32
    )
    second = lax.dot_general(
        up_delta, up_full, (((1,), (1,)), ((), ())), preferred_element_type=jnp.float32
    )
    slot_grad = (first + second).astype(jnp.bfloat16).reshape(n_src // n_dp, capacity, width)
    returned = lax.all_to_all(
        lax.all_to_all(slot_grad, "dp", split_axis=2, concat_axis=0, tiled=True),
        "expert",
        split_axis=0,
        concat_axis=0,
        tiled=True,
    )
    gate_grad = summed[:, :hidden_units].reshape(1, rows_dev, hidden_units)
    up_grad = summed[:, hidden_units:].reshape(1, rows_dev, hidden_units)
    token_grad = jnp.dot(
        placer, returned.reshape(slot_total, width_part), preferred_element_type=jnp.float32
    ).astype(jnp.bfloat16)
    return (hidden.reshape(1, share_rows, hidden_units), gate_grad, up_grad, token_grad)


def solution(mesh):
    placed = (
        P("expert", "dp"),
        P("expert", None),
        P("expert", "dp", None),
        P("expert", "dp", None),
        P("expert", "dp", None),
    )
    return jax.shard_map(
        on_device,
        mesh=mesh,
        in_specs=placed,
        out_specs=(
            P("expert", "dp", None),
            P("expert", "dp", None),
            P("expert", "dp", None),
            P("expert", "dp"),
        ),
        check_vma=False,
    )
```

profile of v0, /device:TPU:1, one launch (start us, length us, event | category | flops | bytes accessed | tf_op | source)
XLA Modules:
  0.0 311.1 jit_solution(18306276494269950496)
XLA Ops:
  7.2 0.0 copy-start
  7.2 0.0 copy-start.3
  7.2 0.0 all-gather.7.cloned.1.call-start
  7.2 0.7 all-gather.7.cloned.1.call-update
  7.9 0.8 copy.33
  8.7 0.1 eq.149
  8.8 0.1 eq.145
  8.9 18.0 %reduce-window.6 = s32[64,8,128]{2,1,0:T(8,128)S(1)} reduce-window(s32[64,8,128]{2,1,0:T(8,128)S(1)} %fusion.32, s32[]{:T(128)} %constant.8.clone.1), window={size=1x1x128 pad=0_0x0_0x127_0}, to_apply=%region_0.0 | reduce-window | flops 8323072 | bytes 524292 | tf_op jit(solution)/shard_map/reduce-window
  26.9 0.1 slice.48
  27.1 0.1 copy.35
  27.3 0.1 copy.36
  27.3 0.1 broadcast_add_fusion
  27.5 0.1 fusion.31
  27.6 0.1 reduce_sum.12
  27.7 0.0 copy-done.3
  27.7 0.0 copy-done
  27.7 2.1 convolution_convert_fusion.1
  29.9 30.4 %all-to-all-start = ((bf16[64,32,128]{2,1,0:T(8,128)(2,1)}), bf16[64,32,128]{2,1,0:T(8,128)(2,1)S(1)}, u32[]{:S(2)}, u32[]{:S(2)}) async-start(bf16[64,32,128]{2,1,0:T(8,128)(2,1)} %bitcast.10), calls=%async_computation | async-start | bytes 1048576 | tf_op jit(solution)/shard_map/all_to_all | solution.py:31
  60.3 0.0 all-gather.5.cloned.1.call-start
  60.3 0.7 all-gather.5.cloned.1.call-update
  61.0 0.0 reduce-scatter.2.cloned.1.call-start
  61.1 63.3 %all-to-all-done = bf16[64,32,128]{2,1,0:T(8,128)(2,1)S(1)} async-done(((bf16[64,32,128]{2,1,0:T(8,128)(2,1)}), bf16[64,32,128]{2,1,0:T(8,128)(2,1)S(1)}, u32[]{:S(2)}, u32[]{:S(2)}) %all-to-all-start) | async-done | bytes 524320 | tf_op jit(solution)/shard_map/all_to_all | solution.py:31
  124.3 15.7 %all_to_all.43 = bf16[64,32,128]{2,1,0:T(8,128)(2,1)S(1)} all-to-all(bf16[64,32,128]{2,1,0:T(8,128)(2,1)S(1)} %all-to-all-done), channel_id=1, replica_groups=mesh['expert'=64,'dp'=16] {'dp'}, dimensions={0} | all-to-all | bytes 1048576 | tf_op jit(solution)/shard_map/all_to_all | solution.py:30
  140.0 0.0 copy-start.4
  140.0 0.3 copy.38
  140.4 0.0 all-gather.7.cloned.1.call-done
  140.4 1.8 fusion.2
  142.2 40.8 %all-gather.5.cloned.1.call-done = bf16[1,2048,384]{2,1,0:T(8,128)(2,1)} async-done(((bf16[1,128,384]{2,1,0:T(8,128)(2,1)}), bf16[1,2048,384]{2,1,0:T(8,128)(2,1)}) %all-gather.5.cloned.1.call-update) | async-done | bytes 1572880 | tf_op jit(solution)/shard_map/all_gather | solution.py:40
  183.1 0.0 copy-done.4
  183.1 2.6 fusion.37
  185.6 2.7 convolution_convert_fusion
  188.3 0.0 copy-start.2
  188.3 0.0 reduce-scatter.2.cloned.1.call-update
  188.3 1.4 copy-done.2
  189.7 0.0 copy-start.1
  189.7 0.6 fusion.4
  190.3 0.8 copy-done.1
  191.1 0.6 fusion
  191.7 1.4 copy.39
  193.1 2.0 reshape.63
  195.1 13.7 %all_to_all.44 = bf16[16,2,8192]{2,1,0:T(2,128)(2,1)S(1)} all-to-all(bf16[16,2,8192]{2,1,0:T(2,128)(2,1)S(1)} %reshape.63), channel_id=1, replica_groups=mesh['expert'=64,'dp'=16] {'dp'}, dimensions={0} | all-to-all | bytes 1048576 | tf_op jit(solution)/shard_map/all_to_all | solution.py:70
  208.8 1.0 reshape.64
  209.8 1.0 copy.43
  210.8 90.2 %all_to_all.45 = bf16[64,32,128]{2,1,0:T(8,128)(2,1)S(1)} all-to-all(bf16[64,32,128]{2,1,0:T(8,128)(2,1)S(1)} %bitcast.90), channel_id=1, replica_groups=mesh['expert'=64,'dp'=16] {'expert'}, dimensions={0} | all-to-all | bytes 1048576 | tf_op jit(solution)/shard_map/all_to_all | solution.py:69
  301.0 1.9 convolution_convert_fusion.2
  302.8 0.0 reduce-scatter.2.cloned.1.call-done
  302.8 1.0 convert_element_type.78
  303.8 0.8 slice_bitcast_fusion
  (6 shorter events, 0.1 us)
Async XLA Ops:
  7.2 20.6 %copy-start = (bf16[128,128]{1,0:T(8,128)(2,1)S(1)}, bf16[128,128]{1,0:T(8,128)(2,1)}, u32[]{:S(2)}) copy-start(bf16[128,128]{1,0:T(8,128)(2,1)} %param.5) | copy-start | bytes 98308
  7.2 20.5 %copy-start.3 = (s32[128,8]{0,1:T(8,128)S(1)}, s32[128,8]{0,1:T(8,128)}, u32[]{:S(2)}) copy-start(s32[128,8]{0,1:T(8,128)} %param.6) | copy-start | bytes 12292
  7.2 133.2 %all-gather.7.cloned.1.call-start = ((), (), s32[]{:S(2)}) async-start(), calls=%async_computation.7 | async-start | bytes 1671168 | tf_op jit(solution)/shard_map/all_gather | solution.py:41
  29.9 94.5 %all-to-all-start = ((bf16[64,32,128]{2,1,0:T(8,128)(2,1)}), bf16[64,32,128]{2,1,0:T(8,128)(2,1)S(1)}, u32[]{:S(2)}, u32[]{:S(2)}) async-start(bf16[64,32,128]{2,1,0:T(8,128)(2,1)} %bitcast.10), calls=%async_computation | async-start | bytes 1048576 | tf_op jit(solution)/shard_map/all_to_all | solution.py:31
  60.3 122.8 %all-gather.5.cloned.1.call-start = ((), (), s32[]{:S(2)}) async-start(), calls=%async_computation.6 | async-start | bytes 1671168 | tf_op jit(solution)/shard_map/all_gather | solution.py:40
  61.0 241.8 %reduce-scatter.2.cloned.1.call-start = ((), (), s32[]{:S(2)}) async-start(), calls=%async_computation.5 | async-start | bytes 3342336 | tf_op jit(solution)/shard_map/reduce_scatter | solution.py:54
  140.0 43.0 %copy-start.4 = (bf16[1,128,384]{2,1,0:T(8,128)(2,1)S(1)}, bf16[1,128,384]{2,1,0:T(8,128)(2,1)}, u32[]{:S(2)}) copy-start(bf16[1,128,384]{2,1,0:T(8,128)(2,1)} %param.9) | copy-start | bytes 294916
  188.3 1.4 copy-start.2
  189.7 1.4 copy-start.1
Sparse Core Ops, SparseCore 0:
  12.2 87.1 all-gather.6
  103.7 79.3 all-gather.4
  188.4 110.7 reduce-scatter.1
where the time goes:
time: 312 us; the launch traced here: 311 us
  blocking collectives  120 us (38%)
  waiting for transfers between devices  105 us (34%)
  starting transfers between devices  30.5 us (10%)
  other arithmetic  19.2 us (6%)
  between operations  13.9 us (4%)
  matrix products  12.3 us (4%)
  local copies, waits for them, and re-layouts  10.1 us (3%)
    all_to_all x1, blocking collectives, on_device(): lax.all_to_all(lax.all_to_all(slot_grad, 'dp', split_axis=2, concat_axis=...  90.2 us
    all_to_all x1, waiting for transfers between devices, on_device(): lax.all_to_all(outgoing, 'expert', split_axis=0, concat_axis=0, tiled=True)  63.3 us
    all_gather x1, waiting for transfers between devices, on_device(): lax.all_gather(gate_weight[0], 'dp', axis=0, tiled=True)  40.8 us
    all_to_all x1, starting transfers between devices, on_device(): lax.all_to_all(outgoing, 'expert', split_axis=0, concat_axis=0, tiled=True)  30.4 us
    another operation x3, other arithmetic  18.2 us
    all_to_all x1, blocking collectives, on_device(): lax.all_to_all(lax.all_to_all(outgoing, 'expert', split_axis=0, concat_ax...  15.7 us
    all_to_all x1, blocking collectives, on_device(): lax.all_to_all(slot_grad, 'dp', split_axis=2, concat_axis=0, tiled=True)  13.7 us
  transfers between devices with their start and end apart: 4, of which 2 were waited for; matrix products, arithmetic and copies ran while one was open for 10% of the time, Pallas kernels for 0%

commit v1 on v0

v1 whole, which is shorter than its diff:
```python
import jax
import jax.numpy as jnp
from jax import lax
from jax.sharding import Mesh, PartitionSpec as P

CORES = 2


def on_device(tokens, expert_ids, gate_weight, up_weight, hidden_grad):
    n_z = lax.axis_size("z")
    n_dp = lax.axis_size("dp")
    core = lax.axis_index("c")
    swap = [(0, 1), (1, 0)]
    tok_rows, width_part = tokens.shape
    top_k = expert_ids.shape[1]
    share_rows = hidden_grad.shape[1]
    hidden_units = gate_weight.shape[2]
    capacity = share_rows * n_dp // (n_z * CORES)
    pair_rows = CORES * capacity

    own_rows = jnp.concatenate([gate_weight[0], up_weight[0]], axis=1)
    weights = lax.all_gather(own_rows, "dp", axis=0, tiled=True)

    other_tokens = lax.ppermute(tokens, "c", swap)
    other_ids = lax.ppermute(expert_ids, "c", swap)
    first = core == 0
    tokens_pair = jnp.concatenate(
        [jnp.where(first, tokens, other_tokens), jnp.where(first, other_tokens, tokens)], axis=0
    )
    ids_pair = jnp.concatenate(
        [jnp.where(first, expert_ids, other_ids), jnp.where(first, other_ids, expert_ids)], axis=0
    ).T
    pair_toks = CORES * tok_rows

    expert_of = jnp.arange(n_z, dtype=jnp.int32)[:, None] * CORES + core
    hit = jnp.zeros((n_z, pair_toks), jnp.bool_)
    for choice_k in range(top_k):
        hit = hit | (ids_pair[choice_k][None, :] == expert_of)
    src_of = jnp.arange(pair_toks, dtype=jnp.int32) // tok_rows
    earlier = (
        (jnp.arange(pair_toks)[:, None] < jnp.arange(pair_toks)[None, :])
        & (src_of[:, None] == src_of[None, :])
    ).astype(jnp.bfloat16)
    ranks = jnp.dot(hit.astype(jnp.bfloat16), earlier, preferred_element_type=jnp.float32)
    row_of = jnp.where(hit, ranks.astype(jnp.int32) + src_of[None, :] * capacity, -1)
    placer = (
        (row_of[:, None, :] == jnp.arange(pair_rows, dtype=jnp.int32)[None, :, None])
        .astype(jnp.bfloat16)
        .reshape(n_z * pair_rows, pair_toks)
    )
    outgoing = jnp.dot(placer, tokens_pair, preferred_element_type=jnp.float32)
    outgoing = outgoing.astype(jnp.bfloat16).reshape(n_z, pair_rows, width_part)
    own_width = lax.all_to_all(outgoing, "z", split_axis=0, concat_axis=0, tiled=True)
    by_share = own_width.reshape(n_dp, share_rows, width_part)
    arrived = lax.all_to_all(by_share, "dp", split_axis=0, concat_axis=0, tiled=True)
    slot_rows = arrived.transpose(1, 0, 2).reshape(share_rows, n_dp * width_part)

    both = jnp.dot(slot_rows, weights, preferred_element_type=jnp.float32)
    gate, up = both[:, :hidden_units], both[:, hidden_units:]
    sigmoid_gate = jax.nn.sigmoid(gate)
    silu_gate = gate * sigmoid_gate
    hidden = (silu_gate * up).astype(jnp.bfloat16)
    delta = hidden_grad[0].astype(jnp.float32)
    gate_delta = (delta * up * sigmoid_gate * (1.0 + gate * (1.0 - sigmoid_gate))).astype(
        jnp.bfloat16
    )
    up_delta = (delta * silu_gate).astype(jnp.bfloat16)
    both_delta = jnp.concatenate([gate_delta, up_delta], axis=1)
    all_delta = lax.all_gather(both_delta, "dp", axis=0, tiled=True)

    slot_grad = lax.dot_general(
        weights.reshape(n_dp, width_part, 2 * hidden_units),
        both_delta,
        (((2,), (1,)), ((), ())),
        preferred_element_type=jnp.float32,
    )
    slot_grad = slot_grad.astype(jnp.bfloat16).transpose(0, 2, 1)
    back = lax.all_to_all(slot_grad, "dp", split_axis=0, concat_axis=0, tiled=True)
    back = back.reshape(n_z, pair_rows, width_part)
    returned = lax.all_to_all(back, "z", split_axis=0, concat_axis=0, tiled=True)
    token_part = lax.dot_general(
        placer,
        returned.reshape(n_z * pair_rows, width_part),
        (((0,), (0,)), ((), ())),
        preferred_element_type=jnp.float32,
    )
    mine = jnp.where(first, token_part[:tok_rows], token_part[tok_rows:])
    theirs = jnp.where(first, token_part[tok_rows:], token_part[:tok_rows])
    token_grad = (mine + lax.ppermute(theirs, "c", swap)).astype(jnp.bfloat16)

    both_grad = lax.dot_general(
        own_width.reshape(n_dp * share_rows, width_part),
        all_delta,
        (((0,), (0,)), ((), ())),
        preferred_element_type=jnp.float32,
    )
    return (
        hidden[None],
        both_grad[None, :, :hidden_units],
        both_grad[None, :, hidden_units:],
        token_grad,
    )


def solution(mesh):
    n_expert, n_dp = mesh.devices.shape
    split = Mesh(mesh.devices.reshape(n_expert // CORES, CORES, n_dp), ("z", "c", "dp"))
    expert = ("z", "c")
    placed = (
        P(expert, "dp"),
        P(expert, None),
        P(expert, "dp", None),
        P(expert, "dp", None),
        P(expert, "dp", None),
    )
    return jax.shard_map(
        on_device,
        mesh=split,
        in_specs=placed,
        out_specs=(
            P(expert, "dp", None),
            P(expert, "dp", None),
            P(expert, "dp", None),
            P(expert, "dp"),
        ),
        check_vma=False,
    )
```

time: 312 us -> 234 us (0.75)
  waiting for transfers between devices: 105 us -> 0.94 us
  blocking collectives: 120 us -> 174 us
  other arithmetic: 19.2 us -> 5.67 us
  local copies, waits for them, and re-layouts: 10.1 us -> 1.42 us
    all_to_all x1 -> x0, waiting for transfers between devices: 63.3 us -> none  [on_device(): lax.all_to_all(outgoing, 'expert', split_axis=0, concat_axis=0, tiled=True)]
    all_to_all x3 -> x4, blocking collectives: 120 us -> 174 us  [the longest x1 80 us: on_device(): lax.all_to_all(outgoing, 'z', split_axis=0, concat_axis=0, tiled=True)]
    all_gather x2, waiting for transfers between devices: 40.8 us -> 0.02 us  [the longest x1 0.02 us: on_device(): weights = lax.all_gather(own_rows, 'dp', axis=0, tiled=True)]
    all_to_all x1 -> x0, starting transfers between devices: 30.4 us -> none  [on_device(): lax.all_to_all(outgoing, 'expert', split_axis=0, concat_axis=0, tiled=True)]
    ppermute x0 -> x3, starting transfers between devices: none -> 27.9 us  [the longest x1 16.1 us: on_device(): other_ids = lax.ppermute(expert_ids, 'c', swap)]
    another operation x3 -> x0, other arithmetic: 18.2 us -> none
    unnamed x13 -> x2, local copies, waits for them, and re-layouts: 5.95 us -> 0.01 us
    dot_general x7 -> x6, matrix products: 12.3 us -> 9.3 us  [the longest x1 2.86 us: on_device(): lax.dot_general(weights.reshape(n_dp, width_part, 2 * hidden_units), both...]
  transfers between devices with their start and end apart: 4 -> 5, of which waited for: 2 -> 1; matrix products, arithmetic and copies ran while one was open for 10% -> 4% of each run, Pallas kernels for 0% -> 0%
where the time goes in v1:
time: 234 us
  blocking collectives  174 us (74%)
  starting transfers between devices  27.9 us (12%)
  between operations  14.2 us (6%)
  matrix products  9.3 us (4%)
  other arithmetic  5.67 us (2%)
    all_to_all x1, blocking collectives, on_device(): lax.all_to_all(outgoing, 'z', split_axis=0, concat_axis=0, tiled=True)  80 us
    all_to_all x1, blocking collectives, on_device(): lax.all_to_all(back, 'z', split_axis=0, concat_axis=0, tiled=True)  65.7 us
    ppermute x1, starting transfers between devices, on_device(): other_ids = lax.ppermute(expert_ids, 'c', swap)  16.1 us
    all_to_all x1, blocking collectives, on_device(): lax.all_to_all(by_share, 'dp', split_axis=0, concat_axis=0, tiled=True)  15.8 us
    all_to_all x1, blocking collectives, on_device(): lax.all_to_all(slot_grad, 'dp', split_axis=0, concat_axis=0, tiled=True)  12.6 us
    ppermute x1, starting transfers between devices, on_device(): token_grad = (mine + lax.ppermute(theirs, 'c', swap)).astype(jnp.bfloat16)  9.88 us
  transfers between devices with their start and end apart: 5, of which 1 were waited for; matrix products, arithmetic and copies ran while one was open for 4% of the time, Pallas kernels for 0%

profile of v1, /device:TPU:1, one launch (start us, length us, event | category | flops | bytes accessed | tf_op | source)
XLA Modules:
  0.0 233.5 jit_solution(15520024695387757225)
XLA Ops:
  7.2 0.0 all-gather.3.cloned.1.call-start
  7.2 16.1 %collective-permute-start = (s32[128,8]{0,1:T(8,128)}, s32[128,8]{0,1:T(8,128)S(1)}, u32[]{:S(2)}, u32[]{:S(2)}) collective-permute-start(s32[128,8]{0,1:T(8,128)} %param.6), channel_id=1, source_target_pairs={{0,16},{16,0},{1,17},{17,1},{2,18},{18,2},{3,19},{19,3},{4,20},{20... | collective-permute-start | bytes 12296 | tf_op jit(solution)/shard_map/ppermute | solution.py:25
  23.3 1.9 collective-permute-start.1
  25.2 1.6 pad_maximum_fusion
  26.8 0.0 all-gather.3.cloned.1.call-update
  26.9 0.0 all-gather.5.cloned.1.call-start
  27.0 0.1 eq.178
  27.0 0.0 collective-permute-done
  27.0 0.7 broadcast_select_fusion.3
  27.8 0.2 fusion.4
  28.0 0.5 bitcast_compare_fusion
  28.5 0.0 collective-permute-done.1
  28.5 0.8 broadcast_select_fusion.1
  29.3 0.4 convolution_convert_fusion
  29.7 80.0 %all_to_all.20 = bf16[32,64,128]{2,1,0:T(8,128)(2,1)S(1)} all-to-all(bf16[32,64,128]{2,1,0:T(8,128)(2,1)S(1)} %bitcast.48), channel_id=1, replica_groups=mesh['z'=32,'c'=2,'dp'=16] {'z'}, dimensions={0} | all-to-all | bytes 1048576 | tf_op jit(solution)/shard_map/all_to_all | solution.py:53
  109.7 0.0 copy-start
  109.7 15.8 %all_to_all.21 = bf16[16,128,128]{2,1,0:T(8,128)(2,1)S(1)} all-to-all(bf16[16,128,128]{2,1,0:T(8,128)(2,1)S(1)} %bitcast.45), channel_id=1, replica_groups=mesh['z'=32,'c'=2,'dp'=16] {'dp'}, dimensions={0} | all-to-all | bytes 1048576 | tf_op jit(solution)/shard_map/all_to_all | solution.py:55
  125.5 0.3 copy.10
  125.8 0.0 all-gather.3.cloned.1.call-done
  125.8 2.5 %fusion.47 = f32[128,768]{1,0:T(8,128)S(1)} fusion(bf16[128,2048]{0,1:T(8,128)(2,1)S(1)} %bitcast.51, bf16[2048,768]{1,0:T(8,128)(2,1)} %all-gather.3.cloned.1.call-done), kind=kOutput, calls=%fused_computation.73 | convolution fusion | flops 402653184 | bytes 4063232 | tf_op jit(solution)/shard_map/dot_general | solution.py:58
  128.3 0.0 copy-done
  128.3 0.8 fusion.11
  129.1 0.7 pad_maximum_fusion.1
  129.8 0.0 all-gather.5.cloned.1.call-update
  129.8 2.9 %fusion.1 = bf16[16,128,128]{1,2,0:T(8,128)(2,1)S(1)} fusion(bf16[16,128,768]{2,1,0:T(8,128)(2,1)} %bitcast.47, bf16[128,384]{1,0:T(8,128)(2,1)S(1)} %get-tuple-element.5, bf16[128,384]{1,0:T(8,128)(2,1)S(1)} %get-tuple-element.4), kind=kOutput, calls=%fused_computation.5 | convolution fusion | flops 403308544 | bytes 3866624 | tf_op jit(solution)/shard_map/dot_general | solution.py:71
  132.7 12.6 %all_to_all.22 = bf16[16,128,128]{1,2,0:T(8,128)(2,1)S(1)} all-to-all(bf16[16,128,128]{1,2,0:T(8,128)(2,1)S(1)} %fusion.1), channel_id=1, replica_groups=mesh['z'=32,'c'=2,'dp'=16] {'dp'}, dimensions={0} | all-to-all | bytes 1048576 | tf_op jit(solution)/shard_map/all_to_all | solution.py:78
  145.3 0.3 copy.11
  145.5 65.7 %all_to_all.23 = bf16[32,64,128]{2,1,0:T(8,128)(2,1)S(1)} all-to-all(bf16[32,64,128]{2,1,0:T(8,128)(2,1)S(1)} %bitcast.49), channel_id=1, replica_groups=mesh['z'=32,'c'=2,'dp'=16] {'z'}, dimensions={0} | all-to-all | bytes 1048576 | tf_op jit(solution)/shard_map/all_to_all | solution.py:80
  211.2 0.7 fusion.2
  212.0 9.9 %collective-permute-start.2 = (f32[128,128]{1,0:T(8,128)S(1)}, f32[128,128]{1,0:T(8,128)S(1)}, u32[]{:S(2)}, u32[]{:S(2)}) collective-permute-start(f32[128,128]{1,0:T(8,128)S(1)} %slice_select_fusion), channel_id=1, source_target_pairs={{0,16},{16,0},{1,17},{17,1},{2,18},{18,2},{3,19},{19,3},{4,20},{20... | collective-permute-start | bytes 196616 | tf_op jit(solution)/shard_map/ppermute | solution.py:89
  221.9 0.9 collective-permute-done.2
  222.8 0.6 add_convert_fusion
  223.4 0.0 all-gather.5.cloned.1.call-done
  223.4 2.5 %fusion.48 = f32[128,768]{1,0:T(8,128)S(1)} fusion(bf16[2048,128]{1,0:T(8,128)(2,1)S(1)} %bitcast.46, bf16[2048,768]{1,0:T(8,128)(2,1)} %all-gather.5.cloned.1.call-done), kind=kOutput, calls=%fused_computation.74 | convolution fusion | flops 402653184 | bytes 4063232 | tf_op jit(solution)/shard_map/dot_general | solution.py:91
  225.9 0.8 slice_bitcast_fusion
  (6 shorter events, 0.0 us)
Async XLA Ops:
  7.2 118.6 %all-gather.3.cloned.1.call-start = ((), (), s32[]{:S(2)}) async-start(), calls=%async_computation.4 | async-start | bytes 3342336 | tf_op jit(solution)/shard_map/all_gather | solution.py:22
  7.2 19.8 %collective-permute-start = (s32[128,8]{0,1:T(8,128)}, s32[128,8]{0,1:T(8,128)S(1)}, u32[]{:S(2)}, u32[]{:S(2)}) collective-permute-start(s32[128,8]{0,1:T(8,128)} %param.6), channel_id=1, source_target_pairs={{0,16},{16,0},{1,17},{17,1},{2,18},{18,2},{3,19},{19,3},{4,20},{20... | collective-permute-start | bytes 12296 | tf_op jit(solution)/shard_map/ppermute | solution.py:25
  23.3 5.2 %collective-permute-start.1 = (bf16[128,128]{1,0:T(8,128)(2,1)}, bf16[128,128]{1,0:T(8,128)(2,1)S(1)}, u32[]{:S(2)}, u32[]{:S(2)}) collective-permute-start(bf16[128,128]{1,0:T(8,128)(2,1)} %param.5), channel_id=1, source_target_pairs={{0,16},{16,0},{1,17},{17,1},{2,18},{18,2},{3,19},{19,3},{4,20},{20... | collective-permute-start | bytes 98312 | tf_op jit(solution)/shard_map/ppermute | solution.py:24
  26.9 196.5 %all-gather.5.cloned.1.call-start = ((), (), s32[]{:S(2)}) async-start(), calls=%async_computation.5 | async-start | bytes 3342336 | tf_op jit(solution)/shard_map/all_gather | solution.py:69
  109.7 18.6 %copy-start = (bf16[1,128,384]{2,1,0:T(8,128)(2,1)S(1)}, bf16[1,128,384]{2,1,0:T(8,128)(2,1)}, u32[]{:S(2)}) copy-start(bf16[1,128,384]{2,1,0:T(8,128)(2,1)} %param.9) | copy-start | bytes 294916
  212.0 10.8 %collective-permute-start.2 = (f32[128,128]{1,0:T(8,128)S(1)}, f32[128,128]{1,0:T(8,128)S(1)}, u32[]{:S(2)}, u32[]{:S(2)}) collective-permute-start(f32[128,128]{1,0:T(8,128)S(1)} %slice_select_fusion), channel_id=1, source_target_pairs={{0,16},{16,0},{1,17},{17,1},{2,18},{18,2},{3,19},{19,3},{4,20},{20... | collective-permute-start | bytes 196616 | tf_op jit(solution)/shard_map/ppermute | solution.py:89
Sparse Core Ops, SparseCore 0:
  27.0 78.1 all-gather.2
  129.9 68.4 all-gather.4

commit v2 on v1

v2 whole, which is shorter than its diff:
```python
import jax
import jax.numpy as jnp
from jax import lax
from jax.sharding import Mesh, PartitionSpec as P

CORES = 2
ZL = 4


def on_device(tokens, expert_ids, gate_weight, up_weight, hidden_grad):
    n_zh = lax.axis_size("zh")
    n_dp = lax.axis_size("dp")
    core = lax.axis_index("c")
    swap = [(0, 1), (1, 0)]
    tok_rows, width_part = tokens.shape
    top_k = expert_ids.shape[1]
    share_rows = hidden_grad.shape[1]
    hidden_units = gate_weight.shape[2]
    capacity = share_rows * n_dp // (n_zh * ZL * CORES)
    pair_rows = CORES * capacity

    own_rows = jnp.concatenate([gate_weight[0], up_weight[0]], axis=1)
    weights = lax.all_gather(own_rows, "dp", axis=0, tiled=True)

    ids_rows = expert_ids.T.astype(jnp.bfloat16)
    sent = jnp.concatenate([tokens, ids_rows], axis=0)
    mine = lax.all_gather(sent, "zh", axis=0, tiled=False)
    other = lax.ppermute(mine, "c", swap)
    first = core == 0
    known = jnp.stack([jnp.where(first, mine, other), jnp.where(first, other, mine)], axis=1)
    known_tokens = known[:, :, :tok_rows].reshape(n_zh, CORES * tok_rows, width_part)
    known_ids = known[:, :, tok_rows:].astype(jnp.float32)

    expert_of = (lax.axis_index("zh") * ZL + jnp.arange(ZL, dtype=jnp.int32)) * CORES + core
    expert_of = expert_of.astype(jnp.float32)[:, None, None, None]
    hit = jnp.zeros((ZL, n_zh, CORES, tok_rows), jnp.bool_)
    for choice_k in range(top_k):
        hit = hit | (known_ids[None, :, :, choice_k] == expert_of)
    earlier = jnp.arange(tok_rows)[:, None] < jnp.arange(tok_rows)[None, :]
    ranks = jnp.dot(
        hit.reshape(-1, tok_rows).astype(jnp.bfloat16),
        earlier.astype(jnp.bfloat16),
        preferred_element_type=jnp.float32,
    ).reshape(hit.shape)
    first_row = jnp.arange(CORES, dtype=jnp.int32)[None, None, :, None] * capacity
    row_of = jnp.where(hit, ranks.astype(jnp.int32) + first_row, -1)
    row_of = row_of.transpose(1, 0, 2, 3).reshape(n_zh, ZL, 1, CORES * tok_rows)
    placer = (
        (row_of == jnp.arange(pair_rows, dtype=jnp.int32)[:, None])
        .astype(jnp.bfloat16)
        .reshape(n_zh, ZL * pair_rows, CORES * tok_rows)
    )
    outgoing = lax.dot_general(
        placer, known_tokens, (((2,), (1,)), ((0,), (0,))), preferred_element_type=jnp.float32
    ).astype(jnp.bfloat16)
    outgoing = outgoing.reshape(n_zh, ZL, pair_rows, width_part).transpose(1, 0, 2, 3)
    own_width = lax.all_to_all(outgoing, "zl", split_axis=0, concat_axis=0, tiled=True)
    own_width = own_width.transpose(1, 0, 2, 3)
    by_share = own_width.reshape(n_dp, share_rows, width_part)
    arrived = lax.all_to_all(by_share, "dp", split_axis=0, concat_axis=0, tiled=True)
    slot_rows = arrived.transpose(1, 0, 2).reshape(share_rows, n_dp * width_part)

    both = jnp.dot(slot_rows, weights, preferred_element_type=jnp.float32)
    gate, up = both[:, :hidden_units], both[:, hidden_units:]
    sigmoid_gate = jax.nn.sigmoid(gate)
    silu_gate = gate * sigmoid_gate
    hidden = (silu_gate * up).astype(jnp.bfloat16)
    delta = hidden_grad[0].astype(jnp.float32)
    gate_delta = (delta * up * sigmoid_gate * (1.0 + gate * (1.0 - sigmoid_gate))).astype(
        jnp.bfloat16
    )
    up_delta = (delta * silu_gate).astype(jnp.bfloat16)
    both_delta = jnp.concatenate([gate_delta, up_delta], axis=1)
    all_delta = lax.all_gather(both_delta, "dp", axis=0, tiled=True)

    slot_grad = lax.dot_general(
        weights.reshape(n_dp, width_part, 2 * hidden_units),
        both_delta,
        (((2,), (1,)), ((), ())),
        preferred_element_type=jnp.float32,
    )
    slot_grad = slot_grad.astype(jnp.bfloat16).transpose(0, 2, 1)
    back = lax.all_to_all(slot_grad, "dp", split_axis=0, concat_axis=0, tiled=True)
    back = back.reshape(n_zh, ZL, pair_rows, width_part).transpose(1, 0, 2, 3)
    returned = lax.all_to_all(back, "zl", split_axis=0, concat_axis=0, tiled=True)
    returned = returned.transpose(1, 0, 2, 3).reshape(n_zh, ZL * pair_rows, width_part)
    token_part = lax.dot_general(
        placer, returned, (((1,), (1,)), ((0,), (0,))), preferred_element_type=jnp.float32
    ).reshape(n_zh, CORES, tok_rows, width_part)
    kept = jnp.where(first, token_part[:, 0], token_part[:, 1])
    given = jnp.where(first, token_part[:, 1], token_part[:, 0]).astype(jnp.bfloat16)
    token_sum = kept + lax.ppermute(given, "c", swap).astype(jnp.float32)
    token_grad = lax.psum_scatter(
        token_sum.astype(jnp.bfloat16), "zh", scatter_dimension=0, tiled=False
    )

    both_grad = lax.dot_general(
        own_width.reshape(n_dp * share_rows, width_part),
        all_delta,
        (((0,), (0,)), ((), ())),
        preferred_element_type=jnp.float32,
    )
    return (
        hidden[None],
        both_grad[None, :, :hidden_units],
        both_grad[None, :, hidden_units:],
        token_grad,
    )


def solution(mesh):
    n_expert, n_dp = mesh.devices.shape
    split = Mesh(mesh.devices.reshape(n_expert // (ZL * CORES), ZL, CORES, n_dp), ("zh", "zl", "c", "dp"))
    expert = ("zh", "zl", "c")
    placed = (
        P(expert, "dp"),
        P(expert, None),
        P(expert, "dp", None),
        P(expert, "dp", None),
        P(expert, "dp", None),
    )
    return jax.shard_map(
        on_device,
        mesh=split,
        in_specs=placed,
        out_specs=(
            P(expert, "dp", None),
            P(expert, "dp", None),
            P(expert, "dp", None),
            P(expert, "dp"),
        ),
        check_vma=False,
    )
```

time: 234 us -> 273 us (1.17)
  the two profiles are of different devices: /device:TPU:1 before, /device:TPU:4 now
where the time goes in v2:
time: 273 us
  blocking collectives  125 us (46%)
  waiting for transfers between devices  113 us (41%)
  between operations  13.9 us (5%)
  matrix products  9.32 us (3%)
  other arithmetic  5.9 us (2%)
  starting transfers between devices  3.96 us (1%)
    reduce_scatter x1, waiting for transfers between devices, on_device(): lax.psum_scatter(token_sum.astype(jnp.bfloat16), 'zh', scatter_dimension=...  70.5 us
    all_gather x1, blocking collectives, on_device(): mine = lax.all_gather(sent, 'zh', axis=0, tiled=False)  52.8 us
    all_gather x1, waiting for transfers between devices, on_device(): all_delta = lax.all_gather(both_delta, 'dp', axis=0, tiled=True)  39.3 us
    all_to_all x1, blocking collectives, on_device(): lax.all_to_all(by_share, 'dp', split_axis=0, concat_axis=0, tiled=True)  20.9 us
    all_to_all x1, blocking collectives, on_device(): lax.all_to_all(outgoing, 'zl', split_axis=0, concat_axis=0, tiled=True)  19.3 us
    all_to_all x1, blocking collectives, on_device(): lax.all_to_all(back, 'zl', split_axis=0, concat_axis=0, tiled=True)  17.7 us
    all_to_all x1, blocking collectives, on_device(): lax.all_to_all(slot_grad, 'dp', split_axis=0, concat_axis=0, tiled=True)  14.4 us
  transfers between devices with their start and end apart: 5, of which 4 were waited for; matrix products, arithmetic and copies ran while one was open for 4% of the time, Pallas kernels for 0%

profile of v2, /device:TPU:4, one launch (start us, length us, event | category | flops | bytes accessed | tf_op | source)
XLA Modules:
  0.0 272.9 jit_solution(5525041961993818787)
XLA Ops:
  7.2 0.0 all-gather.4.cloned.1.call-start
  7.2 1.6 pad_maximum_fusion.1
  8.8 0.0 all-gather.4.cloned.1.call-update
  8.9 0.0 all-gather.6.cloned.1.call-start
  8.9 0.7 convert_bitcast_fusion
  9.6 0.8 pad_maximum_fusion.3
  10.4 52.8 %all-gather = bf16[1088,128]{1,0:T(8,128)(2,1)S(1)} all-gather(bf16[136,128]{1,0:T(8,128)(2,1)S(1)} %pad_maximum_fusion.3), channel_id=2, replica_groups=mesh['zh'=8,'zl'=4,'c'=2,'dp'=16] {'zh'}, dimensions={0}, use_global_device_ids=true | all-gather | bytes 313344 | tf_op jit(solution)/shard_map/all_gather | solution.py:27
  63.2 1.9 collective-permute-start
  65.2 0.1 eq.236
  65.3 1.4 collective-permute-done
  66.8 0.2 fusion.4
  67.0 0.1 pad_maximum_fusion
  67.1 0.1 copy.43
  67.3 0.4 bitcast_compare_fusion
  67.6 0.4 convolution_convert_fusion
  68.1 19.3 %all_to_all.20 = bf16[4,8,64,128]{3,2,1,0:T(8,128)(2,1)S(1)} all-to-all(bf16[4,8,64,128]{3,2,1,0:T(8,128)(2,1)S(1)} %bitcast.117), channel_id=1, replica_groups=mesh['zh'=8,'zl'=4,'c'=2,'dp'=16] {'zl'}, dimensions={0} | all-to-all | bytes 1048576 | tf_op jit(solution)/shard_map/all_to_all | solution.py:57
  87.5 0.0 copy-start
  87.5 20.9 %all_to_all.21 = bf16[16,128,128]{2,1,0:T(8,128)(2,1)S(1)} all-to-all(bf16[16,128,128]{2,1,0:T(8,128)(2,1)S(1)} %bitcast.110), channel_id=1, replica_groups=mesh['zh'=8,'zl'=4,'c'=2,'dp'=16] {'dp'}, dimensions={0} | all-to-all | bytes 1048576 | tf_op jit(solution)/shard_map/all_to_all | solution.py:60
  108.4 0.3 copy.46
  108.7 0.0 all-gather.4.cloned.1.call-done
  108.7 2.5 fusion.40
  111.2 0.0 copy-done
  111.2 0.8 fusion.9
  112.0 0.7 pad_maximum_fusion.2
  112.7 0.0 all-gather.6.cloned.1.call-update
  112.7 0.0 reduce-scatter.2.cloned.1.call-start
  112.8 2.9 %fusion = bf16[16,128,128]{1,2,0:T(8,128)(2,1)S(1)} fusion(bf16[16,128,768]{2,1,0:T(8,128)(2,1)} %bitcast.112, bf16[128,384]{1,0:T(8,128)(2,1)S(1)} %get-tuple-element.7, bf16[128,384]{1,0:T(8,128)(2,1)S(1)} %get-tuple-element.6), kind=kOutput, calls=%fused_computation.3 | convolution fusion | flops 403308544 | bytes 3866624 | tf_op jit(solution)/shard_map/dot_general | solution.py:76
  115.6 14.4 %all_to_all.22 = bf16[16,128,128]{1,2,0:T(8,128)(2,1)S(1)} all-to-all(bf16[16,128,128]{1,2,0:T(8,128)(2,1)S(1)} %fusion), channel_id=1, replica_groups=mesh['zh'=8,'zl'=4,'c'=2,'dp'=16] {'dp'}, dimensions={0} | all-to-all | bytes 1048576 | tf_op jit(solution)/shard_map/all_to_all | solution.py:83
  130.1 0.3 copy.47
  130.4 17.7 %all_to_all.23 = bf16[4,8,64,128]{3,2,1,0:T(8,128)(2,1)S(1)} all-to-all(bf16[4,8,64,128]{3,2,1,0:T(8,128)(2,1)S(1)} %copy.48), channel_id=1, replica_groups=mesh['zh'=8,'zl'=4,'c'=2,'dp'=16] {'zl'}, dimensions={0} | all-to-all | bytes 1048576 | tf_op jit(solution)/shard_map/all_to_all | solution.py:85
  148.2 0.8 fusion.42
  149.0 0.1 fusion.6
  149.0 1.9 collective-permute-start.1
  151.0 1.5 collective-permute-done.1
  152.5 0.8 fusion.5
  153.2 0.0 reduce-scatter.2.cloned.1.call-update
  153.3 39.3 %all-gather.6.cloned.1.call-done = bf16[2048,768]{1,0:T(8,128)(2,1)} async-done(((bf16[128,768]{1,0:T(8,128)(2,1)}), bf16[2048,768]{1,0:T(8,128)(2,1)}) %all-gather.6.cloned.1.call-update) | async-done | bytes 3145744 | tf_op jit(solution)/shard_map/all_gather | solution.py:74
  192.5 2.5 fusion.41
  195.1 0.8 slice_bitcast_fusion.2
  195.8 70.5 %reduce-scatter.2.cloned.1.call-done = bf16[1,128,128]{2,1,0:T(8,128)(2,1)} async-done(((bf16[8,128,128]{2,1,0:T(8,128)(2,1)}), bf16[1,128,128]{2,1,0:T(8,128)(2,1)}) %reduce-scatter.2.cloned.1.call-update) | async-done | bytes 32784 | tf_op jit(solution)/shard_map/reduce_scatter | solution.py:93
  (12 shorter events, 0.3 us)
Async XLA Ops:
  7.2 101.5 %all-gather.4.cloned.1.call-start = ((), (), s32[]{:S(2)}) async-start(), calls=%async_computation.5 | async-start | bytes 3342336 | tf_op jit(solution)/shard_map/all_gather | solution.py:23
  8.9 183.7 %all-gather.6.cloned.1.call-start = ((), (), s32[]{:S(2)}) async-start(), calls=%async_computation.6 | async-start | bytes 3342336 | tf_op jit(solution)/shard_map/all_gather | solution.py:74
  63.2 3.5 %collective-permute-start = (bf16[8,136,128]{2,0,1:T(8,128)(2,1)S(1)}, bf16[8,136,128]{2,0,1:T(8,128)(2,1)S(1)}, u32[]{:S(2)}, u32[]{:S(2)}) collective-permute-start(bf16[8,136,128]{2,0,1:T(8,128)(2,1)S(1)} %copy.39), channel_id=1, source_target_pairs={{0,16},{16,0},{1,17},{17,1},{2,18},{18,2},{3,19},{19,3},{4,20},{20... | collective-permute-start | bytes 835592 | tf_op jit(solution)/shard_map/ppermute | solution.py:28
  87.5 23.8 %copy-start = (bf16[1,128,384]{2,1,0:T(8,128)(2,1)S(1)}, bf16[1,128,384]{2,1,0:T(8,128)(2,1)}, u32[]{:S(2)}) copy-start(bf16[1,128,384]{2,1,0:T(8,128)(2,1)} %param.9) | copy-start | bytes 294916
  112.7 153.6 %reduce-scatter.2.cloned.1.call-start = ((), (), s32[]{:S(2)}) async-start(), calls=%async_computation.7 | async-start | bytes 294912 | tf_op jit(solution)/shard_map/reduce_scatter | solution.py:93
  149.0 3.4 %collective-permute-start.1 = (bf16[8,128,128]{2,1,0:T(8,128)(2,1)S(1)}, bf16[8,128,128]{2,1,0:T(8,128)(2,1)S(1)}, u32[]{:S(2)}, u32[]{:S(2)}) collective-permute-start(bf16[8,128,128]{2,1,0:T(8,128)(2,1)S(1)} %fusion.6), channel_id=1, source_target_pairs={{0,16},{16,0},{1,17},{17,1},{2,18},{18,2},{3,19},{19,3},{4,20},{20... | collective-permute-start | bytes 786440 | tf_op jit(solution)/shard_map/ppermute | solution.py:92
Sparse Core Ops, SparseCore 0:
  12.8 95.5 all-gather.3
  113.2 79.3 all-gather.5
  196.5 69.7 reduce-scatter.1

commit v3 on v2

--- a/solution.py
+++ b/solution.py
@@ -5,6 +5,12 @@
 
 CORES = 2
 ZL = 4
+
+
+def gather_dp(rows, n_dp):
+    copies = jnp.broadcast_to(rows[None], (n_dp, *rows.shape))
+    got = lax.all_to_all(copies, "dp", split_axis=0, concat_axis=0, tiled=True)
+    return got.reshape(n_dp * rows.shape[0], rows.shape[1])
 
 
 def on_device(tokens, expert_ids, gate_weight, up_weight, hidden_grad):
@@ -20,7 +26,7 @@
     pair_rows = CORES * capacity
 
     own_rows = jnp.concatenate([gate_weight[0], up_weight[0]], axis=1)
-    weights = lax.all_gather(own_rows, "dp", axis=0, tiled=True)
+    weights = gather_dp(own_rows, n_dp)
 
     ids_rows = expert_ids.T.astype(jnp.bfloat16)
     sent = jnp.concatenate([tokens, ids_rows], axis=0)
@@ -54,6 +60,7 @@
         placer, known_tokens, (((2,), (1,)), ((0,), (0,))), preferred_element_type=jnp.float32
     ).astype(jnp.bfloat16)
     outgoing = outgoing.reshape(n_zh, ZL, pair_rows, width_part).transpose(1, 0, 2, 3)
+    outgoing, weights = lax.optimization_barrier((outgoing, weights))
     own_width = lax.all_to_all(outgoing, "zl", split_axis=0, concat_axis=0, tiled=True)
     own_width = own_width.transpose(1, 0, 2, 3)
     by_share = own_width.reshape(n_dp, share_rows, width_part)
@@ -71,7 +78,6 @@
     )
     up_delta = (delta * silu_gate).astype(jnp.bfloat16)
     both_delta = jnp.concatenate([gate_delta, up_delta], axis=1)
-    all_delta = lax.all_gather(both_delta, "dp", axis=0, tiled=True)
 
     slot_grad = lax.dot_general(
         weights.reshape(n_dp, width_part, 2 * hidden_units),
@@ -80,18 +86,26 @@
         preferred_element_type=jnp.float32,
     )
     slot_grad = slot_grad.astype(jnp.bfloat16).transpose(0, 2, 1)
-    back = lax.all_to_all(slot_grad, "dp", split_axis=0, concat_axis=0, tiled=True)
-    back = back.reshape(n_zh, ZL, pair_rows, width_part).transpose(1, 0, 2, 3)
-    returned = lax.all_to_all(back, "zl", split_axis=0, concat_axis=0, tiled=True)
-    returned = returned.transpose(1, 0, 2, 3).reshape(n_zh, ZL * pair_rows, width_part)
-    token_part = lax.dot_general(
-        placer, returned, (((1,), (1,)), ((0,), (0,))), preferred_element_type=jnp.float32
-    ).reshape(n_zh, CORES, tok_rows, width_part)
-    kept = jnp.where(first, token_part[:, 0], token_part[:, 1])
-    given = jnp.where(first, token_part[:, 1], token_part[:, 0]).astype(jnp.bfloat16)
-    token_sum = kept + lax.ppermute(given, "c", swap).astype(jnp.float32)
-    token_grad = lax.psum_scatter(
-        token_sum.astype(jnp.bfloat16), "zh", scatter_dimension=0, tiled=False
+    slot_grad, both_delta = lax.optimization_barrier((slot_grad, both_delta))
+    all_delta = lax.all_gather(both_delta, "dp", axis=0, tiled=True)
+    def go_back(slot_grad, placer):
+        back = lax.all_to_all(slot_grad, "dp", split_axis=0, concat_axis=0, tiled=True)
+        back = back.reshape(n_zh, ZL, pair_rows, width_part).transpose(1, 0, 2, 3)
+        returned = lax.all_to_all(back, "zl", split_axis=0, concat_axis=0, tiled=True)
+        returned = returned.transpose(1, 0, 2, 3).reshape(n_zh, ZL * pair_rows, width_part)
+        token_part = lax.dot_general(
+            placer, returned, (((1,), (1,)), ((0,), (0,))), preferred_element_type=jnp.float32
+        ).reshape(n_zh, CORES, tok_rows, width_part)
+        kept = jnp.where(first, token_part[:, 0], token_part[:, 1])
+        given = jnp.where(first, token_part[:, 1], token_part[:, 0]).astype(jnp.bfloat16)
+        token_sum = kept + lax.ppermute(given, "c", swap).astype(jnp.float32)
+        sums = lax.all_to_all(
+            token_sum.astype(jnp.bfloat16), "zh", split_axis=0, concat_axis=0, tiled=True
+        )
+        return jnp.sum(sums.astype(jnp.float32), axis=0).astype(jnp.bfloat16)
+
+    token_grad = lax.cond(
+        expert_ids[0, 0] >= 0, go_back, lambda *_: jnp.zeros_like(tokens), slot_grad, placer
     )
 
     both_grad = lax.dot_general(

time: 273 us -> 220 us (0.81)
  the two profiles are of different devices: /device:TPU:4 before, /device:TPU:32 now
where the time goes in v3:
time: 220 us; the launch traced here: 219 us
  blocking collectives  168 us (76%)
  between operations  14.9 us (7%)
  starting transfers between devices  11 us (5%)
  local copies, waits for them, and re-layouts  9.47 us (4%)
  matrix products  7.11 us (3%)
  other arithmetic  5.17 us (2%)
  waiting for transfers between devices  3.3 us (2%)
    all_gather x1, blocking collectives, on_device(): mine = lax.all_gather(sent, 'zh', axis=0, tiled=False)  53.4 us
    all_to_all x1, blocking collectives, go_back(): lax.all_to_all(token_sum.astype(jnp.bfloat16), 'zh', split_axis=0, concat...  51.4 us
    all_to_all x1, blocking collectives, on_device(): lax.all_to_all(by_share, 'dp', split_axis=0, concat_axis=0, tiled=True)  18.1 us
    all_to_all x1, blocking collectives, on_device(): lax.all_to_all(outgoing, 'zl', split_axis=0, concat_axis=0, tiled=True)  16.6 us
    all_to_all x1, blocking collectives, go_back(): lax.all_to_all(back, 'zl', split_axis=0, concat_axis=0, tiled=True)  14.8 us
    all_to_all x1, blocking collectives, go_back(): lax.all_to_all(slot_grad, 'dp', split_axis=0, concat_axis=0, tiled=True)  13.3 us
    all_to_all x1, starting transfers between devices, gather_dp(): got = lax.all_to_all(copies, 'dp', split_axis=0, concat_axis=0, tiled=True)  7.17 us
  transfers between devices with their start and end apart: 4, of which 2 were waited for; matrix products, arithmetic and copies ran while one was open for 4% of the time, Pallas kernels for 0%

profile of v3, /device:TPU:32, one launch (start us, length us, event | category | flops | bytes accessed | tf_op | source)
XLA Modules:
  0.0 218.8 jit_solution(1398692885573569959)
XLA Ops:
  7.2 1.0 pad_maximum_fusion.1
  8.1 2.0 broadcast_in_dim.24
  10.1 7.2 %all-to-all-start.3 = ((bf16[16,128,768]{2,1,0:T(8,128)(2,1)}), bf16[16,128,768]{2,1,0:T(8,128)(2,1)S(1)}, u32[]{:S(2)}, u32[]{:S(2)}) async-start(bf16[16,128,768]{2,1,0:T(8,128)(2,1)} %broadcast_in_dim.24), calls=%async_computation.3 | async-start | bytes 6291456 | tf_op jit(solution)/shard_map/all_to_all | solution.py:12
  17.3 0.0 all-gather.3.cloned.1.call-start
  17.3 0.0 copy-done.6
  17.3 0.0 copy-done.4
  17.4 53.4 %all-gather = bf16[1088,128]{1,0:T(8,128)(2,1)S(1)} all-gather(bf16[136,128]{1,0:T(8,128)(2,1)S(1)} %pad_maximum_fusion.3), channel_id=2, replica_groups=mesh['zh'=8,'zl'=4,'c'=2,'dp'=16] {'zh'}, dimensions={0}, use_global_device_ids=true | all-gather | bytes 313344 | tf_op jit(solution)/shard_map/all_gather | solution.py:33
  70.7 0.8 copy.68
  71.5 1.9 collective-permute-start.1
  73.4 0.1 eq.237
  73.5 1.8 collective-permute-done.1
  75.3 1.0 select_bitcast_fusion.1
  76.3 0.2 fusion.8
  76.5 0.1 pad_maximum_fusion
  76.6 0.1 copy.72
  76.8 1.5 fusion.42
  78.2 0.4 convolution_convert_fusion
  78.7 0.8 copy.84
  79.5 0.0 all-to-all-done.3
  79.5 16.6 %all_to_all.30 = bf16[4,8,64,128]{3,2,1,0:T(8,128)(2,1)S(1)} all-to-all(bf16[4,8,64,128]{3,2,1,0:T(8,128)(2,1)} %bitcast.123), channel_id=1, replica_groups=mesh['zh'=8,'zl'=4,'c'=2,'dp'=16] {'zl'}, dimensions={0} | all-to-all | bytes 1048576 | tf_op jit(solution)/shard_map/all_to_all | solution.py:64
  96.2 0.0 copy-start
  96.2 0.0 copy-start.3
  96.2 0.8 copy-done
  97.0 18.1 %all_to_all.31 = bf16[16,128,128]{2,1,0:T(8,128)(2,1)} all-to-all(bf16[16,128,128]{2,1,0:T(8,128)(2,1)S(1)} %bitcast.116), channel_id=1, replica_groups=mesh['zh'=8,'zl'=4,'c'=2,'dp'=16] {'dp'}, dimensions={0} | all-to-all | bytes 1048576 | tf_op jit(solution)/shard_map/all_to_all | solution.py:67
  115.2 2.0 copy.75
  117.2 1.7 fusion.44
  118.9 0.0 copy-done.3
  118.9 0.8 fusion.11
  119.6 0.7 pad_maximum_fusion.2
  120.3 1.8 fusion.4
  122.1 0.0 all-gather.3.cloned.1.call-update
  122.2 0.5 slice.67
  123.3 0.0 copy-start.1
  123.3 85.3 %conditional.1 = (bf16[128,128]{1,0:T(8,128)(2,1)S(1)}) conditional(s32[]{:T(128)} %bitcast.47, () %tuple.18, (pred[]{:T(512)}, bf16[16,128,128]{1,2,0:T(8,128)(2,1)}, bf16[8,256,256]{2,1,0:T(8,128)(2,1)}) %tuple.19), branch_computations={%region_0.1_spmd, %region_1.3_spmd} | conditional | flops 134987776 | bytes 16285776 | solution.py:107
  123.4 0.0 copy-start.2
  123.4 1.4 copy.76
  124.8 13.3 %all_to_all.27 = bf16[16,128,128]{2,1,0:T(8,128)(2,1)S(1)} all-to-all(bf16[16,128,128]{2,1,0:T(8,128)(2,1)S(1)} %copy.76), channel_id=1, replica_groups=mesh['zh'=8,'zl'=4,'c'=2,'dp'=16] {'dp'}, dimensions={0} | all-to-all | bytes 1048576 | tf_op jit(solution)/shard_map/cond/branch_1_fun/all_to_all | solution.py:92
  138.2 14.8 %all_to_all.28 = bf16[4,8,64,128]{3,2,1,0:T(8,128)(2,1)S(1)} all-to-all(bf16[4,8,64,128]{3,2,1,0:T(8,128)(2,1)S(1)} %copy.61), channel_id=1, replica_groups=mesh['zh'=8,'zl'=4,'c'=2,'dp'=16] {'zl'}, dimensions={0} | all-to-all | bytes 1048576 | tf_op jit(solution)/shard_map/cond/branch_1_fun/all_to_all | solution.py:94
  153.1 0.5 fusion.43
  153.6 0.1 fusion.3
  153.6 1.9 collective-permute-start
  155.6 1.5 collective-permute-done
  157.1 0.1 fusion.2
  157.1 51.4 %all_to_all.29 = bf16[8,128,128]{2,1,0:T(8,128)(2,1)S(1)} all-to-all(bf16[8,128,128]{2,1,0:T(8,128)(2,1)S(1)} %fusion.2), channel_id=1, replica_groups=mesh['zh'=8,'zl'=4,'c'=2,'dp'=16] {'zh'}, dimensions={0} | all-to-all | bytes 524288 | tf_op jit(solution)/shard_map/cond/branch_1_fun/all_to_all | solution.py:102
  208.6 0.0 copy-start.5
  208.6 0.0 all-gather.3.cloned.1.call-done
  208.7 2.5 %fusion.45 = f32[128,768]{1,0:T(8,128)S(1)} fusion(bf16[2048,128]{1,0:T(8,128)(2,1)S(1)} %bitcast.117, bf16[2048,768]{1,0:T(8,128)(2,1)} %all-gather.3.cloned.1.call-done), kind=kOutput, calls=%fused_computation.76 | convolution fusion | flops 402653184 | bytes 4063232 | tf_op jit(solution)/shard_map/dot_general | solution.py:111
  211.2 0.8 slice_bitcast_fusion
  (17 shorter events, 0.2 us)
Async XLA Ops:
  10.1 7.2 %copy-start.6 = (s32[128,8]{0,1:T(8,128)S(1)}, s32[128,8]{0,1:T(8,128)}, u32[]{:S(2)}) copy-start(s32[128,8]{0,1:T(8,128)} %param.8) | copy-start | bytes 12292
  10.1 7.2 %copy-start.4 = (bf16[128,128]{1,0:T(8,128)(2,1)S(1)}, bf16[128,128]{1,0:T(8,128)(2,1)}, u32[]{:S(2)}) copy-start(bf16[128,128]{1,0:T(8,128)(2,1)} %param.7) | copy-start | bytes 98308
  10.1 69.5 %all-to-all-start.3 = ((bf16[16,128,768]{2,1,0:T(8,128)(2,1)}), bf16[16,128,768]{2,1,0:T(8,128)(2,1)S(1)}, u32[]{:S(2)}, u32[]{:S(2)}) async-start(bf16[16,128,768]{2,1,0:T(8,128)(2,1)} %broadcast_in_dim.24), calls=%async_computation.3 | async-start | bytes 6291456 | tf_op jit(solution)/shard_map/all_to_all | solution.py:12
  17.3 191.4 %all-gather.3.cloned.1.call-start = ((), (), s32[]{:S(2)}) async-start(), calls=%async_computation.6 | async-start | bytes 3342336 | tf_op jit(solution)/shard_map/all_gather | solution.py:90
  71.5 3.8 %collective-permute-start.1 = (bf16[8,136,128]{2,0,1:T(8,128)(2,1)}, bf16[8,136,128]{2,0,1:T(8,128)(2,1)}, u32[]{:S(2)}, u32[]{:S(2)}) collective-permute-start(bf16[8,136,128]{2,0,1:T(8,128)(2,1)} %copy.68), channel_id=1, source_target_pairs={{0,16},{16,0},{1,17},{17,1},{2,18},{18,2},{3,19},{19,3},{4,20},{20... | collective-permute-start | bytes 835592 | tf_op jit(solution)/shard_map/ppermute | solution.py:34
  96.2 0.8 copy-start
  96.2 22.7 %copy-start.3 = (bf16[1,128,384]{2,1,0:T(8,128)(2,1)S(1)}, bf16[1,128,384]{2,1,0:T(8,128)(2,1)}, u32[]{:S(2)}) copy-start(bf16[1,128,384]{2,1,0:T(8,128)(2,1)} %param.11) | copy-start | bytes 294916
  123.3 85.3 %copy-start.1 = (bf16[4,8,64,128]{3,2,0,1:T(8,128)(2,1)S(1)}, bf16[4,8,64,128]{3,2,0,1:T(8,128)(2,1)}, u32[]{:S(2)}) copy-start(bf16[4,8,64,128]{3,2,0,1:T(8,128)(2,1)} %copy-done) | copy-start | bytes 1572868
  123.4 29.7 %copy-start.2 = (bf16[8,256,256]{2,1,0:T(8,128)(2,1)S(1)}, bf16[8,256,256]{2,1,0:T(8,128)(2,1)}, u32[]{:S(2)}) copy-start(bf16[8,256,256]{2,1,0:T(8,128)(2,1)} %get-tuple-element.38) | copy-start | bytes 3145732 | tf_op jit(solution)/shard_map/cond
  153.6 3.4 %collective-permute-start = (bf16[8,128,128]{2,1,0:T(8,128)(2,1)S(1)}, bf16[8,128,128]{2,1,0:T(8,128)(2,1)S(1)}, u32[]{:S(2)}, u32[]{:S(2)}) collective-permute-start(bf16[8,128,128]{2,1,0:T(8,128)(2,1)S(1)} %fusion.3), channel_id=1, source_target_pairs={{0,16},{16,0},{1,17},{17,1},{2,18},{18,2},{3,19},{19,3},{4,20},{20... | collective-permute-start | bytes 786440 | tf_op jit(solution)/shard_map/cond/branch_1_fun/ppermute | solution.py:101
  208.6 3.3 %copy-start.5 = (bf16[128,128]{1,0:T(8,128)(2,1)}, bf16[128,128]{1,0:T(8,128)(2,1)S(1)}, u32[]{:S(2)}) copy-start(bf16[128,128]{1,0:T(8,128)(2,1)S(1)} %get-tuple-element.56) | copy-start | bytes 98308
Sparse Core Ops, SparseCore 0:
  122.3 72.6 all-gather.2

commit v4 on v3

v4 whole, which is shorter than its diff:
```python
import jax
import jax.numpy as jnp
from jax import lax
from jax.experimental import pallas as pl
from jax.experimental.pallas import tpu as pltpu
from jax.sharding import Mesh, PartitionSpec as P

CORES = 2
ZL = 4


def expert_kernel(rows_ref, weights_ref, grad_ref, hidden_ref, delta_ref, slot_grad_ref):
    n_dp, _, width_part = rows_ref.shape
    hidden_units = grad_ref.shape[1]
    rows = jnp.concatenate([rows_ref[part] for part in range(n_dp)], axis=1)
    both = jnp.dot(rows, weights_ref[...], preferred_element_type=jnp.float32)
    gate, up = both[:, :hidden_units], both[:, hidden_units:]
    sigmoid_gate = jax.nn.sigmoid(gate)
    silu_gate = gate * sigmoid_gate
    hidden_ref[...] = (silu_gate * up).astype(jnp.bfloat16)
    grad = grad_ref[...].astype(jnp.float32)
    delta_ref[:, :hidden_units] = (
        grad * up * sigmoid_gate * (1.0 + gate * (1.0 - sigmoid_gate))
    ).astype(jnp.bfloat16)
    delta_ref[:, hidden_units:] = (grad * silu_gate).astype(jnp.bfloat16)
    delta = delta_ref[...]
    for part in range(n_dp):
        slot_grad_ref[part] = lax.dot_general(
            delta,
            weights_ref[part * width_part : (part + 1) * width_part],
            (((1,), (1,)), ((), ())),
            preferred_element_type=jnp.float32,
        ).astype(jnp.bfloat16)


def experts(rows, weights, grad):
    n_dp, share_rows, width_part = rows.shape
    both_units = weights.shape[1]
    flops = 4 * share_rows * n_dp * width_part * both_units
    return pl.pallas_call(
        expert_kernel,
        out_shape=(
            jax.ShapeDtypeStruct((share_rows, both_units // 2), jnp.bfloat16),
            jax.ShapeDtypeStruct((share_rows, both_units), jnp.bfloat16),
            jax.ShapeDtypeStruct(rows.shape, jnp.bfloat16),
        ),
        compiler_params=pltpu.CompilerParams(vmem_limit_bytes=32 * 1024 * 1024),
        cost_estimate=pl.CostEstimate(
            flops=flops, bytes_accessed=2 * weights.size, transcendentals=grad.size
        ),
    )(rows, weights, grad)


def gather_dp(parts, n_dp):
    copies = [jnp.broadcast_to(part[None], (n_dp, *part.shape)) for part in parts]
    copies = jnp.concatenate(copies, axis=2) if len(parts) > 1 else copies[0]
    got = lax.all_to_all(copies, "dp", split_axis=0, concat_axis=0, tiled=True)
    return got.reshape(-1, got.shape[2])


def on_device(tokens, expert_ids, gate_weight, up_weight, hidden_grad):
    n_zh = lax.axis_size("zh")
    n_dp = lax.axis_size("dp")
    near = ("zl", "c")
    tok_rows, width_part = tokens.shape
    top_k = expert_ids.shape[1]
    share_rows = hidden_grad.shape[1]
    hidden_units = gate_weight.shape[2]
    capacity = share_rows * n_dp // (n_zh * ZL * CORES)

    weights = gather_dp([gate_weight[0], up_weight[0]], n_dp)

    ids_rows = expert_ids.T.astype(jnp.bfloat16)
    sent = jnp.concatenate([tokens, ids_rows], axis=0)
    known = lax.all_gather(sent, "zh", axis=0, tiled=False)
    known_tokens = known[:, :tok_rows]
    known_ids = known[:, tok_rows:].astype(jnp.float32)

    n_near = ZL * CORES
    expert_of = lax.axis_index("zh") * n_near + jnp.arange(n_near, dtype=jnp.int32)
    expert_of = expert_of.astype(jnp.float32)[None, :, None]
    hit = jnp.zeros((n_zh, n_near, tok_rows), jnp.bool_)
    for choice_k in range(top_k):
        hit = hit | (known_ids[:, choice_k][:, None] == expert_of)
    earlier = jnp.arange(tok_rows)[:, None] < jnp.arange(tok_rows)[None, :]
    ranks = jnp.dot(
        hit.reshape(-1, tok_rows).astype(jnp.bfloat16),
        earlier.astype(jnp.bfloat16),
        preferred_element_type=jnp.float32,
    ).reshape(hit.shape)
    row_of = jnp.where(hit, ranks.astype(jnp.int32), -1)[:, :, None]
    placer = (
        (row_of == jnp.arange(capacity, dtype=jnp.int32)[:, None])
        .astype(jnp.bfloat16)
        .reshape(n_zh, n_near * capacity, tok_rows)
    )
    outgoing = lax.dot_general(
        placer, known_tokens, (((2,), (1,)), ((0,), (0,))), preferred_element_type=jnp.float32
    ).astype(jnp.bfloat16)
    outgoing = outgoing.reshape(n_zh, n_near, capacity, width_part).transpose(1, 0, 2, 3)
    outgoing, weights = lax.optimization_barrier((outgoing, weights))
    own_width = lax.all_to_all(outgoing, near, split_axis=0, concat_axis=0, tiled=True)
    own_width = own_width.transpose(1, 0, 2, 3)
    by_share = own_width.reshape(n_dp, share_rows, width_part)
    arrived = lax.all_to_all(by_share, "dp", split_axis=0, concat_axis=0, tiled=True)
    hidden, both_delta, slot_grad = experts(arrived, weights, hidden_grad[0])
    all_delta = lax.all_gather(both_delta, "dp", axis=0, tiled=True)
    def go_back(slot_grad, placer):
        back = lax.all_to_all(slot_grad, "dp", split_axis=0, concat_axis=0, tiled=True)
        back = back.reshape(n_zh, n_near, capacity, width_part).transpose(1, 0, 2, 3)
        returned = lax.all_to_all(back, near, split_axis=0, concat_axis=0, tiled=True)
        returned = returned.transpose(1, 0, 2, 3).reshape(n_zh, n_near * capacity, width_part)
        token_sum = lax.dot_general(
            placer, returned, (((1,), (1,)), ((0,), (0,))), preferred_element_type=jnp.float32
        )
        sums = lax.all_to_all(
            token_sum.astype(jnp.bfloat16), "zh", split_axis=0, concat_axis=0, tiled=True
        )
        return jnp.sum(sums.astype(jnp.float32), axis=0).astype(jnp.bfloat16)

    token_grad = lax.cond(
        expert_ids[0, 0] >= 0, go_back, lambda *_: jnp.zeros_like(tokens), slot_grad, placer
    )

    both_grad = lax.dot_general(
        own_width.reshape(n_dp * share_rows, width_part),
        all_delta,
        (((0,), (0,)), ((), ())),
        preferred_element_type=jnp.float32,
    )
    return (
        hidden[None],
        both_grad[None, :, :hidden_units],
        both_grad[None, :, hidden_units:],
        token_grad,
    )


def solution(mesh):
    n_expert, n_dp = mesh.devices.shape
    split = Mesh(mesh.devices.reshape(n_expert // (ZL * CORES), ZL, CORES, n_dp), ("zh", "zl", "c", "dp"))
    expert = ("zh", "zl", "c")
    placed = (
        P(expert, "dp"),
        P(expert, None),
        P(expert, "dp", None),
        P(expert, "dp", None),
        P(expert, "dp", None),
    )
    return jax.shard_map(
        on_device,
        mesh=split,
        in_specs=placed,
        out_specs=(
            P(expert, "dp", None),
            P(expert, "dp", None),
            P(expert, "dp", None),
            P(expert, "dp"),
        ),
        check_vma=False,
    )
```

time: 220 us -> 213 us (0.968)
  blocking collectives: 168 us -> 176 us
  local copies, waits for them, and re-layouts: 9.47 us -> 5.34 us
  starting transfers between devices: 11 us -> 7.21 us
  matrix products: 7.11 us -> 3.36 us
  waiting for transfers between devices: 3.3 us -> 0.04 us
  Pallas kernels: 0 us -> 2.53 us
    all_to_all x2, blocking collectives: 31.5 us -> 35.3 us  [the longest x1 18.7 us: go_back(): lax.all_to_all(back, near, split_axis=0, concat_axis=0, tiled=True)]
    ppermute x2 -> x0, starting transfers between devices: 3.83 us -> none  [the longest x1 1.92 us: go_back(): token_sum = kept + lax.ppermute(given, 'c', swap).astype(jnp.float32)]
    all_to_all x1, blocking collectives: 51.4 us -> 55 us  [go_back(): lax.all_to_all(token_sum.astype(jnp.bfloat16), 'zh', split_axis=0, concat...]
    dot_general x2 -> x0, matrix products: 3.46 us -> none  [the longest x1 1.79 us: on_device(): lax.dot_general(weights.reshape(n_dp, width_part, 2 * hidden_units), both...]
    ppermute x2 -> x0, waiting for transfers between devices: 3.26 us -> none  [the longest x1 1.76 us: on_device(): other = lax.ppermute(mine, 'c', swap)]
    pallas_call x0 -> x1, Pallas kernels: none -> 2.53 us  [experts(): pl.pallas_call(expert_kernel, out_shape=(jax.ShapeDtypeStruct((share_rows...]
  transfers between devices with their start and end apart: 4 -> 2, of which waited for: 2 -> 0; matrix products, arithmetic and copies ran while one was open for 4% -> 2% of each run, Pallas kernels for 0% -> 0%
where the time goes in v4:
time: 213 us; the launch traced here: 212 us
  blocking collectives  176 us (83%)
  between operations  14.8 us (7%)
  starting transfers between devices  7.21 us (3%)
  local copies, waits for them, and re-layouts  5.34 us (3%)
  matrix products  3.36 us (2%)
  other arithmetic  3.13 us (1%)
  Pallas kernels  2.53 us (1%)
    all_to_all x1, blocking collectives, go_back(): lax.all_to_all(token_sum.astype(jnp.bfloat16), 'zh', split_axis=0, concat...  55 us
    all_gather x1, blocking collectives, on_device(): known = lax.all_gather(sent, 'zh', axis=0, tiled=False)  53.4 us
    all_to_all x1, blocking collectives, go_back(): lax.all_to_all(back, near, split_axis=0, concat_axis=0, tiled=True)  18.7 us
    all_to_all x1, blocking collectives, on_device(): lax.all_to_all(by_share, 'dp', split_axis=0, concat_axis=0, tiled=True)  18.2 us
    all_to_all x1, blocking collectives, on_device(): lax.all_to_all(outgoing, near, split_axis=0, concat_axis=0, tiled=True)  16.6 us
    all_to_all x1, blocking collectives, go_back(): lax.all_to_all(slot_grad, 'dp', split_axis=0, concat_axis=0, tiled=True)  13.8 us
    all_to_all x1, starting transfers between devices, gather_dp(): got = lax.all_to_all(copies, 'dp', split_axis=0, concat_axis=0, tiled=True)  7.17 us
  transfers between devices with their start and end apart: 2, of which 0 were waited for; matrix products, arithmetic and copies ran while one was open for 2% of the time, Pallas kernels for 0%

profile of v4, /device:TPU:32, one launch (start us, length us, event | category | flops | bytes accessed | tf_op | source)
XLA Modules:
  0.0 212.2 jit_solution(5812409903309091929)
XLA Ops:
  7.2 1.1 broadcast_in_dim.33
  8.3 1.1 broadcast_in_dim.35
  9.4 2.0 pad_maximum_fusion
  11.3 0.0 copy-start.6
  11.3 0.0 copy-start.4
  11.4 7.2 %all-to-all-start.3 = ((bf16[16,128,768]{2,1,0:T(8,128)(2,1)}), bf16[16,128,768]{2,1,0:T(8,128)(2,1)S(1)}, u32[]{:S(2)}, u32[]{:S(2)}) async-start(bf16[16,128,768]{2,1,0:T(8,128)(2,1)} %pad_maximum_fusion), calls=%async_computation.3 | async-start | bytes 6291456 | tf_op jit(solution)/shard_map/all_to_all | solution.py:57
  18.5 0.0 all-gather.3.cloned.1.call-start
  18.6 0.1 eq.171
  18.7 0.0 copy-done.6
  18.7 0.0 copy-done.4
  18.7 53.4 %all-gather = bf16[1088,128]{1,0:T(8,128)(2,1)S(1)} all-gather(bf16[136,128]{1,0:T(8,128)(2,1)S(1)} %pad_maximum_fusion.1), channel_id=2, replica_groups=mesh['zh'=8,'zl'=4,'c'=2,'dp'=16] {'zh'}, dimensions={0}, use_global_device_ids=true | all-gather | bytes 313344 | tf_op jit(solution)/shard_map/all_gather | solution.py:75
  72.1 0.0 copy-start
  72.1 0.2 fusion
  72.3 1.1 fusion.28
  73.4 0.3 convolution_convert_fusion.1
  73.7 0.8 copy.23
  74.6 0.0 all-to-all-done.3
  74.6 16.6 %all_to_all.30 = bf16[8,8,32,128]{3,2,1,0:T(8,128)(2,1)S(1)} all-to-all(bf16[8,8,32,128]{3,2,1,0:T(8,128)(2,1)} %bitcast.51), channel_id=1, replica_groups=mesh['zh'=8,'zl'=4,'c'=2,'dp'=16] {'zl','c'}, dimensions={0} | all-to-all | bytes 1048576 | tf_op jit(solution)/shard_map/all_to_all | solution.py:102
  91.2 0.0 copy-start.1
  91.2 0.8 copy-done.1
  92.0 18.2 %all_to_all.31.rows_ref = bf16[16,128,128]{2,1,0:T(8,128)(2,1)S(1)} all-to-all(bf16[16,128,128]{2,1,0:T(8,128)(2,1)S(1)} %bitcast.49), channel_id=1, replica_groups=mesh['zh'=8,'zl'=4,'c'=2,'dp'=16] {'dp'}, dimensions={0} | all-to-all | bytes 1048576 | tf_op jit(solution)/shard_map/all_to_all | solution.py:105
  110.2 0.0 copy-done
  110.2 2.5 %shard_map.84 = (bf16[128,384]{1,0:T(8,128)(2,1)}, bf16[128,768]{1,0:T(8,128)(2,1)}, bf16[16,128,128]{2,1,0:T(8,128)(2,1)}) custom-call(bf16[16,128,128]{2,1,0:T(8,128)(2,1)S(1)} %all_to_all.31.rows_ref, bf16[2048,768]{1,0:T(8,128)(2,1)S(1)} %bitcast.47, bf16[128,384]{1,0:T(8,128)(2,1)S(1)} %bitcast.48), custom_call_target="tpu_custom_call" | custom-call | flops 805306368 | bytes 3145728 | tf_op jit(solution)/shard_map/pallas_call | solution.py:40
  112.7 0.0 all-gather.3.cloned.1.call-update
  112.8 0.5 slice.51
  113.9 0.0 copy-start.2
  113.9 88.1 %conditional.1 = (bf16[128,128]{1,0:T(8,128)(2,1)S(1)}) conditional(s32[]{:T(128)} %bitcast.28, () %tuple.16, (bf16[16,128,128]{2,1,0:T(8,128)(2,1)}, bf16[8,256,128]{2,1,0:T(8,128)(2,1)}) %tuple.17), branch_computations={%region_0.1_spmd, %region_1.3_spmd} | conditional | flops 67354624 | bytes 8421414 | solution.py:121
  114.0 0.0 copy-start.3
  114.0 13.8 %all_to_all.27 = bf16[16,128,128]{2,1,0:T(8,128)(2,1)S(1)} all-to-all(bf16[16,128,128]{2,1,0:T(8,128)(2,1)} %get-tuple-element.8), channel_id=1, replica_groups=mesh['zh'=8,'zl'=4,'c'=2,'dp'=16] {'dp'}, dimensions={0} | all-to-all | bytes 1048576 | tf_op jit(solution)/shard_map/cond/branch_1_fun/all_to_all | solution.py:109
  127.8 18.7 %all_to_all.28 = bf16[8,8,32,128]{3,2,1,0:T(8,128)(2,1)S(1)} all-to-all(bf16[8,8,32,128]{3,2,1,0:T(8,128)(2,1)S(1)} %copy.16), channel_id=1, replica_groups=mesh['zh'=8,'zl'=4,'c'=2,'dp'=16] {'zl','c'}, dimensions={0} | all-to-all | bytes 1048576 | tf_op jit(solution)/shard_map/cond/branch_1_fun/all_to_all | solution.py:111
  146.6 0.0 copy-done.3
  146.6 0.3 convolution_convert_fusion
  146.9 55.0 %all_to_all.29 = bf16[8,128,128]{2,1,0:T(8,128)(2,1)S(1)} all-to-all(bf16[8,128,128]{2,1,0:T(8,128)(2,1)S(1)} %convolution_convert_fusion), channel_id=1, replica_groups=mesh['zh'=8,'zl'=4,'c'=2,'dp'=16] {'zh'}, dimensions={0} | all-to-all | bytes 524288 | tf_op jit(solution)/shard_map/cond/branch_1_fun/all_to_all | solution.py:116
  202.0 0.0 copy-start.5
  202.0 0.0 all-gather.3.cloned.1.call-done
  202.0 0.0 copy-done.2
  202.0 2.5 %fusion.30 = f32[128,768]{1,0:T(8,128)S(1)} fusion(bf16[2048,128]{1,0:T(8,128)(2,1)S(1)} %bitcast.50, bf16[2048,768]{1,0:T(8,128)(2,1)} %all-gather.3.cloned.1.call-done), kind=kOutput, calls=%fused_computation.42 | convolution fusion | flops 402653184 | bytes 4063232 | tf_op jit(solution)/shard_map/dot_general | solution.py:125
  204.6 0.8 slice_bitcast_fusion
  205.3 0.0 copy-done.5
  (10 shorter events, 0.2 us)
Async XLA Ops:
  11.3 7.3 %copy-start.6 = (s32[128,8]{0,1:T(8,128)S(1)}, s32[128,8]{0,1:T(8,128)}, u32[]{:S(2)}) copy-start(s32[128,8]{0,1:T(8,128)} %param.8) | copy-start | bytes 12292
  11.3 7.3 %copy-start.4 = (bf16[128,128]{1,0:T(8,128)(2,1)S(1)}, bf16[128,128]{1,0:T(8,128)(2,1)}, u32[]{:S(2)}) copy-start(bf16[128,128]{1,0:T(8,128)(2,1)} %param.7) | copy-start | bytes 98308
  11.4 63.2 %all-to-all-start.3 = ((bf16[16,128,768]{2,1,0:T(8,128)(2,1)}), bf16[16,128,768]{2,1,0:T(8,128)(2,1)S(1)}, u32[]{:S(2)}, u32[]{:S(2)}) async-start(bf16[16,128,768]{2,1,0:T(8,128)(2,1)} %pad_maximum_fusion), calls=%async_computation.3 | async-start | bytes 6291456 | tf_op jit(solution)/shard_map/all_to_all | solution.py:57
  18.5 183.5 %all-gather.3.cloned.1.call-start = ((), (), s32[]{:S(2)}) async-start(), calls=%async_computation.6 | async-start | bytes 3342336 | tf_op jit(solution)/shard_map/all_gather | solution.py:107
  72.1 38.1 %copy-start = (bf16[1,128,384]{2,1,0:T(8,128)(2,1)S(1)}, bf16[1,128,384]{2,1,0:T(8,128)(2,1)}, u32[]{:S(2)}) copy-start(bf16[1,128,384]{2,1,0:T(8,128)(2,1)} %param.11) | copy-start | bytes 294916
  91.2 0.8 copy-start.1
  113.9 88.1 %copy-start.2 = (bf16[8,8,32,128]{3,2,0,1:T(8,128)(2,1)S(1)}, bf16[8,8,32,128]{3,2,0,1:T(8,128)(2,1)}, u32[]{:S(2)}) copy-start(bf16[8,8,32,128]{3,2,0,1:T(8,128)(2,1)} %copy-done.1) | copy-start | bytes 1572868
  114.0 32.6 %copy-start.3 = (bf16[8,256,128]{2,1,0:T(8,128)(2,1)S(1)}, bf16[8,256,128]{2,1,0:T(8,128)(2,1)}, u32[]{:S(2)}) copy-start(bf16[8,256,128]{2,1,0:T(8,128)(2,1)} %get-tuple-element.28) | copy-start | bytes 1572868 | tf_op jit(solution)/shard_map/cond
  202.0 3.3 %copy-start.5 = (bf16[128,128]{1,0:T(8,128)(2,1)}, bf16[128,128]{1,0:T(8,128)(2,1)S(1)}, u32[]{:S(2)}) copy-start(bf16[128,128]{1,0:T(8,128)(2,1)S(1)} %get-tuple-element.41) | copy-start | bytes 98308
Sparse Core Ops, SparseCore 0:
  112.9 76.5 all-gather.2

commit v5 on v4

v5 whole, which is shorter than its diff:
```python
import jax
import jax.numpy as jnp
from jax import lax
from jax.experimental import pallas as pl
from jax.experimental.pallas import tpu as pltpu
from jax.sharding import Mesh, PartitionSpec as P

CORES = 2
ZL = 4


def expert_kernel(rows_ref, gate_w_ref, up_w_ref, grad_ref, hidden_ref, delta_ref, slot_grad_ref):
    n_dp, _, width_part = rows_ref.shape
    hidden_units = grad_ref.shape[1]
    rows = jnp.concatenate([rows_ref[part] for part in range(n_dp)], axis=1)
    gate = jnp.dot(rows, gate_w_ref[...], preferred_element_type=jnp.float32)
    up = jnp.dot(rows, up_w_ref[...], preferred_element_type=jnp.float32)
    sigmoid_gate = jax.nn.sigmoid(gate)
    silu_gate = gate * sigmoid_gate
    hidden_ref[...] = (silu_gate * up).astype(jnp.bfloat16)
    grad = grad_ref[...].astype(jnp.float32)
    gate_delta = (grad * up * sigmoid_gate * (1.0 + gate * (1.0 - sigmoid_gate))).astype(
        jnp.bfloat16
    )
    up_delta = (grad * silu_gate).astype(jnp.bfloat16)
    delta_ref[:, :hidden_units] = gate_delta
    delta_ref[:, hidden_units:] = up_delta
    for part in range(n_dp):
        own = slice(part * width_part, (part + 1) * width_part)
        first = lax.dot_general(
            gate_delta,
            gate_w_ref[own],
            (((1,), (1,)), ((), ())),
            preferred_element_type=jnp.float32,
        )
        second = lax.dot_general(
            up_delta, up_w_ref[own], (((1,), (1,)), ((), ())), preferred_element_type=jnp.float32
        )
        slot_grad_ref[part] = (first + second).astype(jnp.bfloat16)


def experts(rows, gate_w, up_w, grad):
    share_rows, hidden_units = grad.shape
    return pl.pallas_call(
        expert_kernel,
        out_shape=(
            jax.ShapeDtypeStruct((share_rows, hidden_units), jnp.bfloat16),
            jax.ShapeDtypeStruct((share_rows, 2 * hidden_units), jnp.bfloat16),
            jax.ShapeDtypeStruct(rows.shape, jnp.bfloat16),
        ),
        compiler_params=pltpu.CompilerParams(vmem_limit_bytes=32 * 1024 * 1024),
        cost_estimate=pl.CostEstimate(
            flops=8 * share_rows * gate_w.size,
            bytes_accessed=4 * gate_w.size,
            transcendentals=grad.size,
        ),
    )(rows, gate_w, up_w, grad)


def weight_grad_kernel(rows_ref, delta_ref, gate_grad_ref, up_grad_ref):
    n_part, share_rows, _ = rows_ref.shape
    hidden_units = gate_grad_ref.shape[1]

    @pl.when(pl.program_id(0) == 0)
    def _():
        gate_grad_ref[...] = jnp.zeros_like(gate_grad_ref)
        up_grad_ref[...] = jnp.zeros_like(up_grad_ref)

    rows = rows_ref[...].reshape(n_part * share_rows, rows_ref.shape[2])
    both = lax.dot_general(
        rows, delta_ref[...], (((0,), (0,)), ((), ())), preferred_element_type=jnp.float32
    )
    gate_grad_ref[...] += both[:, :hidden_units]
    up_grad_ref[...] += both[:, hidden_units:]


def weight_grads(rows, delta):
    n_dp, share_rows, width_part = rows.shape
    both_units = delta.shape[1]
    step = n_dp // 4 if n_dp % 4 == 0 else n_dp
    out = jax.ShapeDtypeStruct((width_part, both_units // 2), jnp.float32)
    out_spec = pl.BlockSpec((width_part, both_units // 2), lambda i: (0, 0))
    return pl.pallas_call(
        weight_grad_kernel,
        grid=(n_dp // step,),
        in_specs=[
            pl.BlockSpec((step, share_rows, width_part), lambda i: (i, 0, 0)),
            pl.BlockSpec((step * share_rows, both_units), lambda i: (i, 0)),
        ],
        out_specs=(out_spec, out_spec),
        out_shape=(out, out),
        compiler_params=pltpu.CompilerParams(vmem_limit_bytes=32 * 1024 * 1024),
        cost_estimate=pl.CostEstimate(
            flops=2 * rows.size * both_units, bytes_accessed=2 * delta.size, transcendentals=0
        ),
    )(rows, delta)


def on_device(tokens, expert_ids, gate_weight, up_weight, hidden_grad):
    n_zh = lax.axis_size("zh")
    n_dp = lax.axis_size("dp")
    near = ("zl", "c")
    tok_rows, width_part = tokens.shape
    top_k = expert_ids.shape[1]
    share_rows = hidden_grad.shape[1]
    hidden_units = gate_weight.shape[2]
    capacity = share_rows * n_dp // (n_zh * ZL * CORES)

    n_near = ZL * CORES

    up_rows = lax.all_gather(up_weight, "dp", axis=1, tiled=True)[0]

    def go_out(tokens, expert_ids, gate_weight):
        copies = jnp.broadcast_to(gate_weight, (n_dp, width_part, hidden_units))
        gate_rows = lax.all_to_all(copies, "dp", split_axis=0, concat_axis=0, tiled=True)
        gate_rows = gate_rows.reshape(-1, hidden_units)

        ids_rows = expert_ids.T.astype(jnp.bfloat16)
        sent = jnp.concatenate([tokens, ids_rows], axis=0)
        known = lax.all_gather(sent, "zh", axis=0, tiled=False)
        known_tokens = known[:, :tok_rows]
        known_ids = known[:, tok_rows:].astype(jnp.float32)

        expert_of = lax.axis_index("zh") * n_near + jnp.arange(n_near, dtype=jnp.int32)
        expert_of = expert_of.astype(jnp.float32)[None, :, None]
        hit = jnp.zeros((n_zh, n_near, tok_rows), jnp.bool_)
        for choice_k in range(top_k):
            hit = hit | (known_ids[:, choice_k][:, None] == expert_of)
        earlier = jnp.arange(tok_rows)[:, None] < jnp.arange(tok_rows)[None, :]
        ranks = jnp.dot(
            hit.reshape(-1, tok_rows).astype(jnp.bfloat16),
            earlier.astype(jnp.bfloat16),
            preferred_element_type=jnp.float32,
        ).reshape(hit.shape)
        row_of = jnp.where(hit, ranks.astype(jnp.int32), -1)[:, :, None]
        placer = (
            (row_of == jnp.arange(capacity, dtype=jnp.int32)[:, None])
            .astype(jnp.bfloat16)
            .reshape(n_zh, n_near * capacity, tok_rows)
        )
        outgoing = lax.dot_general(
            placer, known_tokens, (((2,), (1,)), ((0,), (0,))), preferred_element_type=jnp.float32
        ).astype(jnp.bfloat16)
        outgoing = outgoing.reshape(n_zh, n_near, capacity, width_part).transpose(1, 0, 2, 3)
        outgoing, gate_rows = lax.optimization_barrier((outgoing, gate_rows))
        own_width = lax.all_to_all(outgoing, near, split_axis=0, concat_axis=0, tiled=True)
        own_width = own_width.transpose(1, 0, 2, 3)
        by_share = own_width.reshape(n_dp, share_rows, width_part)
        arrived = lax.all_to_all(by_share, "dp", split_axis=0, concat_axis=0, tiled=True)
        return gate_rows, placer, by_share, arrived

    def stay(tokens, expert_ids, gate_weight):
        return (
            jnp.zeros((n_dp * width_part, hidden_units), jnp.bfloat16),
            jnp.zeros((n_zh, n_near * capacity, tok_rows), jnp.bfloat16),
            jnp.zeros((n_dp, share_rows, width_part), jnp.bfloat16),
            jnp.zeros((n_dp, share_rows, width_part), jnp.bfloat16),
        )

    taken = expert_ids[0, 0] >= 0
    gate_rows, placer, by_share, arrived = lax.cond(
        taken, go_out, stay, tokens, expert_ids, gate_weight
    )
    hidden, both_delta, slot_grad = experts(arrived, gate_rows, up_rows, hidden_grad[0])
    all_delta = lax.all_gather(both_delta, "dp", axis=0, tiled=True)
    def go_back(slot_grad, placer):
        back = lax.all_to_all(slot_grad, "dp", split_axis=0, concat_axis=0, tiled=True)
        back = back.reshape(n_zh, n_near, capacity, width_part).transpose(1, 0, 2, 3)
        returned = lax.all_to_all(back, near, split_axis=0, concat_axis=0, tiled=True)
        returned = returned.transpose(1, 0, 2, 3).reshape(n_zh, n_near * capacity, width_part)
        token_sum = lax.dot_general(
            placer, returned, (((1,), (1,)), ((0,), (0,))), preferred_element_type=jnp.float32
        )
        sums = lax.all_to_all(
            token_sum.astype(jnp.bfloat16), "zh", split_axis=0, concat_axis=0, tiled=True
        )
        return jnp.sum(sums.astype(jnp.float32), axis=0).astype(jnp.bfloat16)

    token_grad = lax.cond(
        taken, go_back, lambda *_: jnp.zeros_like(tokens), slot_grad, placer
    )

    gate_grad, up_grad = weight_grads(by_share, all_delta)
    return hidden[None], gate_grad[None], up_grad[None], token_grad


def solution(mesh):
    n_expert, n_dp = mesh.devices.shape
    split = Mesh(mesh.devices.reshape(n_expert // (ZL * CORES), ZL, CORES, n_dp), ("zh", "zl", "c", "dp"))
    expert = ("zh", "zl", "c")
    placed = (
        P(expert, "dp"),
        P(expert, None),
        P(expert, "dp", None),
        P(expert, "dp", None),
        P(expert, "dp", None),
    )
    return jax.shard_map(
        on_device,
        mesh=split,
        in_specs=placed,
        out_specs=(
            P(expert, "dp", None),
            P(expert, "dp", None),
            P(expert, "dp", None),
            P(expert, "dp"),
        ),
        check_vma=False,
    )
```

time: 213 us -> 215 us (level)
  Pallas kernels: 2.53 us -> 6.98 us
  other arithmetic: 3.13 us -> 0.33 us
  local copies, waits for them, and re-layouts: 5.34 us -> 7.86 us
  matrix products: 3.36 us -> 0.86 us
    pallas_call x0 -> x1, Pallas kernels: none -> 3.55 us  [weight_grads(): pl.pallas_call(weight_grad_kernel, grid=(n_dp // step,), in_specs=[pl.Blo...]
    dot_general x3 -> x2, matrix products: 3.02 us -> 0.51 us  [the longest x1 0.29 us: go_out(): lax.dot_general(placer, known_tokens, (((2,), (1,)), ((0,), (0,))), prefe...]
    unnamed x12 -> x8, local copies, waits for them, and re-layouts: 0.81 us -> 3.3 us
  transfers between devices with their start and end apart: 2 -> 3, of which waited for: 0 -> 0; matrix products, arithmetic and copies ran while one was open for 2% -> 3% of each run, Pallas kernels for 0% -> 0%
where the time goes in v5:
time: 215 us
  blocking collectives  176 us (82%)
  between operations  14.7 us (7%)
  local copies, waits for them, and re-layouts  7.86 us (4%)
  starting transfers between devices  7.29 us (3%)
  Pallas kernels  6.98 us (3%)
    all_to_all x1, blocking collectives, go_back(): lax.all_to_all(token_sum.astype(jnp.bfloat16), 'zh', split_axis=0, concat...  55.8 us
    all_gather x1, blocking collectives, go_out(): known = lax.all_gather(sent, 'zh', axis=0, tiled=False)  53.5 us
    all_to_all x1, blocking collectives, go_back(): lax.all_to_all(back, near, split_axis=0, concat_axis=0, tiled=True)  18.8 us
    all_to_all x1, blocking collectives, go_out(): lax.all_to_all(by_share, 'dp', split_axis=0, concat_axis=0, tiled=True)  18 us
    all_to_all x1, blocking collectives, go_out(): lax.all_to_all(outgoing, near, split_axis=0, concat_axis=0, tiled=True)  16.2 us
    all_to_all x1, blocking collectives, go_back(): lax.all_to_all(slot_grad, 'dp', split_axis=0, concat_axis=0, tiled=True)  13.3 us
    all_to_all x1, starting transfers between devices, go_out(): lax.all_to_all(copies, 'dp', split_axis=0, concat_axis=0, tiled=True)  7.21 us
  transfers between devices with their start and end apart: 3, of which 0 were waited for; matrix products, arithmetic and copies ran while one was open for 3% of the time, Pallas kernels for 0%

profile of v5, /device:TPU:32, one launch (start us, length us, event | category | flops | bytes accessed | tf_op | source)
XLA Modules:
  0.0 214.5 jit_solution(14119344163072128868)
XLA Ops:
  7.2 0.0 all-gather.4.cloned.1.call-start
  7.2 0.7 all-gather.4.cloned.1.call-update
  7.9 0.0 all-gather.6.cloned.1.call-start
  7.9 1.2 slice.33
  9.8 0.0 copy-start.2
  9.8 99.1 %conditional.2 = (bf16[2048,384]{1,0:T(8,128)(2,1)}, bf16[8,256,128]{2,1,0:T(8,128)(2,1)S(1)}, bf16[16,128,128]{2,1,0:T(8,128)(2,1)}, bf16[16,128,128]{2,1,0:T(8,128)(2,1)S(1)}) conditional(s32[]{:T(128)} %bitcast.23, () %tuple.23, (s32[128,8]{0,1:T(8,128)}, bf16[128,128]{1,0:T(8,128)(2,1)}, bf16[1,128,384]{2,1,0:T(8,128)(2,1)}) %tuple.24), branch_computations={%region_0.0_spmd, %region_1.2_spmd} | conditional | flops 70349840 | bytes 13172968 | solution.py:161
  9.8 2.3 %broadcast_in_dim.18 = bf16[16,128,384]{2,1,0:T(8,128)(2,1)} broadcast(bf16[128,384]{1,0:T(8,128)(2,1)} %bitcast.50), dimensions={1,2} | broadcast | bytes 1671168 | tf_op jit(solution)/shard_map/cond/branch_1_fun/broadcast_in_dim | solution.py:114
  12.1 0.0 copy-start.5
  12.1 0.0 copy-start.3
  12.1 7.2 %all-to-all-start = ((bf16[16,128,384]{2,1,0:T(8,128)(2,1)}), bf16[16,128,384]{2,1,0:T(8,128)(2,1)}, u32[]{:S(2)}, u32[]{:S(2)}) async-start(bf16[16,128,384]{2,1,0:T(8,128)(2,1)} %broadcast_in_dim.18), calls=%async_computation | async-start | bytes 3145728 | tf_op jit(solution)/shard_map/cond/branch_1_fun/all_to_all | solution.py:115
  19.4 0.1 eq.140
  19.4 0.0 copy-done.5
  19.4 0.0 copy-done.3
  19.5 53.5 %all-gather = bf16[1088,128]{1,0:T(8,128)(2,1)S(1)} all-gather(bf16[136,128]{1,0:T(8,128)(2,1)S(1)} %pad_maximum_fusion), channel_id=2, replica_groups=mesh['zh'=8,'zl'=4,'c'=2,'dp'=16] {'zh'}, dimensions={0}, use_global_device_ids=true | all-gather | bytes 313344 | tf_op jit(solution)/shard_map/cond/branch_1_fun/all_gather | solution.py:120
  73.0 0.2 fusion
  73.2 0.3 fusion.28
  73.5 0.3 convolution_convert_fusion
  73.8 0.0 all-to-all-done
  73.8 16.2 %all_to_all.24 = bf16[8,8,32,128]{3,2,1,0:T(8,128)(2,1)S(1)} all-to-all(bf16[8,8,32,128]{3,2,1,0:T(8,128)(2,1)S(1)} %bitcast.43), channel_id=1, replica_groups=mesh['zh'=8,'zl'=4,'c'=2,'dp'=16] {'zl','c'}, dimensions={0} | all-to-all | bytes 1048576 | tf_op jit(solution)/shard_map/cond/branch_1_fun/all_to_all | solution.py:146
  90.0 0.8 copy.16
  90.9 18.0 %all_to_all.25 = bf16[16,128,128]{2,1,0:T(8,128)(2,1)S(1)} all-to-all(bf16[16,128,128]{2,1,0:T(8,128)(2,1)} %bitcast.17), channel_id=1, replica_groups=mesh['zh'=8,'zl'=4,'c'=2,'dp'=16] {'dp'}, dimensions={0} | all-to-all | bytes 1048576 | tf_op jit(solution)/shard_map/cond/branch_1_fun/all_to_all | solution.py:149
  108.9 0.0 all-gather.4.cloned.1.call-done
  108.9 0.0 copy-done.2
  108.9 0.0 copy-start.1
  108.9 1.4 copy-done.1
  110.3 3.4 %shard_map.86 = (bf16[128,384]{1,0:T(8,128)(2,1)}, bf16[128,768]{1,0:T(8,128)(2,1)}, bf16[16,128,128]{2,1,0:T(8,128)(2,1)S(1)}) custom-call(bf16[16,128,128]{2,1,0:T(8,128)(2,1)S(1)} %get-tuple-element.33.rows_ref, bf16[2048,384]{1,0:T(8,128)(2,1)} %get-tuple-element.34.gate_w_ref, bf16[2048,384]{1,0:T(8,128)(2,1)S(1)} %bitcast.41, bf16[128,384]{1,0:T(8,128)(2,1)S(1)} %bitcast.42), custom_call_target="tpu_custom_call" | custom-call | flops 805306368 | bytes 3145728 | tf_op jit(solution)/shard_map/pallas_call | solution.py:44
  113.7 0.0 all-gather.6.cloned.1.call-update
  113.7 88.4 %conditional.3 = (bf16[128,128]{1,0:T(8,128)(2,1)S(1)}) conditional(s32[]{:T(128)} %bitcast.23, () %tuple.25, (bf16[16,128,128]{2,1,0:T(8,128)(2,1)S(1)}, bf16[8,256,128]{2,1,0:T(8,128)(2,1)S(1)}) %tuple.26), branch_computations={%region_2.3_spmd, %region_3.5_spmd} | conditional | flops 67354624 | bytes 6324234 | solution.py:179
  113.8 13.3 %all_to_all.26 = bf16[16,128,128]{2,1,0:T(8,128)(2,1)S(1)} all-to-all(bf16[16,128,128]{2,1,0:T(8,128)(2,1)S(1)} %get-tuple-element.19), channel_id=1, replica_groups=mesh['zh'=8,'zl'=4,'c'=2,'dp'=16] {'dp'}, dimensions={0} | all-to-all | bytes 1048576 | tf_op jit(solution)/shard_map/cond/branch_1_fun/all_to_all | solution.py:167
  127.2 18.8 %all_to_all.27 = bf16[8,8,32,128]{3,2,1,0:T(8,128)(2,1)S(1)} all-to-all(bf16[8,8,32,128]{3,2,1,0:T(8,128)(2,1)S(1)} %copy.17), channel_id=1, replica_groups=mesh['zh'=8,'zl'=4,'c'=2,'dp'=16] {'zl','c'}, dimensions={0} | all-to-all | bytes 1048576 | tf_op jit(solution)/shard_map/cond/branch_1_fun/all_to_all | solution.py:169
  146.0 0.4 convolution_convert_fusion.2
  146.4 55.8 %all_to_all.28 = bf16[8,128,128]{2,1,0:T(8,128)(2,1)S(1)} all-to-all(bf16[8,128,128]{2,1,0:T(8,128)(2,1)S(1)} %convolution_convert_fusion.2), channel_id=1, replica_groups=mesh['zh'=8,'zl'=4,'c'=2,'dp'=16] {'zh'}, dimensions={0} | all-to-all | bytes 524288 | tf_op jit(solution)/shard_map/cond/branch_1_fun/all_to_all | solution.py:174
  202.2 0.0 copy-start.4
  202.2 0.0 all-gather.6.cloned.1.call-done.delta_ref
  202.2 0.0 copy-start
  202.2 1.9 copy-done
  204.1 3.6 %shard_map.87 = (f32[128,384]{1,0:T(8,128)}, f32[128,384]{1,0:T(8,128)}) custom-call(bf16[16,128,128]{2,1,0:T(8,128)(2,1)} %get-tuple-element.36.rows_ref, bf16[2048,768]{1,0:T(8,128)(2,1)S(1)} %copy-done), custom_call_target="tpu_custom_call" | custom-call | flops 402653184 | bytes 3145728 | tf_op jit(solution)/shard_map/pallas_call | solution.py:83
  207.7 0.0 copy-done.4
  (10 shorter events, 0.2 us)
Async XLA Ops:
  7.2 101.7 %all-gather.4.cloned.1.call-start = ((), (), s32[]{:S(2)}) async-start(), calls=%async_computation.6 | async-start | bytes 1671168 | tf_op jit(solution)/shard_map/all_gather | solution.py:111
  7.9 194.3 %all-gather.6.cloned.1.call-start = ((), (), s32[]{:S(2)}) async-start(), calls=%async_computation.7 | async-start | bytes 3342336 | tf_op jit(solution)/shard_map/all_gather | solution.py:165
  9.8 99.1 %copy-start.2 = (bf16[1,128,384]{2,1,0:T(8,128)(2,1)S(1)}, bf16[1,128,384]{2,1,0:T(8,128)(2,1)}, u32[]{:S(2)}) copy-start(bf16[1,128,384]{2,1,0:T(8,128)(2,1)} %param.13) | copy-start | bytes 294916
  12.1 7.3 %copy-start.5 = (s32[128,8]{0,1:T(8,128)S(1)}, s32[128,8]{0,1:T(8,128)}, u32[]{:S(2)}) copy-start(s32[128,8]{0,1:T(8,128)} %get-tuple-element.14) | copy-start | bytes 12292 | tf_op jit(solution)/shard_map/cond
  12.1 7.3 %copy-start.3 = (bf16[128,128]{1,0:T(8,128)(2,1)S(1)}, bf16[128,128]{1,0:T(8,128)(2,1)}, u32[]{:S(2)}) copy-start(bf16[128,128]{1,0:T(8,128)(2,1)} %get-tuple-element.44) | copy-start | bytes 98308 | tf_op jit(solution)/shard_map/cond
  12.1 61.7 %all-to-all-start = ((bf16[16,128,384]{2,1,0:T(8,128)(2,1)}), bf16[16,128,384]{2,1,0:T(8,128)(2,1)}, u32[]{:S(2)}, u32[]{:S(2)}) async-start(bf16[16,128,384]{2,1,0:T(8,128)(2,1)} %broadcast_in_dim.18), calls=%async_computation | async-start | bytes 3145728 | tf_op jit(solution)/shard_map/cond/branch_1_fun/all_to_all | solution.py:115
  108.9 1.4 copy-start.1
  202.2 5.5 %copy-start.4 = (bf16[128,128]{1,0:T(8,128)(2,1)}, bf16[128,128]{1,0:T(8,128)(2,1)S(1)}, u32[]{:S(2)}) copy-start(bf16[128,128]{1,0:T(8,128)(2,1)S(1)} %get-tuple-element.70) | copy-start | bytes 98308
  202.2 1.9 copy-start
Sparse Core Ops, SparseCore 0:
  12.2 86.9 all-gather.3
  113.9 77.9 all-gather.5

commit v6 on v4

--- a/solution.py
+++ b/solution.py
@@ -7,6 +7,7 @@
 
 CORES = 2
 ZL = 4
+DP_X = 4
 
 
 def expert_kernel(rows_ref, weights_ref, grad_ref, hidden_ref, delta_ref, slot_grad_ref):
@@ -51,16 +52,76 @@
     )(rows, weights, grad)
 
 
-def gather_dp(parts, n_dp):
-    copies = [jnp.broadcast_to(part[None], (n_dp, *part.shape)) for part in parts]
-    copies = jnp.concatenate(copies, axis=2) if len(parts) > 1 else copies[0]
-    got = lax.all_to_all(copies, "dp", split_axis=0, concat_axis=0, tiled=True)
-    return got.reshape(-1, got.shape[2])
+def copies_kernel(gate_ref, up_ref, out_ref, rows, sems):
+    hidden_units = gate_ref.shape[2]
+    rows[:, :hidden_units] = gate_ref[0]
+    rows[:, hidden_units:] = up_ref[0]
+    copies = [
+        pltpu.make_async_copy(rows, out_ref.at[part], sems.at[part])
+        for part in range(out_ref.shape[0])
+    ]
+    for copy in copies:
+        copy.start()
+    for copy in copies:
+        copy.wait()
+
+
+def weight_copies(gate_w, up_w, n_dp):
+    _, rows, hidden_units = gate_w.shape
+    return pl.pallas_call(
+        copies_kernel,
+        out_shape=jax.ShapeDtypeStruct((n_dp, rows, 2 * hidden_units), gate_w.dtype),
+        out_specs=pl.BlockSpec(memory_space=pl.ANY),
+        scratch_shapes=[
+            pltpu.VMEM((rows, 2 * hidden_units), gate_w.dtype),
+            pltpu.SemaphoreType.DMA((n_dp,)),
+        ],
+    )(gate_w, up_w)
+
+
+def weight_grad_kernel(order_ref, rows_ref, *refs):
+    delta_refs, (gate_grad_ref, up_grad_ref) = refs[:-2], refs[-2:]
+    share_rows = rows_ref.shape[1]
+    hidden_units = gate_grad_ref.shape[1]
+    n_x = rows_ref.shape[0] // len(delta_refs)
+    total = jnp.zeros((rows_ref.shape[2], 2 * hidden_units), jnp.float32)
+    for block, delta_ref in enumerate(delta_refs):
+        rows = jnp.concatenate(
+            [rows_ref[order_ref[block * n_x + part]] for part in range(n_x)], axis=0
+        )
+        total = total + lax.dot_general(
+            rows, delta_ref[...], (((0,), (0,)), ((), ())), preferred_element_type=jnp.float32
+        )
+    gate_grad_ref[...] = total[:, :hidden_units]
+    up_grad_ref[...] = total[:, hidden_units:]
+
+
+def weight_grads(order, rows, deltas):
+    both_units = deltas[0].shape[1]
+    out = jax.ShapeDtypeStruct((rows.shape[2], both_units // 2), jnp.float32)
+    in_vmem = pl.BlockSpec(memory_space=pltpu.VMEM)
+    return pl.pallas_call(
+        weight_grad_kernel,
+        in_specs=[pl.BlockSpec(memory_space=pltpu.SMEM)] + [in_vmem] * (1 + len(deltas)),
+        out_shape=(out, out),
+        compiler_params=pltpu.CompilerParams(vmem_limit_bytes=32 * 1024 * 1024),
+        cost_estimate=pl.CostEstimate(
+            flops=2 * rows.size * both_units, bytes_accessed=2 * rows.size, transcendentals=0
+        ),
+    )(order, rows, *deltas)
+
+
+def blocks_along(block, axis):
+    n = lax.axis_size(axis)
+    steps = [[(i, (i - k) % n) for i in range(n)] for k in range(1, n)]
+    return [block] + [lax.ppermute(block, axis, step) for step in steps]
 
 
 def on_device(tokens, expert_ids, gate_weight, up_weight, hidden_grad):
     n_zh = lax.axis_size("zh")
-    n_dp = lax.axis_size("dp")
+    dp = ("x", "y")
+    n_x, n_y = lax.axis_size("x"), lax.axis_size("y")
+    n_dp = n_x * n_y
     near = ("zl", "c")
     tok_rows, width_part = tokens.shape
     top_k = expert_ids.shape[1]
@@ -68,7 +129,9 @@
     hidden_units = gate_weight.shape[2]
     capacity = share_rows * n_dp // (n_zh * ZL * CORES)
 
-    weights = gather_dp([gate_weight[0], up_weight[0]], n_dp)
+    weights = weight_copies(gate_weight, up_weight, n_dp)
+    weights = lax.all_to_all(weights, dp, split_axis=0, concat_axis=0, tiled=True)
+    weights = weights.reshape(-1, 2 * hidden_units)
 
     ids_rows = expert_ids.T.astype(jnp.bfloat16)
     sent = jnp.concatenate([tokens, ids_rows], axis=0)
@@ -102,11 +165,13 @@
     own_width = lax.all_to_all(outgoing, near, split_axis=0, concat_axis=0, tiled=True)
     own_width = own_width.transpose(1, 0, 2, 3)
     by_share = own_width.reshape(n_dp, share_rows, width_part)
-    arrived = lax.all_to_all(by_share, "dp", split_axis=0, concat_axis=0, tiled=True)
+    arrived = lax.all_to_all(by_share, dp, split_axis=0, concat_axis=0, tiled=True)
     hidden, both_delta, slot_grad = experts(arrived, weights, hidden_grad[0])
-    all_delta = lax.all_gather(both_delta, "dp", axis=0, tiled=True)
-    def go_back(slot_grad, placer):
-        back = lax.all_to_all(slot_grad, "dp", split_axis=0, concat_axis=0, tiled=True)
+
+    def swap_shares(slot_grad):
+        return lax.all_to_all(slot_grad, dp, split_axis=0, concat_axis=0, tiled=True)
+
+    def go_back(back, placer):
         back = back.reshape(n_zh, n_near, capacity, width_part).transpose(1, 0, 2, 3)
         returned = lax.all_to_all(back, near, split_axis=0, concat_axis=0, tiled=True)
         returned = returned.transpose(1, 0, 2, 3).reshape(n_zh, n_near * capacity, width_part)
@@ -118,44 +183,43 @@
         )
         return jnp.sum(sums.astype(jnp.float32), axis=0).astype(jnp.bfloat16)
 
-    token_grad = lax.cond(
-        expert_ids[0, 0] >= 0, go_back, lambda *_: jnp.zeros_like(tokens), slot_grad, placer
-    )
-
-    both_grad = lax.dot_general(
-        own_width.reshape(n_dp * share_rows, width_part),
-        all_delta,
-        (((0,), (0,)), ((), ())),
-        preferred_element_type=jnp.float32,
-    )
-    return (
-        hidden[None],
-        both_grad[None, :, :hidden_units],
-        both_grad[None, :, hidden_units:],
-        token_grad,
-    )
+    taken = expert_ids[0, 0] >= 0
+    along_x = jnp.concatenate(blocks_along(both_delta, "x"), axis=0)
+    back = lax.cond(taken, swap_shares, jnp.zeros_like, slot_grad)
+    along_x, back = lax.optimization_barrier((along_x, back))
+    deltas = blocks_along(along_x, "y")
+    token_grad = lax.cond(taken, go_back, lambda *_: jnp.zeros_like(tokens), back, placer)
+
+    place_x = (lax.axis_index("x") + jnp.arange(n_x, dtype=jnp.int32)) % n_x
+    place_y = (lax.axis_index("y") + jnp.arange(n_y, dtype=jnp.int32)) % n_y
+    order = (place_x[None, :] * n_y + place_y[:, None]).reshape(n_dp)
+    gate_grad, up_grad = weight_grads(order, by_share, deltas)
+    return hidden[None], gate_grad[None], up_grad[None], token_grad
 
 
 def solution(mesh):
     n_expert, n_dp = mesh.devices.shape
-    split = Mesh(mesh.devices.reshape(n_expert // (ZL * CORES), ZL, CORES, n_dp), ("zh", "zl", "c", "dp"))
-    expert = ("zh", "zl", "c")
+    split = Mesh(
+        mesh.devices.reshape(n_expert // (ZL * CORES), ZL, CORES, DP_X, n_dp // DP_X),
+        ("zh", "zl", "c", "x", "y"),
+    )
+    expert, dp = ("zh", "zl", "c"), ("x", "y")
     placed = (
-        P(expert, "dp"),
+        P(expert, dp),
         P(expert, None),
-        P(expert, "dp", None),
-        P(expert, "dp", None),
-        P(expert, "dp", None),
+        P(expert, dp, None),
+        P(expert, dp, None),
+        P(expert, dp, None),
     )
     return jax.shard_map(
         on_device,
         mesh=split,
         in_specs=placed,
         out_specs=(
-            P(expert, "dp", None),
-            P(expert, "dp", None),
-            P(expert, "dp", None),
-            P(expert, "dp"),
+            P(expert, dp, None),
+            P(expert, dp, None),
+            P(expert, dp, None),
+            P(expert, dp),
         ),
         check_vma=False,
     )

time: 213 us -> 218 us (1.023)
  the two profiles are of different devices: /device:TPU:32 before, /device:TPU:48 now
where the time goes in v6:
time: 218 us; the launch traced here: 217 us
  blocking collectives  175 us (80%)
  starting transfers between devices  26.7 us (12%)
  Pallas kernels  7.81 us (4%)
  local copies, waits for them, and re-layouts  4.4 us (2%)
    all_to_all x1, blocking collectives, go_back(): lax.all_to_all(token_sum.astype(jnp.bfloat16), 'zh', split_axis=0, concat...  55.1 us
    all_gather x1, blocking collectives, on_device(): known = lax.all_gather(sent, 'zh', axis=0, tiled=False)  53.4 us
    ppermute x6, starting transfers between devices, blocks_along(): return [block] + [lax.ppermute(block, axis, step) for step in steps]  19.4 us
    all_to_all x1, blocking collectives, go_back(): lax.all_to_all(back, near, split_axis=0, concat_axis=0, tiled=True)  18.3 us
    all_to_all x1, blocking collectives, on_device(): lax.all_to_all(outgoing, near, split_axis=0, concat_axis=0, tiled=True)  17.1 us
    all_to_all x1, blocking collectives, on_device(): lax.all_to_all(by_share, dp, split_axis=0, concat_axis=0, tiled=True)  15.5 us
    all_to_all x1, blocking collectives, swap_shares(): lax.all_to_all(slot_grad, dp, split_axis=0, concat_axis=0, tiled=True)  15.3 us
    all_to_all x1, starting transfers between devices, on_device(): lax.all_to_all(weights, dp, split_axis=0, concat_axis=0, tiled=True)  7.29 us
  transfers between devices with their start and end apart: 7, of which 0 were waited for; matrix products, arithmetic and copies ran while one was open for 2% of the time, Pallas kernels for 0%

profile of v6, /device:TPU:48, one launch (start us, length us, event | category | flops | bytes accessed | tf_op | source)
XLA Modules:
  0.0 217.3 jit_solution(4951550285972119080)
XLA Ops:
  0.6 2.8 %shard_map.84 = bf16[16,128,768]{2,1,0:T(8,128)(2,1)} custom-call(bf16[1,128,384]{2,1,0:T(8,128)(2,1)} %gate_ref.1, bf16[1,128,384]{2,1,0:T(8,128)(2,1)} %up_ref.1), custom_call_target="tpu_custom_call" | custom-call | tf_op jit(solution)/shard_map/pallas_call | solution.py:71
  3.4 0.0 copy-start.7
  3.4 0.0 copy-start.5
  3.4 7.3 %all-to-all-start.3 = ((bf16[16,128,768]{2,1,0:T(8,128)(2,1)}), bf16[16,128,768]{2,1,0:T(8,128)(2,1)S(1)}, u32[]{:S(2)}, u32[]{:S(2)}) async-start(bf16[16,128,768]{2,1,0:T(8,128)(2,1)} %shard_map.84), calls=%async_computation.3 | async-start | bytes 6291456 | tf_op jit(solution)/shard_map/all_to_all | solution.py:133
  10.7 0.1 eq.174
  10.8 0.0 copy-done.7
  10.8 0.0 copy-done.5
  10.8 53.4 %all-gather = bf16[1088,128]{1,0:T(8,128)(2,1)S(1)} all-gather(bf16[136,128]{1,0:T(8,128)(2,1)S(1)} %pad_maximum_fusion.1), channel_id=2, replica_groups=mesh['zh'=8,'zl'=4,'c'=2,'x'=4,'y'=4] {'zh'}, dimensions={0}, use_global_device_ids=true | all-gather | bytes 313344 | tf_op jit(solution)/shard_map/all_gather | solution.py:138
  64.2 0.2 fusion
  64.4 1.1 fusion.31
  65.5 0.3 convolution_convert_fusion.1
  65.8 0.8 copy.23
  66.6 0.0 all-to-all-done.3
  66.7 0.0 copy-start.2
  66.7 17.1 %all_to_all.30 = bf16[8,8,32,128]{3,2,1,0:T(8,128)(2,1)S(1)} all-to-all(bf16[8,8,32,128]{3,2,1,0:T(8,128)(2,1)} %bitcast.42), channel_id=1, replica_groups=mesh['zh'=8,'zl'=4,'c'=2,'x'=4,'y'=4] {'zl','c'}, dimensions={0} | all-to-all | bytes 1048576 | tf_op jit(solution)/shard_map/all_to_all | solution.py:165
  83.8 15.5 %all_to_all.31.rows_ref = bf16[16,128,128]{2,1,0:T(8,128)(2,1)S(1)} all-to-all(bf16[16,128,128]{2,1,0:T(8,128)(2,1)S(1)} %bitcast.39), channel_id=1, replica_groups=mesh['zh'=8,'zl'=4,'c'=2,'x'=4,'y'=4] {'x','y'}, dimensions={0} | all-to-all | bytes 1048576 | tf_op jit(solution)/shard_map/all_to_all | solution.py:168
  99.3 0.8 copy-done
  100.1 0.0 copy-done.2
  100.1 2.5 %shard_map.85 = (bf16[128,384]{1,0:T(8,128)(2,1)}, bf16[128,768]{1,0:T(8,128)(2,1)S(1)}, bf16[16,128,128]{2,1,0:T(8,128)(2,1)}) custom-call(bf16[16,128,128]{2,1,0:T(8,128)(2,1)S(1)} %all_to_all.31.rows_ref, bf16[2048,768]{1,0:T(8,128)(2,1)S(1)} %bitcast.38, bf16[128,384]{1,0:T(8,128)(2,1)S(1)} %bitcast.41), custom_call_target="tpu_custom_call" | custom-call | flops 805306368 | bytes 3145728 | tf_op jit(solution)/shard_map/pallas_call | solution.py:41
  102.7 3.0 %collective-permute-start = (bf16[128,768]{1,0:T(8,128)(2,1)S(1)}, bf16[128,768]{1,0:T(8,128)(2,1)S(1)}, u32[]{:S(2)}, u32[]{:S(2)}) collective-permute-start(bf16[128,768]{1,0:T(8,128)(2,1)S(1)} %get-tuple-element.29), channel_id=1, source_target_pairs={{0,12},{4,0},{8,4},{12,8},{1,13},{5,1},{9,5},{13,9},{2,14},{6,2},{... | collective-permute-start | bytes 589832 | tf_op jit(solution)/shard_map/ppermute | solution.py:117
  105.7 3.2 %collective-permute-start.1 = (bf16[128,768]{1,0:T(8,128)(2,1)S(1)}, bf16[128,768]{1,0:T(8,128)(2,1)S(1)}, u32[]{:S(2)}, u32[]{:S(2)}) collective-permute-start(bf16[128,768]{1,0:T(8,128)(2,1)S(1)} %get-tuple-element.29), channel_id=1, source_target_pairs={{0,8},{4,12},{8,0},{12,4},{1,9},{5,13},{9,1},{13,5},{2,10},{6,14},... | collective-permute-start | bytes 589832 | tf_op jit(solution)/shard_map/ppermute | solution.py:117
  108.9 2.5 %collective-permute-start.2 = (bf16[128,768]{1,0:T(8,128)(2,1)S(1)}, bf16[128,768]{1,0:T(8,128)(2,1)S(1)}, u32[]{:S(2)}, u32[]{:S(2)}) collective-permute-start(bf16[128,768]{1,0:T(8,128)(2,1)S(1)} %get-tuple-element.29), channel_id=1, source_target_pairs={{0,4},{4,8},{8,12},{12,0},{1,5},{5,9},{9,13},{13,1},{2,6},{6,10},{... | collective-permute-start | bytes 589832 | tf_op jit(solution)/shard_map/ppermute | solution.py:117
  111.4 0.5 slice.43
  112.5 15.3 %conditional.2 = (bf16[16,128,128]{2,1,0:T(8,128)(2,1)S(1)}) conditional(s32[]{:T(128)} %bitcast.23, () %tuple.23, bf16[16,128,128]{2,1,0:T(8,128)(2,1)} %get-tuple-element.30), branch_computations={%region_0.1_spmd, %region_1.2_spmd} | conditional | bytes 1048584 | solution.py:188
  112.5 15.3 %all_to_all.27 = bf16[16,128,128]{2,1,0:T(8,128)(2,1)S(1)} all-to-all(bf16[16,128,128]{2,1,0:T(8,128)(2,1)} %param.1), channel_id=1, replica_groups=mesh['zh'=8,'zl'=4,'c'=2,'x'=4,'y'=4] {'x','y'}, dimensions={0} | all-to-all | bytes 1048576 | tf_op jit(solution)/shard_map/cond/branch_1_fun/all_to_all | solution.py:172
  127.8 0.0 collective-permute-done
  127.8 0.0 collective-permute-done.1
  127.8 0.8 copy-done.4
  128.6 0.0 collective-permute-done.2
  128.6 0.1 pad_maximum_fusion.refs_0_
  128.7 3.4 %collective-permute-start.3 = (bf16[512,768]{1,0:T(8,128)(2,1)S(1)}, bf16[512,768]{1,0:T(8,128)(2,1)S(1)}, u32[]{:S(2)}, u32[]{:S(2)}) collective-permute-start(bf16[512,768]{1,0:T(8,128)(2,1)S(1)} %pad_maximum_fusion.refs_0_), channel_id=1, source_target_pairs={{0,3},{1,0},{2,1},{3,2},{4,7},{5,4},{6,5},{7,6},{8,11},{9,8},{10,9... | collective-permute-start | bytes 2359304 | tf_op jit(solution)/shard_map/ppermute | solution.py:117
  132.1 3.4 %collective-permute-start.4 = (bf16[512,768]{1,0:T(8,128)(2,1)S(1)}, bf16[512,768]{1,0:T(8,128)(2,1)S(1)}, u32[]{:S(2)}, u32[]{:S(2)}) collective-permute-start(bf16[512,768]{1,0:T(8,128)(2,1)S(1)} %pad_maximum_fusion.refs_0_), channel_id=1, source_target_pairs={{0,2},{1,3},{2,0},{3,1},{4,6},{5,7},{6,4},{7,5},{8,10},{9,11},{10,... | collective-permute-start | bytes 2359304 | tf_op jit(solution)/shard_map/ppermute | solution.py:117
  135.5 4.0 %collective-permute-start.5 = (bf16[512,768]{1,0:T(8,128)(2,1)S(1)}, bf16[512,768]{1,0:T(8,128)(2,1)}, u32[]{:S(2)}, u32[]{:S(2)}) collective-permute-start(bf16[512,768]{1,0:T(8,128)(2,1)S(1)} %pad_maximum_fusion.refs_0_), channel_id=1, source_target_pairs={{0,1},{1,2},{2,3},{3,0},{4,5},{5,6},{6,7},{7,4},{8,9},{9,10},{10,1... | collective-permute-start | bytes 2359304 | tf_op jit(solution)/shard_map/ppermute | solution.py:117
  139.5 0.1 broadcast_add_fusion
  139.5 0.1 add.76.order_ref
  139.6 75.1 %conditional.3 = (bf16[128,128]{1,0:T(8,128)(2,1)S(1)}) conditional(s32[]{:T(128)} %bitcast.23, () %tuple.25, (bf16[16,128,128]{2,1,0:T(8,128)(2,1)}, bf16[8,256,128]{2,1,0:T(8,128)(2,1)}) %tuple.44), branch_computations={%region_2.3_spmd, %region_3.5_spmd} | conditional | flops 67354624 | bytes 7372838 | solution.py:191
  139.6 1.2 copy.16
  140.8 18.3 %all_to_all.28 = bf16[8,8,32,128]{3,2,1,0:T(8,128)(2,1)S(1)} all-to-all(bf16[8,8,32,128]{3,2,1,0:T(8,128)(2,1)S(1)} %copy.16), channel_id=1, replica_groups=mesh['zh'=8,'zl'=4,'c'=2,'x'=4,'y'=4] {'zl','c'}, dimensions={0} | all-to-all | bytes 1048576 | tf_op jit(solution)/shard_map/cond/branch_1_fun/all_to_all | solution.py:176
  159.2 0.0 copy-done.3
  159.2 0.4 convolution_convert_fusion
  159.6 55.1 %all_to_all.29 = bf16[8,128,128]{2,1,0:T(8,128)(2,1)S(1)} all-to-all(bf16[8,128,128]{2,1,0:T(8,128)(2,1)S(1)} %convolution_convert_fusion), channel_id=1, replica_groups=mesh['zh'=8,'zl'=4,'c'=2,'x'=4,'y'=4] {'zh'}, dimensions={0} | all-to-all | bytes 524288 | tf_op jit(solution)/shard_map/cond/branch_1_fun/all_to_all | solution.py:181
  214.7 0.0 copy-start.6
  214.7 0.0 collective-permute-done.3.refs_1_
  214.8 0.0 collective-permute-done.4.refs_2_
  214.8 0.0 collective-permute-done.5.refs_3_
  214.8 0.0 copy-done.1
  214.8 2.5 %shard_map.86 = (f32[128,384]{1,0:T(8,128)}, f32[128,384]{1,0:T(8,128)}) custom-call(s32[16]{0:T(128)S(1)} %add.76.order_ref, bf16[16,128,128]{2,1,0:T(8,128)(2,1)S(1)} %bitcast.40, bf16[512,768]{1,0:T(8,128)(2,1)S(1)} %pad_maximum_fusion.refs_0_, bf16[512,768]{1,0:T(8,128)(2,1)S(1)} %collective-permute-done.3.refs_1_, ...), custom_call_target="tpu_custom_call" | custom-call | flops 402653184 | bytes 524288 | tf_op jit(solution)/shard_map/pallas_call | solution.py:103
  217.3 0.0 copy-done.6
  (14 shorter events, 0.2 us)
Async XLA Ops:
  3.4 7.4 %copy-start.7 = (s32[128,8]{0,1:T(8,128)S(1)}, s32[128,8]{0,1:T(8,128)}, u32[]{:S(2)}) copy-start(s32[128,8]{0,1:T(8,128)} %param.10) | copy-start | bytes 12292
  3.4 7.4 %copy-start.5 = (bf16[128,128]{1,0:T(8,128)(2,1)S(1)}, bf16[128,128]{1,0:T(8,128)(2,1)}, u32[]{:S(2)}) copy-start(bf16[128,128]{1,0:T(8,128)(2,1)} %param.9) | copy-start | bytes 98308
  3.4 63.2 %all-to-all-start.3 = ((bf16[16,128,768]{2,1,0:T(8,128)(2,1)}), bf16[16,128,768]{2,1,0:T(8,128)(2,1)S(1)}, u32[]{:S(2)}, u32[]{:S(2)}) async-start(bf16[16,128,768]{2,1,0:T(8,128)(2,1)} %shard_map.84), calls=%async_computation.3 | async-start | bytes 6291456 | tf_op jit(solution)/shard_map/all_to_all | solution.py:133
  66.7 33.5 %copy-start.2 = (bf16[1,128,384]{2,1,0:T(8,128)(2,1)S(1)}, bf16[1,128,384]{2,1,0:T(8,128)(2,1)}, u32[]{:S(2)}) copy-start(bf16[1,128,384]{2,1,0:T(8,128)(2,1)} %param.13) | copy-start | bytes 294916
  99.3 0.8 copy-start
  102.7 25.1 %collective-permute-start = (bf16[128,768]{1,0:T(8,128)(2,1)S(1)}, bf16[128,768]{1,0:T(8,128)(2,1)S(1)}, u32[]{:S(2)}, u32[]{:S(2)}) collective-permute-start(bf16[128,768]{1,0:T(8,128)(2,1)S(1)} %get-tuple-element.29), channel_id=1, source_target_pairs={{0,12},{4,0},{8,4},{12,8},{1,13},{5,1},{9,5},{13,9},{2,14},{6,2},{... | collective-permute-start | bytes 589832 | tf_op jit(solution)/shard_map/ppermute | solution.py:117
  105.7 22.2 %collective-permute-start.1 = (bf16[128,768]{1,0:T(8,128)(2,1)S(1)}, bf16[128,768]{1,0:T(8,128)(2,1)S(1)}, u32[]{:S(2)}, u32[]{:S(2)}) collective-permute-start(bf16[128,768]{1,0:T(8,128)(2,1)S(1)} %get-tuple-element.29), channel_id=1, source_target_pairs={{0,8},{4,12},{8,0},{12,4},{1,9},{5,13},{9,1},{13,5},{2,10},{6,14},... | collective-permute-start | bytes 589832 | tf_op jit(solution)/shard_map/ppermute | solution.py:117
  108.9 19.7 %collective-permute-start.2 = (bf16[128,768]{1,0:T(8,128)(2,1)S(1)}, bf16[128,768]{1,0:T(8,128)(2,1)S(1)}, u32[]{:S(2)}, u32[]{:S(2)}) collective-permute-start(bf16[128,768]{1,0:T(8,128)(2,1)S(1)} %get-tuple-element.29), channel_id=1, source_target_pairs={{0,4},{4,8},{8,12},{12,0},{1,5},{5,9},{9,13},{13,1},{2,6},{6,10},{... | collective-permute-start | bytes 589832 | tf_op jit(solution)/shard_map/ppermute | solution.py:117
  127.8 0.8 copy-start.4
  128.7 86.1 %collective-permute-start.3 = (bf16[512,768]{1,0:T(8,128)(2,1)S(1)}, bf16[512,768]{1,0:T(8,128)(2,1)S(1)}, u32[]{:S(2)}, u32[]{:S(2)}) collective-permute-start(bf16[512,768]{1,0:T(8,128)(2,1)S(1)} %pad_maximum_fusion.refs_0_), channel_id=1, source_target_pairs={{0,3},{1,0},{2,1},{3,2},{4,7},{5,4},{6,5},{7,6},{8,11},{9,8},{10,9... | collective-permute-start | bytes 2359304 | tf_op jit(solution)/shard_map/ppermute | solution.py:117
  132.1 82.7 %collective-permute-start.4 = (bf16[512,768]{1,0:T(8,128)(2,1)S(1)}, bf16[512,768]{1,0:T(8,128)(2,1)S(1)}, u32[]{:S(2)}, u32[]{:S(2)}) collective-permute-start(bf16[512,768]{1,0:T(8,128)(2,1)S(1)} %pad_maximum_fusion.refs_0_), channel_id=1, source_target_pairs={{0,2},{1,3},{2,0},{3,1},{4,6},{5,7},{6,4},{7,5},{8,10},{9,11},{10,... | collective-permute-start | bytes 2359304 | tf_op jit(solution)/shard_map/ppermute | solution.py:117
  135.5 79.3 %collective-permute-start.5 = (bf16[512,768]{1,0:T(8,128)(2,1)S(1)}, bf16[512,768]{1,0:T(8,128)(2,1)}, u32[]{:S(2)}, u32[]{:S(2)}) collective-permute-start(bf16[512,768]{1,0:T(8,128)(2,1)S(1)} %pad_maximum_fusion.refs_0_), channel_id=1, source_target_pairs={{0,1},{1,2},{2,3},{3,0},{4,5},{5,6},{6,7},{7,4},{8,9},{9,10},{10,1... | collective-permute-start | bytes 2359304 | tf_op jit(solution)/shard_map/ppermute | solution.py:117
  139.6 75.1 %copy-start.1 = (bf16[8,8,32,128]{3,2,1,0:T(8,128)(2,1)S(1)}, bf16[8,8,32,128]{3,2,1,0:T(8,128)(2,1)}, u32[]{:S(2)}) copy-start(bf16[8,8,32,128]{3,2,1,0:T(8,128)(2,1)} %copy-done) | copy-start | bytes 1572868
  139.6 19.6 %copy-start.3 = (bf16[8,256,128]{2,1,0:T(8,128)(2,1)S(1)}, bf16[8,256,128]{2,1,0:T(8,128)(2,1)}, u32[]{:S(2)}) copy-start(bf16[8,256,128]{2,1,0:T(8,128)(2,1)} %get-tuple-element.40) | copy-start | bytes 1572868 | tf_op jit(solution)/shard_map/cond
  214.7 2.6 %copy-start.6 = (bf16[128,128]{1,0:T(8,128)(2,1)}, bf16[128,128]{1,0:T(8,128)(2,1)S(1)}, u32[]{:S(2)}) copy-start(bf16[128,128]{1,0:T(8,128)(2,1)S(1)} %get-tuple-element.54) | copy-start | bytes 98308

commit v7 on v6

--- a/solution.py
+++ b/solution.py
@@ -171,12 +171,18 @@
     def swap_shares(slot_grad):
         return lax.all_to_all(slot_grad, dp, split_axis=0, concat_axis=0, tiled=True)
 
-    def go_back(back, placer):
+    def go_near(back):
         back = back.reshape(n_zh, n_near, capacity, width_part).transpose(1, 0, 2, 3)
         returned = lax.all_to_all(back, near, split_axis=0, concat_axis=0, tiled=True)
-        returned = returned.transpose(1, 0, 2, 3).reshape(n_zh, n_near * capacity, width_part)
+        return returned.reshape(slot_grad.shape)
+
+    def go_home(returned, placer):
+        returned = returned.reshape(n_near, n_zh, capacity, width_part).transpose(1, 0, 2, 3)
         token_sum = lax.dot_general(
-            placer, returned, (((1,), (1,)), ((0,), (0,))), preferred_element_type=jnp.float32
+            placer,
+            returned.reshape(n_zh, n_near * capacity, width_part),
+            (((1,), (1,)), ((0,), (0,))),
+            preferred_element_type=jnp.float32,
         )
         sums = lax.all_to_all(
             token_sum.astype(jnp.bfloat16), "zh", split_axis=0, concat_axis=0, tiled=True
@@ -184,13 +190,19 @@
         return jnp.sum(sums.astype(jnp.float32), axis=0).astype(jnp.bfloat16)
 
     taken = expert_ids[0, 0] >= 0
-    along_x = jnp.concatenate(blocks_along(both_delta, "x"), axis=0)
-    back = lax.cond(taken, swap_shares, jnp.zeros_like, slot_grad)
-    along_x, back = lax.optimization_barrier((along_x, back))
+    along_x = both_delta
+    step = 1
+    for window in (swap_shares, go_near):
+        if step < n_x:
+            pair = [(i, i ^ step) for i in range(n_x)]
+            along_x = jnp.concatenate([along_x, lax.ppermute(along_x, "x", pair)], axis=0)
+            step *= 2
+        slot_grad = lax.cond(taken, window, jnp.zeros_like, slot_grad)
+        along_x, slot_grad = lax.optimization_barrier((along_x, slot_grad))
     deltas = blocks_along(along_x, "y")
-    token_grad = lax.cond(taken, go_back, lambda *_: jnp.zeros_like(tokens), back, placer)
-
-    place_x = (lax.axis_index("x") + jnp.arange(n_x, dtype=jnp.int32)) % n_x
+    token_grad = lax.cond(taken, go_home, lambda *_: jnp.zeros_like(tokens), slot_grad, placer)
+
+    place_x = lax.axis_index("x") ^ jnp.arange(n_x, dtype=jnp.int32)
     place_y = (lax.axis_index("y") + jnp.arange(n_y, dtype=jnp.int32)) % n_y
     order = (place_x[None, :] * n_y + place_y[:, None]).reshape(n_dp)
     gate_grad, up_grad = weight_grads(order, by_share, deltas)

time: 218 us -> 215 us (0.986)
  the two profiles are of different devices: /device:TPU:48 before, /device:TPU:8 now
where the time goes in v7:
time: 215 us; the launch traced here: 214 us
  blocking collectives  167 us (78%)
  starting transfers between devices  31.3 us (15%)
  Pallas kernels  7.81 us (4%)
  local copies, waits for them, and re-layouts  4.38 us (2%)
    all_to_all x1, blocking collectives, go_home(): lax.all_to_all(token_sum.astype(jnp.bfloat16), 'zh', split_axis=0, concat...  54 us
    all_gather x1, blocking collectives, on_device(): known = lax.all_gather(sent, 'zh', axis=0, tiled=False)  44.6 us
    all_to_all x1, blocking collectives, on_device(): lax.all_to_all(outgoing, near, split_axis=0, concat_axis=0, tiled=True)  18.9 us
    all_to_all x1, blocking collectives, go_near(): lax.all_to_all(back, near, split_axis=0, concat_axis=0, tiled=True)  18.4 us
    all_to_all x1, starting transfers between devices, on_device(): lax.all_to_all(weights, dp, split_axis=0, concat_axis=0, tiled=True)  16.6 us
    all_to_all x1, blocking collectives, on_device(): lax.all_to_all(by_share, dp, split_axis=0, concat_axis=0, tiled=True)  16.6 us
    all_to_all x1, blocking collectives, swap_shares(): lax.all_to_all(slot_grad, dp, split_axis=0, concat_axis=0, tiled=True)  14.6 us
    ppermute x3, starting transfers between devices, blocks_along(): return [block] + [lax.ppermute(block, axis, step) for step in steps]  9.99 us
  transfers between devices with their start and end apart: 6, of which 0 were waited for; matrix products, arithmetic and copies ran while one was open for 2% of the time, Pallas kernels for 0%

profile of v7, /device:TPU:8, one launch (start us, length us, event | category | flops | bytes accessed | tf_op | source)
XLA Modules:
  0.0 214.2 jit_solution(14941635562014935563)
XLA Ops:
  0.6 2.8 %shard_map.84 = bf16[16,128,768]{2,1,0:T(8,128)(2,1)} custom-call(bf16[1,128,384]{2,1,0:T(8,128)(2,1)} %gate_ref.1, bf16[1,128,384]{2,1,0:T(8,128)(2,1)} %up_ref.1), custom_call_target="tpu_custom_call" | custom-call | tf_op jit(solution)/shard_map/pallas_call | solution.py:71
  3.4 0.0 copy-start.7
  3.4 0.0 copy-start.5
  3.4 16.6 %all-to-all-start.3 = ((bf16[16,128,768]{2,1,0:T(8,128)(2,1)}), bf16[16,128,768]{2,1,0:T(8,128)(2,1)S(1)}, u32[]{:S(2)}, u32[]{:S(2)}) async-start(bf16[16,128,768]{2,1,0:T(8,128)(2,1)} %shard_map.84), calls=%async_computation.3 | async-start | bytes 6291456 | tf_op jit(solution)/shard_map/all_to_all | solution.py:133
  20.1 0.1 eq.173
  20.1 0.0 copy-done.7
  20.2 0.0 copy-done.5
  20.2 44.6 %all-gather = bf16[1088,128]{1,0:T(8,128)(2,1)S(1)} all-gather(bf16[136,128]{1,0:T(8,128)(2,1)S(1)} %pad_maximum_fusion.2), channel_id=2, replica_groups=mesh['zh'=8,'zl'=4,'c'=2,'x'=4,'y'=4] {'zh'}, dimensions={0}, use_global_device_ids=true | all-gather | bytes 313344 | tf_op jit(solution)/shard_map/all_gather | solution.py:138
  64.8 0.2 fusion
  65.0 1.1 fusion.29
  66.1 0.3 convolution_convert_fusion.1
  66.4 0.8 copy.25
  67.2 0.0 all-to-all-done.3
  67.2 0.0 copy-start.2
  67.2 18.9 %all_to_all.30 = bf16[8,8,32,128]{3,2,1,0:T(8,128)(2,1)S(1)} all-to-all(bf16[8,8,32,128]{3,2,1,0:T(8,128)(2,1)} %bitcast.46), channel_id=1, replica_groups=mesh['zh'=8,'zl'=4,'c'=2,'x'=4,'y'=4] {'zl','c'}, dimensions={0} | all-to-all | bytes 1048576 | tf_op jit(solution)/shard_map/all_to_all | solution.py:165
  86.2 16.6 %all_to_all.31.rows_ref = bf16[16,128,128]{2,1,0:T(8,128)(2,1)S(1)} all-to-all(bf16[16,128,128]{2,1,0:T(8,128)(2,1)S(1)} %bitcast.43), channel_id=1, replica_groups=mesh['zh'=8,'zl'=4,'c'=2,'x'=4,'y'=4] {'x','y'}, dimensions={0} | all-to-all | bytes 1048576 | tf_op jit(solution)/shard_map/all_to_all | solution.py:168
  102.7 0.8 copy-done
  103.5 0.0 copy-done.2
  103.5 2.5 %shard_map.85 = (bf16[128,384]{1,0:T(8,128)(2,1)}, bf16[128,768]{1,0:T(8,128)(2,1)S(1)}, bf16[16,128,128]{2,1,0:T(8,128)(2,1)}) custom-call(bf16[16,128,128]{2,1,0:T(8,128)(2,1)S(1)} %all_to_all.31.rows_ref, bf16[2048,768]{1,0:T(8,128)(2,1)S(1)} %bitcast.42, bf16[128,384]{1,0:T(8,128)(2,1)S(1)} %bitcast.45), custom_call_target="tpu_custom_call" | custom-call | flops 805306368 | bytes 3145728 | tf_op jit(solution)/shard_map/pallas_call | solution.py:41
  106.1 1.9 collective-permute-start
  108.0 0.5 slice.43
  109.2 14.6 %conditional.3 = (bf16[16,128,128]{2,1,0:T(8,128)(2,1)S(1)}) conditional(s32[]{:T(128)} %bitcast.25, () %tuple.30, bf16[16,128,128]{2,1,0:T(8,128)(2,1)} %get-tuple-element.36), branch_computations={%region_0.1_spmd, %region_1.2_spmd} | conditional | bytes 1048584 | solution.py:200
  109.2 14.6 %all_to_all.27 = bf16[16,128,128]{2,1,0:T(8,128)(2,1)S(1)} all-to-all(bf16[16,128,128]{2,1,0:T(8,128)(2,1)} %param.1), channel_id=1, replica_groups=mesh['zh'=8,'zl'=4,'c'=2,'x'=4,'y'=4] {'x','y'}, dimensions={0} | all-to-all | bytes 1048576 | tf_op jit(solution)/shard_map/cond/branch_1_fun/all_to_all | solution.py:172
  123.7 0.0 collective-permute-done
  123.8 2.8 %collective-permute-start.1 = (bf16[256,768]{1,0:T(8,128)(2,1)S(1)}, bf16[256,768]{1,0:T(8,128)(2,1)S(1)}, u32[]{:S(2)}, u32[]{:S(2)}) collective-permute-start(bf16[256,768]{1,0:T(8,128)(2,1)S(1)} %pad_maximum_fusion.1), channel_id=1, source_target_pairs={{0,8},{4,12},{8,0},{12,4},{1,9},{5,13},{9,1},{13,5},{2,10},{6,14},... | collective-permute-start | bytes 1179656 | tf_op jit(solution)/shard_map/ppermute | solution.py:198
  126.6 0.0 copy-start.3
  126.6 18.5 %conditional.4 = (bf16[16,128,128]{2,1,0:T(8,128)(2,1)S(1)}) conditional(s32[]{:T(128)} %bitcast.25, () %tuple.32, bf16[16,128,128]{2,1,0:T(8,128)(2,1)S(1)} %get-tuple-element.59), branch_computations={%region_2.3_spmd, %region_3.4_spmd} | conditional | bytes 2097160 | solution.py:200
  126.6 18.4 %all_to_all.28 = bf16[8,8,32,128]{3,2,1,0:T(8,128)(2,1)S(1)} all-to-all(bf16[8,8,32,128]{3,2,1,0:T(8,128)(2,1)S(1)} %bitcast.52), channel_id=1, replica_groups=mesh['zh'=8,'zl'=4,'c'=2,'x'=4,'y'=4] {'zl','c'}, dimensions={0} | all-to-all | bytes 1048576 | tf_op jit(solution)/shard_map/cond/branch_1_fun/all_to_all | solution.py:176
  145.0 0.8 copy-done.4
  145.8 0.0 collective-permute-done.1
  145.8 0.1 pad_maximum_fusion.refs_0_
  145.9 3.6 %collective-permute-start.2 = (bf16[512,768]{1,0:T(8,128)(2,1)S(1)}, bf16[512,768]{1,0:T(8,128)(2,1)S(1)}, u32[]{:S(2)}, u32[]{:S(2)}) collective-permute-start(bf16[512,768]{1,0:T(8,128)(2,1)S(1)} %pad_maximum_fusion.refs_0_), channel_id=1, source_target_pairs={{0,3},{1,0},{2,1},{3,2},{4,7},{5,4},{6,5},{7,6},{8,11},{9,8},{10,9... | collective-permute-start | bytes 2359304 | tf_op jit(solution)/shard_map/ppermute | solution.py:117
  149.5 2.9 %collective-permute-start.3 = (bf16[512,768]{1,0:T(8,128)(2,1)S(1)}, bf16[512,768]{1,0:T(8,128)(2,1)S(1)}, u32[]{:S(2)}, u32[]{:S(2)}) collective-permute-start(bf16[512,768]{1,0:T(8,128)(2,1)S(1)} %pad_maximum_fusion.refs_0_), channel_id=1, source_target_pairs={{0,2},{1,3},{2,0},{3,1},{4,6},{5,7},{6,4},{7,5},{8,10},{9,11},{10,... | collective-permute-start | bytes 2359304 | tf_op jit(solution)/shard_map/ppermute | solution.py:117
  152.4 3.5 %collective-permute-start.4 = (bf16[512,768]{1,0:T(8,128)(2,1)S(1)}, bf16[512,768]{1,0:T(8,128)(2,1)}, u32[]{:S(2)}, u32[]{:S(2)}) collective-permute-start(bf16[512,768]{1,0:T(8,128)(2,1)S(1)} %pad_maximum_fusion.refs_0_), channel_id=1, source_target_pairs={{0,1},{1,2},{2,3},{3,0},{4,5},{5,6},{6,7},{7,4},{8,9},{9,10},{10,1... | collective-permute-start | bytes 2359304 | tf_op jit(solution)/shard_map/ppermute | solution.py:117
  155.9 0.1 broadcast_add_fusion
  156.0 0.1 add.55.order_ref
  156.1 0.0 copy-done.3
  156.1 55.5 %conditional.5 = (bf16[128,128]{1,0:T(8,128)(2,1)S(1)}) conditional(s32[]{:T(128)} %bitcast.25, () %tuple.34, (bf16[16,128,128]{2,1,0:T(8,128)(2,1)}, bf16[8,256,128]{2,1,0:T(8,128)(2,1)S(1)}) %tuple.55), branch_computations={%region_4.5_spmd, %region_5.7_spmd} | conditional | flops 67354624 | bytes 3178506 | solution.py:203
  156.1 1.1 copy.17
  157.2 0.3 convolution_convert_fusion
  157.6 54.0 %all_to_all.29 = bf16[8,128,128]{2,1,0:T(8,128)(2,1)S(1)} all-to-all(bf16[8,128,128]{2,1,0:T(8,128)(2,1)S(1)} %convolution_convert_fusion), channel_id=1, replica_groups=mesh['zh'=8,'zl'=4,'c'=2,'x'=4,'y'=4] {'zh'}, dimensions={0} | all-to-all | bytes 524288 | tf_op jit(solution)/shard_map/cond/branch_1_fun/all_to_all | solution.py:187
  211.6 0.0 copy-start.6
  211.6 0.0 collective-permute-done.2.refs_1_
  211.7 0.0 collective-permute-done.3.refs_2_
  211.7 0.0 collective-permute-done.4.refs_3_
  211.7 0.0 copy-done.1
  211.7 2.5 %shard_map.86 = (f32[128,384]{1,0:T(8,128)}, f32[128,384]{1,0:T(8,128)}) custom-call(s32[16]{0:T(128)S(1)} %add.55.order_ref, bf16[16,128,128]{2,1,0:T(8,128)(2,1)S(1)} %bitcast.44, bf16[512,768]{1,0:T(8,128)(2,1)S(1)} %pad_maximum_fusion.refs_0_, bf16[512,768]{1,0:T(8,128)(2,1)S(1)} %collective-permute-done.2.refs_1_, ...), custom_call_target="tpu_custom_call" | custom-call | flops 402653184 | bytes 524288 | tf_op jit(solution)/shard_map/pallas_call | solution.py:103
  214.2 0.0 copy-done.6
  (14 shorter events, 0.2 us)
Async XLA Ops:
  3.4 16.8 %copy-start.7 = (s32[128,8]{0,1:T(8,128)S(1)}, s32[128,8]{0,1:T(8,128)}, u32[]{:S(2)}) copy-start(s32[128,8]{0,1:T(8,128)} %param.12) | copy-start | bytes 12292
  3.4 16.8 %copy-start.5 = (bf16[128,128]{1,0:T(8,128)(2,1)S(1)}, bf16[128,128]{1,0:T(8,128)(2,1)}, u32[]{:S(2)}) copy-start(bf16[128,128]{1,0:T(8,128)(2,1)} %param.11) | copy-start | bytes 98308
  3.4 63.8 %all-to-all-start.3 = ((bf16[16,128,768]{2,1,0:T(8,128)(2,1)}), bf16[16,128,768]{2,1,0:T(8,128)(2,1)S(1)}, u32[]{:S(2)}, u32[]{:S(2)}) async-start(bf16[16,128,768]{2,1,0:T(8,128)(2,1)} %shard_map.84), calls=%async_computation.3 | async-start | bytes 6291456 | tf_op jit(solution)/shard_map/all_to_all | solution.py:133
  67.2 36.3 %copy-start.2 = (bf16[1,128,384]{2,1,0:T(8,128)(2,1)S(1)}, bf16[1,128,384]{2,1,0:T(8,128)(2,1)}, u32[]{:S(2)}) copy-start(bf16[1,128,384]{2,1,0:T(8,128)(2,1)} %param.15) | copy-start | bytes 294916
  102.7 0.8 copy-start
  106.1 17.7 %collective-permute-start = (bf16[128,768]{1,0:T(8,128)(2,1)S(1)}, bf16[128,768]{1,0:T(8,128)(2,1)S(1)}, u32[]{:S(2)}, u32[]{:S(2)}) collective-permute-start(bf16[128,768]{1,0:T(8,128)(2,1)S(1)} %get-tuple-element.35), channel_id=1, source_target_pairs={{0,4},{4,0},{8,12},{12,8},{1,5},{5,1},{9,13},{13,9},{2,6},{6,2},{1... | collective-permute-start | bytes 589832 | tf_op jit(solution)/shard_map/ppermute | solution.py:198
  123.8 22.1 %collective-permute-start.1 = (bf16[256,768]{1,0:T(8,128)(2,1)S(1)}, bf16[256,768]{1,0:T(8,128)(2,1)S(1)}, u32[]{:S(2)}, u32[]{:S(2)}) collective-permute-start(bf16[256,768]{1,0:T(8,128)(2,1)S(1)} %pad_maximum_fusion.1), channel_id=1, source_target_pairs={{0,8},{4,12},{8,0},{12,4},{1,9},{5,13},{9,1},{13,5},{2,10},{6,14},... | collective-permute-start | bytes 1179656 | tf_op jit(solution)/shard_map/ppermute | solution.py:198
  126.6 29.5 %copy-start.3 = (bf16[8,256,128]{2,1,0:T(8,128)(2,1)S(1)}, bf16[8,256,128]{2,1,0:T(8,128)(2,1)}, u32[]{:S(2)}) copy-start(bf16[8,256,128]{2,1,0:T(8,128)(2,1)} %get-tuple-element.47) | copy-start | bytes 1572868
  145.0 0.8 copy-start.4
  145.9 65.7 %collective-permute-start.2 = (bf16[512,768]{1,0:T(8,128)(2,1)S(1)}, bf16[512,768]{1,0:T(8,128)(2,1)S(1)}, u32[]{:S(2)}, u32[]{:S(2)}) collective-permute-start(bf16[512,768]{1,0:T(8,128)(2,1)S(1)} %pad_maximum_fusion.refs_0_), channel_id=1, source_target_pairs={{0,3},{1,0},{2,1},{3,2},{4,7},{5,4},{6,5},{7,6},{8,11},{9,8},{10,9... | collective-permute-start | bytes 2359304 | tf_op jit(solution)/shard_map/ppermute | solution.py:117
  149.5 62.2 %collective-permute-start.3 = (bf16[512,768]{1,0:T(8,128)(2,1)S(1)}, bf16[512,768]{1,0:T(8,128)(2,1)S(1)}, u32[]{:S(2)}, u32[]{:S(2)}) collective-permute-start(bf16[512,768]{1,0:T(8,128)(2,1)S(1)} %pad_maximum_fusion.refs_0_), channel_id=1, source_target_pairs={{0,2},{1,3},{2,0},{3,1},{4,6},{5,7},{6,4},{7,5},{8,10},{9,11},{10,... | collective-permute-start | bytes 2359304 | tf_op jit(solution)/shard_map/ppermute | solution.py:117
  152.4 59.3 %collective-permute-start.4 = (bf16[512,768]{1,0:T(8,128)(2,1)S(1)}, bf16[512,768]{1,0:T(8,128)(2,1)}, u32[]{:S(2)}, u32[]{:S(2)}) collective-permute-start(bf16[512,768]{1,0:T(8,128)(2,1)S(1)} %pad_maximum_fusion.refs_0_), channel_id=1, source_target_pairs={{0,1},{1,2},{2,3},{3,0},{4,5},{5,6},{6,7},{7,4},{8,9},{9,10},{10,1... | collective-permute-start | bytes 2359304 | tf_op jit(solution)/shard_map/ppermute | solution.py:117
  156.1 55.6 %copy-start.1 = (bf16[8,8,32,128]{3,2,1,0:T(8,128)(2,1)S(1)}, bf16[8,8,32,128]{3,2,1,0:T(8,128)(2,1)}, u32[]{:S(2)}) copy-start(bf16[8,8,32,128]{3,2,1,0:T(8,128)(2,1)} %copy-done) | copy-start | bytes 1572868
  211.6 2.6 %copy-start.6 = (bf16[128,128]{1,0:T(8,128)(2,1)}, bf16[128,128]{1,0:T(8,128)(2,1)S(1)}, u32[]{:S(2)}) copy-start(bf16[128,128]{1,0:T(8,128)(2,1)S(1)} %get-tuple-element.61) | copy-start | bytes 98308

commit v8 on v6

--- a/solution.py
+++ b/solution.py
@@ -7,7 +7,7 @@
 
 CORES = 2
 ZL = 4
-DP_X = 4
+X_HIGH, X_LOW = 2, 2
 
 
 def expert_kernel(rows_ref, weights_ref, grad_ref, hidden_ref, delta_ref, slot_grad_ref):
@@ -79,49 +79,10 @@
     )(gate_w, up_w)
 
 
-def weight_grad_kernel(order_ref, rows_ref, *refs):
-    delta_refs, (gate_grad_ref, up_grad_ref) = refs[:-2], refs[-2:]
-    share_rows = rows_ref.shape[1]
-    hidden_units = gate_grad_ref.shape[1]
-    n_x = rows_ref.shape[0] // len(delta_refs)
-    total = jnp.zeros((rows_ref.shape[2], 2 * hidden_units), jnp.float32)
-    for block, delta_ref in enumerate(delta_refs):
-        rows = jnp.concatenate(
-            [rows_ref[order_ref[block * n_x + part]] for part in range(n_x)], axis=0
-        )
-        total = total + lax.dot_general(
-            rows, delta_ref[...], (((0,), (0,)), ((), ())), preferred_element_type=jnp.float32
-        )
-    gate_grad_ref[...] = total[:, :hidden_units]
-    up_grad_ref[...] = total[:, hidden_units:]
-
-
-def weight_grads(order, rows, deltas):
-    both_units = deltas[0].shape[1]
-    out = jax.ShapeDtypeStruct((rows.shape[2], both_units // 2), jnp.float32)
-    in_vmem = pl.BlockSpec(memory_space=pltpu.VMEM)
-    return pl.pallas_call(
-        weight_grad_kernel,
-        in_specs=[pl.BlockSpec(memory_space=pltpu.SMEM)] + [in_vmem] * (1 + len(deltas)),
-        out_shape=(out, out),
-        compiler_params=pltpu.CompilerParams(vmem_limit_bytes=32 * 1024 * 1024),
-        cost_estimate=pl.CostEstimate(
-            flops=2 * rows.size * both_units, bytes_accessed=2 * rows.size, transcendentals=0
-        ),
-    )(order, rows, *deltas)
-
-
-def blocks_along(block, axis):
-    n = lax.axis_size(axis)
-    steps = [[(i, (i - k) % n) for i in range(n)] for k in range(1, n)]
-    return [block] + [lax.ppermute(block, axis, step) for step in steps]
-
-
 def on_device(tokens, expert_ids, gate_weight, up_weight, hidden_grad):
     n_zh = lax.axis_size("zh")
-    dp = ("x", "y")
-    n_x, n_y = lax.axis_size("x"), lax.axis_size("y")
-    n_dp = n_x * n_y
+    dp = ("xh", "xl", "y")
+    n_dp = lax.axis_size(dp)
     near = ("zl", "c")
     tok_rows, width_part = tokens.shape
     top_k = expert_ids.shape[1]
@@ -184,26 +145,43 @@
         return jnp.sum(sums.astype(jnp.float32), axis=0).astype(jnp.bfloat16)
 
     taken = expert_ids[0, 0] >= 0
-    along_x = jnp.concatenate(blocks_along(both_delta, "x"), axis=0)
+    other_delta = lax.ppermute(both_delta, "xl", [(0, 1), (1, 0)])
     back = lax.cond(taken, swap_shares, jnp.zeros_like, slot_grad)
-    along_x, back = lax.optimization_barrier((along_x, back))
-    deltas = blocks_along(along_x, "y")
+    other_delta, back = lax.optimization_barrier((other_delta, back))
+    low = lax.axis_index("xl") == 0
+    pair_delta = jnp.concatenate(
+        [jnp.where(low, both_delta, other_delta), jnp.where(low, other_delta, both_delta)], axis=0
+    )
+    pair_delta, back = lax.optimization_barrier((pair_delta, back))
+    all_delta = lax.all_gather(pair_delta, ("xh", "y"), axis=0, tiled=True)
     token_grad = lax.cond(taken, go_back, lambda *_: jnp.zeros_like(tokens), back, placer)
 
-    place_x = (lax.axis_index("x") + jnp.arange(n_x, dtype=jnp.int32)) % n_x
-    place_y = (lax.axis_index("y") + jnp.arange(n_y, dtype=jnp.int32)) % n_y
-    order = (place_x[None, :] * n_y + place_y[:, None]).reshape(n_dp)
-    gate_grad, up_grad = weight_grads(order, by_share, deltas)
-    return hidden[None], gate_grad[None], up_grad[None], token_grad
+    ordered = by_share.reshape(
+        lax.axis_size("xh"), X_LOW, lax.axis_size("y"), share_rows, width_part
+    ).transpose(0, 2, 1, 3, 4)
+    both_grad = lax.dot_general(
+        ordered.reshape(n_dp * share_rows, width_part),
+        all_delta,
+        (((0,), (0,)), ((), ())),
+        preferred_element_type=jnp.float32,
+    )
+    return (
+        hidden[None],
+        both_grad[None, :, :hidden_units],
+        both_grad[None, :, hidden_units:],
+        token_grad,
+    )
 
 
 def solution(mesh):
     n_expert, n_dp = mesh.devices.shape
     split = Mesh(
-        mesh.devices.reshape(n_expert // (ZL * CORES), ZL, CORES, DP_X, n_dp // DP_X),
-        ("zh", "zl", "c", "x", "y"),
-    )
-    expert, dp = ("zh", "zl", "c"), ("x", "y")
+        mesh.devices.reshape(
+            n_expert // (ZL * CORES), ZL, CORES, X_HIGH, X_LOW, n_dp // (X_HIGH * X_LOW)
+        ),
+        ("zh", "zl", "c", "xh", "xl", "y"),
+    )
+    expert, dp = ("zh", "zl", "c"), ("xh", "xl", "y")
     placed = (
         P(expert, dp),
         P(expert, None),

time: 218 us -> 232 us (1.064)
  the two profiles are of different devices: /device:TPU:48 before, /device:TPU:1 now
where the time goes in v8:
time: 232 us; the launch traced here: 231 us
  blocking collectives  167 us (72%)
  waiting for transfers between devices  26.7 us (12%)
  between operations  14.9 us (6%)
  starting transfers between devices  10.1 us (4%)
  Pallas kernels  5.29 us (2%)
  matrix products  3.36 us (1%)
  local copies, waits for them, and re-layouts  2.43 us (1%)
    all_gather x1, blocking collectives, on_device(): known = lax.all_gather(sent, 'zh', axis=0, tiled=False)  49.1 us
    all_to_all x1, blocking collectives, go_back(): lax.all_to_all(token_sum.astype(jnp.bfloat16), 'zh', split_axis=0, concat...  43.8 us
    all_gather x1, waiting for transfers between devices, on_device(): all_delta = lax.all_gather(pair_delta, ('xh', 'y'), axis=0, tiled=True)  26.7 us
    all_to_all x1, blocking collectives, on_device(): lax.all_to_all(outgoing, near, split_axis=0, concat_axis=0, tiled=True)  23 us
    all_to_all x1, blocking collectives, go_back(): lax.all_to_all(back, near, split_axis=0, concat_axis=0, tiled=True)  20.9 us
    all_to_all x1, blocking collectives, on_device(): lax.all_to_all(by_share, dp, split_axis=0, concat_axis=0, tiled=True)  15.9 us
    all_to_all x1, blocking collectives, swap_shares(): lax.all_to_all(slot_grad, dp, split_axis=0, concat_axis=0, tiled=True)  14 us
    all_to_all x1, starting transfers between devices, on_device(): lax.all_to_all(weights, dp, split_axis=0, concat_axis=0, tiled=True)  7.6 us
  transfers between devices with their start and end apart: 3, of which 1 were waited for; matrix products, arithmetic and copies ran while one was open for 2% of the time, Pallas kernels for 0%

profile of v8, /device:TPU:1, one launch (start us, length us, event | category | flops | bytes accessed | tf_op | source)
XLA Modules:
  0.0 231.5 jit_solution(4479364090670047829)
XLA Ops:
  7.2 2.7 %shard_map.84 = bf16[16,128,768]{2,1,0:T(8,128)(2,1)} custom-call(bf16[1,128,384]{2,1,0:T(8,128)(2,1)} %gate_ref.1, bf16[1,128,384]{2,1,0:T(8,128)(2,1)} %up_ref.1), custom_call_target="tpu_custom_call" | custom-call | tf_op jit(solution)/shard_map/pallas_call | solution.py:71
  9.9 0.0 copy-start.6
  9.9 0.0 copy-start.4
  9.9 7.6 %all-to-all-start.3 = ((bf16[16,128,768]{2,1,0:T(8,128)(2,1)}), bf16[16,128,768]{2,1,0:T(8,128)(2,1)S(1)}, u32[]{:S(2)}, u32[]{:S(2)}) async-start(bf16[16,128,768]{2,1,0:T(8,128)(2,1)} %shard_map.84), calls=%async_computation.3 | async-start | bytes 6291456 | tf_op jit(solution)/shard_map/all_to_all | solution.py:94
  17.5 0.0 all-gather.3.cloned.1.call-start
  17.6 0.1 eq.174
  17.7 0.0 copy-done.6
  17.7 0.0 copy-done.4
  17.7 49.1 %all-gather = bf16[1088,128]{1,0:T(8,128)(2,1)S(1)} all-gather(bf16[136,128]{1,0:T(8,128)(2,1)S(1)} %pad_maximum_fusion.1), channel_id=2, replica_groups=mesh['zh'=8,'zl'=4,'c'=2,'xh'=2,'xl'=2,'y'=4] {'zh'}, dimensions={0}, use_global_device_ids=true | all-gather | bytes 313344 | tf_op jit(solution)/shard_map/all_gather | solution.py:99
  66.9 0.0 copy-start
  66.9 0.2 fusion
  67.1 1.1 fusion.28
  68.2 0.3 convolution_convert_fusion.1
  68.5 0.8 copy.27
  69.4 0.0 all-to-all-done.3
  69.4 23.0 %all_to_all.30 = bf16[8,8,32,128]{3,2,1,0:T(8,128)(2,1)S(1)} all-to-all(bf16[8,8,32,128]{3,2,1,0:T(8,128)(2,1)} %bitcast.52), channel_id=1, replica_groups=mesh['zh'=8,'zl'=4,'c'=2,'xh'=2,'xl'=2,'y'=4] {'zl','c'}, dimensions={0} | all-to-all | bytes 1048576 | tf_op jit(solution)/shard_map/all_to_all | solution.py:126
  92.4 0.0 copy-start.1
  92.4 15.9 %all_to_all.31.rows_ref = bf16[16,128,128]{2,1,0:T(8,128)(2,1)S(1)} all-to-all(bf16[16,128,128]{2,1,0:T(8,128)(2,1)S(1)} %bitcast.50), channel_id=1, replica_groups=mesh['zh'=8,'zl'=4,'c'=2,'xh'=2,'xl'=2,'y'=4] {'xh','xl','y'}, dimensions={0} | all-to-all | bytes 1048576 | tf_op jit(solution)/shard_map/all_to_all | solution.py:129
  108.3 0.0 copy-done.1
  108.3 0.0 copy-done
  108.3 2.5 %shard_map.85 = (bf16[128,384]{1,0:T(8,128)(2,1)}, bf16[128,768]{1,0:T(8,128)(2,1)S(1)}, bf16[16,128,128]{2,1,0:T(8,128)(2,1)}) custom-call(bf16[16,128,128]{2,1,0:T(8,128)(2,1)S(1)} %all_to_all.31.rows_ref, bf16[2048,768]{1,0:T(8,128)(2,1)S(1)} %bitcast.48, bf16[128,384]{1,0:T(8,128)(2,1)S(1)} %bitcast.49), custom_call_target="tpu_custom_call" | custom-call | flops 805306368 | bytes 3145728 | tf_op jit(solution)/shard_map/pallas_call | solution.py:41
  110.9 0.0 copy-start.2
  110.9 0.0 copy-start.3
  110.9 2.4 %collective-permute-start = (bf16[128,768]{1,0:T(8,128)(2,1)S(1)}, bf16[128,768]{1,0:T(8,128)(2,1)S(1)}, u32[]{:S(2)}, u32[]{:S(2)}) collective-permute-start(bf16[128,768]{1,0:T(8,128)(2,1)S(1)} %get-tuple-element.29), channel_id=1, source_target_pairs={{0,4},{4,0},{1,5},{5,1},{2,6},{6,2},{3,7},{7,3},{8,12},{12,8},{9,1... | collective-permute-start | bytes 589832 | tf_op jit(solution)/shard_map/ppermute | solution.py:148
  113.3 0.5 slice.49
  114.5 14.0 %conditional.2 = (bf16[16,128,128]{2,1,0:T(8,128)(2,1)S(1)}) conditional(s32[]{:T(128)} %bitcast.26, () %tuple.24, bf16[16,128,128]{2,1,0:T(8,128)(2,1)} %get-tuple-element.30), branch_computations={%region_0.1_spmd, %region_1.2_spmd} | conditional | bytes 1048584 | solution.py:149
  114.5 14.0 %all_to_all.27 = bf16[16,128,128]{2,1,0:T(8,128)(2,1)S(1)} all-to-all(bf16[16,128,128]{2,1,0:T(8,128)(2,1)} %param.1), channel_id=1, replica_groups=mesh['zh'=8,'zl'=4,'c'=2,'xh'=2,'xl'=2,'y'=4] {'xh','xl','y'}, dimensions={0} | all-to-all | bytes 1048576 | tf_op jit(solution)/shard_map/cond/branch_1_fun/all_to_all | solution.py:133
  128.4 0.0 collective-permute-done
  128.5 0.8 pad_maximum_fusion
  129.3 0.0 all-gather.3.cloned.1.call-update
  129.3 0.0 copy-done.2
  129.4 0.0 copy-done.3
  129.4 65.2 %conditional.3 = (bf16[128,128]{1,0:T(8,128)(2,1)S(1)}) conditional(s32[]{:T(128)} %bitcast.26, () %tuple.27, (bf16[16,128,128]{2,1,0:T(8,128)(2,1)S(1)}, bf16[8,256,128]{2,1,0:T(8,128)(2,1)S(1)}) %tuple.50), branch_computations={%region_2.3_spmd, %region_3.5_spmd} | conditional | flops 67354624 | bytes 5275658 | solution.py:157
  129.4 20.9 %all_to_all.28 = bf16[8,8,32,128]{3,2,1,0:T(8,128)(2,1)S(1)} all-to-all(bf16[8,8,32,128]{3,2,1,0:T(8,128)(2,1)S(1)} %copy.19), channel_id=1, replica_groups=mesh['zh'=8,'zl'=4,'c'=2,'xh'=2,'xl'=2,'y'=4] {'zl','c'}, dimensions={0} | all-to-all | bytes 1048576 | tf_op jit(solution)/shard_map/cond/branch_1_fun/all_to_all | solution.py:137
  150.4 0.3 convolution_convert_fusion
  150.7 43.8 %all_to_all.29 = bf16[8,128,128]{2,1,0:T(8,128)(2,1)S(1)} all-to-all(bf16[8,128,128]{2,1,0:T(8,128)(2,1)S(1)} %convolution_convert_fusion), channel_id=1, replica_groups=mesh['zh'=8,'zl'=4,'c'=2,'xh'=2,'xl'=2,'y'=4] {'zh'}, dimensions={0} | all-to-all | bytes 524288 | tf_op jit(solution)/shard_map/cond/branch_1_fun/all_to_all | solution.py:142
  194.6 0.0 copy-start.5
  194.6 26.7 %all-gather.3.cloned.1.call-done = bf16[2048,768]{1,0:T(8,128)(2,1)} async-done(((bf16[256,768]{1,0:T(8,128)(2,1)}), bf16[2048,768]{1,0:T(8,128)(2,1)}) %all-gather.3.cloned.1.call-update) | async-done | bytes 3145744 | tf_op jit(solution)/shard_map/all_gather | solution.py:156
  221.3 2.5 %fusion.30 = f32[128,768]{1,0:T(8,128)S(1)} fusion(bf16[2048,128]{1,0:T(8,128)(2,1)S(1)} %bitcast.57, bf16[2048,768]{1,0:T(8,128)(2,1)} %all-gather.3.cloned.1.call-done), kind=kOutput, calls=%fused_computation.44 | convolution fusion | flops 402653184 | bytes 4063232 | tf_op jit(solution)/shard_map/dot_general | solution.py:162
  223.8 0.8 slice_bitcast_fusion
  224.6 0.0 copy-done.5
  (12 shorter events, 0.3 us)
Async XLA Ops:
  9.9 7.8 %copy-start.6 = (s32[128,8]{0,1:T(8,128)S(1)}, s32[128,8]{0,1:T(8,128)}, u32[]{:S(2)}) copy-start(s32[128,8]{0,1:T(8,128)} %param.10) | copy-start | bytes 12292
  9.9 7.8 %copy-start.4 = (bf16[128,128]{1,0:T(8,128)(2,1)S(1)}, bf16[128,128]{1,0:T(8,128)(2,1)}, u32[]{:S(2)}) copy-start(bf16[128,128]{1,0:T(8,128)(2,1)} %param.9) | copy-start | bytes 98308
  9.9 59.4 %all-to-all-start.3 = ((bf16[16,128,768]{2,1,0:T(8,128)(2,1)}), bf16[16,128,768]{2,1,0:T(8,128)(2,1)S(1)}, u32[]{:S(2)}, u32[]{:S(2)}) async-start(bf16[16,128,768]{2,1,0:T(8,128)(2,1)} %shard_map.84), calls=%async_computation.3 | async-start | bytes 6291456 | tf_op jit(solution)/shard_map/all_to_all | solution.py:94
  17.5 203.8 %all-gather.3.cloned.1.call-start = ((), (), s32[]{:S(2)}) async-start(), calls=%async_computation.6 | async-start | bytes 3538944 | tf_op jit(solution)/shard_map/all_gather | solution.py:156
  66.9 41.4 %copy-start = (bf16[1,128,384]{2,1,0:T(8,128)(2,1)S(1)}, bf16[1,128,384]{2,1,0:T(8,128)(2,1)}, u32[]{:S(2)}) copy-start(bf16[1,128,384]{2,1,0:T(8,128)(2,1)} %param.13) | copy-start | bytes 294916
  92.4 15.9 %copy-start.1 = (bf16[8,8,32,128]{3,2,0,1:T(8,128)(2,1)}, bf16[8,8,32,128]{3,2,0,1:T(8,128)(2,1)S(1)}, u32[]{:S(2)}) copy-start(bf16[8,8,32,128]{3,2,0,1:T(8,128)(2,1)S(1)} %copy.22) | copy-start | bytes 1572868
  110.9 18.4 %copy-start.2 = (bf16[8,8,32,128]{3,2,0,1:T(8,128)(2,1)S(1)}, bf16[8,8,32,128]{3,2,0,1:T(8,128)(2,1)}, u32[]{:S(2)}) copy-start(bf16[8,8,32,128]{3,2,0,1:T(8,128)(2,1)} %copy-done.1) | copy-start | bytes 1572868
  110.9 18.5 %copy-start.3 = (bf16[8,256,128]{2,1,0:T(8,128)(2,1)S(1)}, bf16[8,256,128]{2,1,0:T(8,128)(2,1)}, u32[]{:S(2)}) copy-start(bf16[8,256,128]{2,1,0:T(8,128)(2,1)} %get-tuple-element.47) | copy-start | bytes 1572868
  110.9 17.6 %collective-permute-start = (bf16[128,768]{1,0:T(8,128)(2,1)S(1)}, bf16[128,768]{1,0:T(8,128)(2,1)S(1)}, u32[]{:S(2)}, u32[]{:S(2)}) collective-permute-start(bf16[128,768]{1,0:T(8,128)(2,1)S(1)} %get-tuple-element.29), channel_id=1, source_target_pairs={{0,4},{4,0},{1,5},{5,1},{2,6},{6,2},{3,7},{7,3},{8,12},{12,8},{9,1... | collective-permute-start | bytes 589832 | tf_op jit(solution)/shard_map/ppermute | solution.py:148
  194.6 30.0 %copy-start.5 = (bf16[128,128]{1,0:T(8,128)(2,1)}, bf16[128,128]{1,0:T(8,128)(2,1)S(1)}, u32[]{:S(2)}) copy-start(bf16[128,128]{1,0:T(8,128)(2,1)S(1)} %get-tuple-element.58) | copy-start | bytes 98308
Sparse Core Ops, SparseCore 0:
  129.4 91.8 all-gather.2

commit v9 on v4

--- a/solution.py
+++ b/solution.py
@@ -9,8 +9,8 @@
 ZL = 4
 
 
-def expert_kernel(rows_ref, weights_ref, grad_ref, hidden_ref, delta_ref, slot_grad_ref):
-    n_dp, _, width_part = rows_ref.shape
+def expert_kernel(rows_ref, weights_ref, grad_ref, hidden_ref, delta_ref):
+    n_dp = rows_ref.shape[0]
     hidden_units = grad_ref.shape[1]
     rows = jnp.concatenate([rows_ref[part] for part in range(n_dp)], axis=1)
     both = jnp.dot(rows, weights_ref[...], preferred_element_type=jnp.float32)
@@ -23,6 +23,27 @@
         grad * up * sigmoid_gate * (1.0 + gate * (1.0 - sigmoid_gate))
     ).astype(jnp.bfloat16)
     delta_ref[:, hidden_units:] = (grad * silu_gate).astype(jnp.bfloat16)
+
+
+def experts(rows, weights, grad):
+    share_rows, hidden_units = grad.shape
+    return pl.pallas_call(
+        expert_kernel,
+        out_shape=(
+            jax.ShapeDtypeStruct((share_rows, hidden_units), jnp.bfloat16),
+            jax.ShapeDtypeStruct((share_rows, 2 * hidden_units), jnp.bfloat16),
+        ),
+        compiler_params=pltpu.CompilerParams(vmem_limit_bytes=32 * 1024 * 1024),
+        cost_estimate=pl.CostEstimate(
+            flops=2 * share_rows * weights.size,
+            bytes_accessed=2 * weights.size,
+            transcendentals=grad.size,
+        ),
+    )(rows, weights, grad)
+
+
+def slot_grad_kernel(delta_ref, weights_ref, slot_grad_ref):
+    n_dp, _, width_part = slot_grad_ref.shape
     delta = delta_ref[...]
     for part in range(n_dp):
         slot_grad_ref[part] = lax.dot_general(
@@ -33,29 +54,81 @@
         ).astype(jnp.bfloat16)
 
 
-def experts(rows, weights, grad):
-    n_dp, share_rows, width_part = rows.shape
-    both_units = weights.shape[1]
-    flops = 4 * share_rows * n_dp * width_part * both_units
-    return pl.pallas_call(
-        expert_kernel,
-        out_shape=(
-            jax.ShapeDtypeStruct((share_rows, both_units // 2), jnp.bfloat16),
-            jax.ShapeDtypeStruct((share_rows, both_units), jnp.bfloat16),
-            jax.ShapeDtypeStruct(rows.shape, jnp.bfloat16),
+def slot_grads(delta, weights, n_dp):
+    share_rows = delta.shape[0]
+    return pl.pallas_call(
+        slot_grad_kernel,
+        out_shape=jax.ShapeDtypeStruct(
+            (n_dp, share_rows, weights.shape[0] // n_dp), jnp.bfloat16
         ),
         compiler_params=pltpu.CompilerParams(vmem_limit_bytes=32 * 1024 * 1024),
         cost_estimate=pl.CostEstimate(
-            flops=flops, bytes_accessed=2 * weights.size, transcendentals=grad.size
-        ),
-    )(rows, weights, grad)
-
-
-def gather_dp(parts, n_dp):
-    copies = [jnp.broadcast_to(part[None], (n_dp, *part.shape)) for part in parts]
-    copies = jnp.concatenate(copies, axis=2) if len(parts) > 1 else copies[0]
-    got = lax.all_to_all(copies, "dp", split_axis=0, concat_axis=0, tiled=True)
-    return got.reshape(-1, got.shape[2])
+            flops=2 * share_rows * weights.size,
+            bytes_accessed=2 * weights.size,
+            transcendentals=0,
+        ),
+    )(delta, weights)
+
+
+def copies_kernel(gate_ref, up_ref, out_ref, rows, sems):
+    hidden_units = gate_ref.shape[2]
+    rows[:, :hidden_units] = gate_ref[0]
+    rows[:, hidden_units:] = up_ref[0]
+    copies = [
+        pltpu.make_async_copy(rows, out_ref.at[part], sems.at[part])
+        for part in range(out_ref.shape[0])
+    ]
+    for copy in copies:
+        copy.start()
+    for copy in copies:
+        copy.wait()
+
+
+def weight_copies(gate_w, up_w, n_dp):
+    _, rows, hidden_units = gate_w.shape
+    return pl.pallas_call(
+        copies_kernel,
+        out_shape=jax.ShapeDtypeStruct((n_dp, rows, 2 * hidden_units), gate_w.dtype),
+        out_specs=pl.BlockSpec(memory_space=pl.ANY),
+        scratch_shapes=[
+            pltpu.VMEM((rows, 2 * hidden_units), gate_w.dtype),
+            pltpu.SemaphoreType.DMA((n_dp,)),
+        ],
+    )(gate_w, up_w)
+
+
+def weight_grad_kernel(rows_ref, delta_ref, gate_grad_ref, up_grad_ref):
+    hidden_units = gate_grad_ref.shape[1]
+
+    @pl.when(pl.program_id(0) == 0)
+    def _():
+        gate_grad_ref[...] = jnp.zeros_like(gate_grad_ref)
+        up_grad_ref[...] = jnp.zeros_like(up_grad_ref)
+
+    both = jnp.dot(rows_ref[...], delta_ref[...], preferred_element_type=jnp.float32)
+    gate_grad_ref[...] += both[:, :hidden_units]
+    up_grad_ref[...] += both[:, hidden_units:]
+
+
+def weight_grads(rows, delta):
+    width_part, slots = rows.shape
+    both_units = delta.shape[1]
+    step = slots // 4
+    out = jax.ShapeDtypeStruct((width_part, both_units // 2), jnp.float32)
+    out_spec = pl.BlockSpec((width_part, both_units // 2), lambda i: (0, 0))
+    return pl.pallas_call(
+        weight_grad_kernel,
+        grid=(slots // step,),
+        in_specs=[
+            pl.BlockSpec((width_part, step), lambda i: (0, i)),
+            pl.BlockSpec((step, both_units), lambda i: (i, 0)),
+        ],
+        out_specs=(out_spec, out_spec),
+        out_shape=(out, out),
+        cost_estimate=pl.CostEstimate(
+            flops=2 * rows.size * both_units, bytes_accessed=2 * delta.size, transcendentals=0
+        ),
+    )(rows, delta)
 
 
 def on_device(tokens, expert_ids, gate_weight, up_weight, hidden_grad):
@@ -68,7 +141,9 @@
     hidden_units = gate_weight.shape[2]
     capacity = share_rows * n_dp // (n_zh * ZL * CORES)
 
-    weights = gather_dp([gate_weight[0], up_weight[0]], n_dp)
+    weights = weight_copies(gate_weight, up_weight, n_dp)
+    weights = lax.all_to_all(weights, "dp", split_axis=0, concat_axis=0, tiled=True)
+    weights = weights.reshape(-1, 2 * hidden_units)
 
     ids_rows = expert_ids.T.astype(jnp.bfloat16)
     sent = jnp.concatenate([tokens, ids_rows], axis=0)
@@ -103,9 +178,10 @@
     own_width = own_width.transpose(1, 0, 2, 3)
     by_share = own_width.reshape(n_dp, share_rows, width_part)
     arrived = lax.all_to_all(by_share, "dp", split_axis=0, concat_axis=0, tiled=True)
-    hidden, both_delta, slot_grad = experts(arrived, weights, hidden_grad[0])
+    hidden, both_delta = experts(arrived, weights, hidden_grad[0])
     all_delta = lax.all_gather(both_delta, "dp", axis=0, tiled=True)
-    def go_back(slot_grad, placer):
+    def go_back(both_delta, weights, placer):
+        slot_grad = slot_grads(both_delta, weights, n_dp)
         back = lax.all_to_all(slot_grad, "dp", split_axis=0, concat_axis=0, tiled=True)
         back = back.reshape(n_zh, n_near, capacity, width_part).transpose(1, 0, 2, 3)
         returned = lax.all_to_all(back, near, split_axis=0, concat_axis=0, tiled=True)
@@ -119,21 +195,12 @@
         return jnp.sum(sums.astype(jnp.float32), axis=0).astype(jnp.bfloat16)
 
     token_grad = lax.cond(
-        expert_ids[0, 0] >= 0, go_back, lambda *_: jnp.zeros_like(tokens), slot_grad, placer
-    )
-
-    both_grad = lax.dot_general(
-        own_width.reshape(n_dp * share_rows, width_part),
-        all_delta,
-        (((0,), (0,)), ((), ())),
-        preferred_element_type=jnp.float32,
-    )
-    return (
-        hidden[None],
-        both_grad[None, :, :hidden_units],
-        both_grad[None, :, hidden_units:],
-        token_grad,
-    )
+        expert_ids[0, 0] >= 0, go_back, lambda *_: jnp.zeros_like(tokens), both_delta, weights, placer
+    )
+
+    rows = by_share.reshape(n_dp * share_rows, width_part).T
+    gate_grad, up_grad = weight_grads(rows, all_delta)
+    return hidden[None], gate_grad[None], up_grad[None], token_grad
 
 
 def solution(mesh):

time: 213 us -> 215 us (level)
  Pallas kernels: 2.53 us -> 10.1 us
  matrix products: 3.36 us -> 0.86 us
    pallas_call x0 -> x3, Pallas kernels: none -> 8.78 us  [the longest x1 4.09 us: weight_grads(): pl.pallas_call(weight_grad_kernel, grid=(slots // step,), in_specs=[pl.Bl...]
    broadcast_in_dim x3 -> x0, local copies, waits for them, and re-layouts: 2.95 us -> none  [the longest x2 2.18 us: gather_dp(): jnp.broadcast_to(part[None], (n_dp, *part.shape))]
    dot_general x1 -> x0, matrix products: 2.51 us -> none  [on_device(): lax.dot_general(own_width.reshape(n_dp * share_rows, width_part), all_del...]
  transfers between devices with their start and end apart: 2 -> 2, of which waited for: 0 -> 0; matrix products, arithmetic and copies ran while one was open for 2% -> 3% of each run, Pallas kernels for 0% -> 1%
where the time goes in v9:
time: 215 us; the launch traced here: 214 us
  blocking collectives  175 us (81%)
  between operations  14.8 us (7%)
  Pallas kernels  10.1 us (5%)
  starting transfers between devices  7.09 us (3%)
  local copies, waits for them, and re-layouts  4.55 us (2%)
    all_to_all x1, blocking collectives, go_back(): lax.all_to_all(token_sum.astype(jnp.bfloat16), 'zh', split_axis=0, concat...  55 us
    all_gather x1, blocking collectives, on_device(): known = lax.all_gather(sent, 'zh', axis=0, tiled=False)  53.4 us
    all_to_all x1, blocking collectives, go_back(): lax.all_to_all(back, near, split_axis=0, concat_axis=0, tiled=True)  18.8 us
    all_to_all x1, blocking collectives, on_device(): lax.all_to_all(by_share, 'dp', split_axis=0, concat_axis=0, tiled=True)  18.2 us
    all_to_all x1, blocking collectives, on_device(): lax.all_to_all(outgoing, near, split_axis=0, concat_axis=0, tiled=True)  16.6 us
    all_to_all x1, blocking collectives, go_back(): lax.all_to_all(slot_grad, 'dp', split_axis=0, concat_axis=0, tiled=True)  13.3 us
    all_to_all x1, starting transfers between devices, on_device(): lax.all_to_all(weights, 'dp', split_axis=0, concat_axis=0, tiled=True)  7.05 us
  transfers between devices with their start and end apart: 2, of which 0 were waited for; matrix products, arithmetic and copies ran while one was open for 3% of the time, Pallas kernels for 1%

profile of v9, /device:TPU:32, one launch (start us, length us, event | category | flops | bytes accessed | tf_op | source)
XLA Modules:
  0.0 214.0 jit_solution(9647751911649762130)
XLA Ops:
  7.2 2.7 %shard_map.84 = bf16[16,128,768]{2,1,0:T(8,128)(2,1)} custom-call(bf16[1,128,384]{2,1,0:T(8,128)(2,1)} %gate_ref.1, bf16[1,128,384]{2,1,0:T(8,128)(2,1)} %up_ref.1), custom_call_target="tpu_custom_call" | custom-call | tf_op jit(solution)/shard_map/pallas_call | solution.py:89
  9.9 0.0 copy-start.5
  9.9 0.0 copy-start.3
  9.9 7.0 %all-to-all-start.3 = ((bf16[16,128,768]{2,1,0:T(8,128)(2,1)}), bf16[16,128,768]{2,1,0:T(8,128)(2,1)S(1)}, u32[]{:S(2)}, u32[]{:S(2)}) async-start(bf16[16,128,768]{2,1,0:T(8,128)(2,1)} %shard_map.84), calls=%async_computation.3 | async-start | bytes 6291456 | tf_op jit(solution)/shard_map/all_to_all | solution.py:145
  17.0 0.0 all-gather.3.cloned.1.call-start
  17.0 0.1 eq.171
  17.1 0.0 copy-done.5
  17.1 0.0 copy-done.3
  17.2 53.4 %all-gather = bf16[1088,128]{1,0:T(8,128)(2,1)S(1)} all-gather(bf16[136,128]{1,0:T(8,128)(2,1)S(1)} %pad_maximum_fusion), channel_id=2, replica_groups=mesh['zh'=8,'zl'=4,'c'=2,'dp'=16] {'zh'}, dimensions={0}, use_global_device_ids=true | all-gather | bytes 313344 | tf_op jit(solution)/shard_map/all_gather | solution.py:150
  70.6 0.0 copy-start
  70.6 0.2 fusion.1
  70.8 1.1 fusion.29
  71.9 0.3 convolution_convert_fusion.1
  72.2 0.8 copy.27
  73.0 0.0 all-to-all-done.3
  73.0 16.6 %all_to_all.30 = bf16[8,8,32,128]{3,2,1,0:T(8,128)(2,1)S(1)} all-to-all(bf16[8,8,32,128]{3,2,1,0:T(8,128)(2,1)} %bitcast.52), channel_id=1, replica_groups=mesh['zh'=8,'zl'=4,'c'=2,'dp'=16] {'zl','c'}, dimensions={0} | all-to-all | bytes 1048576 | tf_op jit(solution)/shard_map/all_to_all | solution.py:177
  89.6 0.0 copy-start.1
  89.6 0.8 copy-done.1
  90.4 18.2 %all_to_all.31.rows_ref = bf16[16,128,128]{2,1,0:T(8,128)(2,1)S(1)} all-to-all(bf16[16,128,128]{2,1,0:T(8,128)(2,1)S(1)} %bitcast.49), channel_id=1, replica_groups=mesh['zh'=8,'zl'=4,'c'=2,'dp'=16] {'dp'}, dimensions={0} | all-to-all | bytes 1048576 | tf_op jit(solution)/shard_map/all_to_all | solution.py:180
  108.7 0.0 copy-done
  108.7 1.3 shard_map.85
  110.0 0.0 all-gather.3.cloned.1.call-update
  110.0 0.5 slice.43
  111.2 2.0 copy.19
  113.2 89.8 %conditional.1 = (bf16[128,128]{1,0:T(8,128)(2,1)S(1)}) conditional(s32[]{:T(128)} %bitcast.28, () %tuple.16, (bf16[128,768]{1,0:T(8,128)(2,1)}, bf16[2048,768]{1,0:T(8,128)(2,1)S(1)}, bf16[8,256,128]{2,1,0:T(8,128)(2,1)}) %tuple.34), branch_computations={%region_0.1_spmd, %region_1.3_spmd} | conditional | flops 470007808 | bytes 11632678 | solution.py:197
  113.2 0.0 copy-start.2
  113.2 2.0 branch_1_fun.1
  115.2 13.3 %all_to_all.27 = bf16[16,128,128]{2,1,0:T(8,128)(2,1)S(1)} all-to-all(bf16[16,128,128]{2,1,0:T(8,128)(2,1)S(1)} %branch_1_fun.1), channel_id=1, replica_groups=mesh['zh'=8,'zl'=4,'c'=2,'dp'=16] {'dp'}, dimensions={0} | all-to-all | bytes 1048576 | tf_op jit(solution)/shard_map/cond/branch_1_fun/all_to_all | solution.py:185
  128.6 18.8 %all_to_all.28 = bf16[8,8,32,128]{3,2,1,0:T(8,128)(2,1)S(1)} all-to-all(bf16[8,8,32,128]{3,2,1,0:T(8,128)(2,1)S(1)} %bitcast.55), channel_id=1, replica_groups=mesh['zh'=8,'zl'=4,'c'=2,'dp'=16] {'zl','c'}, dimensions={0} | all-to-all | bytes 1048576 | tf_op jit(solution)/shard_map/cond/branch_1_fun/all_to_all | solution.py:187
  147.5 0.0 copy-done.2
  147.5 0.3 fusion
  147.8 55.0 %all_to_all.29 = bf16[8,128,128]{1,2,0:T(8,128)(2,1)S(1)} all-to-all(bf16[8,128,128]{1,2,0:T(8,128)(2,1)S(1)} %fusion), channel_id=1, replica_groups=mesh['zh'=8,'zl'=4,'c'=2,'dp'=16] {'zh'}, dimensions={0} | all-to-all | bytes 524288 | tf_op jit(solution)/shard_map/cond/branch_1_fun/all_to_all | solution.py:192
  202.9 0.1 copy.23
  203.0 0.0 copy-start.4
  203.0 0.0 all-gather.3.cloned.1.call-done.delta_ref
  203.1 4.1 %shard_map.86 = (f32[128,384]{1,0:T(8,128)}, f32[128,384]{1,0:T(8,128)}) custom-call(bf16[128,2048]{1,0:T(8,128)(2,1)} %bitcast.51, bf16[2048,768]{1,0:T(8,128)(2,1)} %all-gather.3.cloned.1.call-done.delta_ref), custom_call_target="tpu_custom_call" | custom-call | flops 402653184 | bytes 3145728 | tf_op jit(solution)/shard_map/pallas_call | solution.py:119
  207.2 0.0 copy-done.4
  (10 shorter events, 0.2 us)
Async XLA Ops:
  9.9 7.2 %copy-start.5 = (s32[128,8]{0,1:T(8,128)S(1)}, s32[128,8]{0,1:T(8,128)}, u32[]{:S(2)}) copy-start(s32[128,8]{0,1:T(8,128)} %param.8) | copy-start | bytes 12292
  9.9 7.2 %copy-start.3 = (bf16[128,128]{1,0:T(8,128)(2,1)S(1)}, bf16[128,128]{1,0:T(8,128)(2,1)}, u32[]{:S(2)}) copy-start(bf16[128,128]{1,0:T(8,128)(2,1)} %param.7) | copy-start | bytes 98308
  9.9 63.1 %all-to-all-start.3 = ((bf16[16,128,768]{2,1,0:T(8,128)(2,1)}), bf16[16,128,768]{2,1,0:T(8,128)(2,1)S(1)}, u32[]{:S(2)}, u32[]{:S(2)}) async-start(bf16[16,128,768]{2,1,0:T(8,128)(2,1)} %shard_map.84), calls=%async_computation.3 | async-start | bytes 6291456 | tf_op jit(solution)/shard_map/all_to_all | solution.py:145
  17.0 186.1 %all-gather.3.cloned.1.call-start = ((), (), s32[]{:S(2)}) async-start(), calls=%async_computation.6 | async-start | bytes 3342336 | tf_op jit(solution)/shard_map/all_gather | solution.py:182
  70.6 38.1 %copy-start = (bf16[1,128,384]{2,1,0:T(8,128)(2,1)S(1)}, bf16[1,128,384]{2,1,0:T(8,128)(2,1)}, u32[]{:S(2)}) copy-start(bf16[1,128,384]{2,1,0:T(8,128)(2,1)} %param.11) | copy-start | bytes 294916
  89.6 0.8 copy-start.1
  113.2 34.2 %copy-start.2 = (bf16[8,256,128]{2,1,0:T(8,128)(2,1)S(1)}, bf16[8,256,128]{2,1,0:T(8,128)(2,1)}, u32[]{:S(2)}) copy-start(bf16[8,256,128]{2,1,0:T(8,128)(2,1)} %get-tuple-element.11) | copy-start | bytes 1572868 | tf_op jit(solution)/shard_map/cond
  203.0 4.1 %copy-start.4 = (bf16[128,128]{1,0:T(8,128)(2,1)}, bf16[128,128]{1,0:T(8,128)(2,1)S(1)}, u32[]{:S(2)}) copy-start(bf16[128,128]{1,0:T(8,128)(2,1)S(1)} %get-tuple-element.32) | copy-start | bytes 98308
Sparse Core Ops, SparseCore 0:
  110.2 76.5 all-gather.2

commit v10 on v9

--- a/solution.py
+++ b/solution.py
@@ -95,40 +95,6 @@
             pltpu.SemaphoreType.DMA((n_dp,)),
         ],
     )(gate_w, up_w)
-
-
-def weight_grad_kernel(rows_ref, delta_ref, gate_grad_ref, up_grad_ref):
-    hidden_units = gate_grad_ref.shape[1]
-
-    @pl.when(pl.program_id(0) == 0)
-    def _():
-        gate_grad_ref[...] = jnp.zeros_like(gate_grad_ref)
-        up_grad_ref[...] = jnp.zeros_like(up_grad_ref)
-
-    both = jnp.dot(rows_ref[...], delta_ref[...], preferred_element_type=jnp.float32)
-    gate_grad_ref[...] += both[:, :hidden_units]
-    up_grad_ref[...] += both[:, hidden_units:]
-
-
-def weight_grads(rows, delta):
-    width_part, slots = rows.shape
-    both_units = delta.shape[1]
-    step = slots // 4
-    out = jax.ShapeDtypeStruct((width_part, both_units // 2), jnp.float32)
-    out_spec = pl.BlockSpec((width_part, both_units // 2), lambda i: (0, 0))
-    return pl.pallas_call(
-        weight_grad_kernel,
-        grid=(slots // step,),
-        in_specs=[
-            pl.BlockSpec((width_part, step), lambda i: (0, i)),
-            pl.BlockSpec((step, both_units), lambda i: (i, 0)),
-        ],
-        out_specs=(out_spec, out_spec),
-        out_shape=(out, out),
-        cost_estimate=pl.CostEstimate(
-            flops=2 * rows.size * both_units, bytes_accessed=2 * delta.size, transcendentals=0
-        ),
-    )(rows, delta)
 
 
 def on_device(tokens, expert_ids, gate_weight, up_weight, hidden_grad):
@@ -198,9 +164,18 @@
         expert_ids[0, 0] >= 0, go_back, lambda *_: jnp.zeros_like(tokens), both_delta, weights, placer
     )
 
-    rows = by_share.reshape(n_dp * share_rows, width_part).T
-    gate_grad, up_grad = weight_grads(rows, all_delta)
-    return hidden[None], gate_grad[None], up_grad[None], token_grad
+    both_grad = lax.dot_general(
+        own_width.reshape(n_dp * share_rows, width_part),
+        all_delta,
+        (((0,), (0,)), ((), ())),
+        preferred_element_type=jnp.float32,
+    )
+    return (
+        hidden[None],
+        both_grad[None, :, :hidden_units],
+        both_grad[None, :, hidden_units:],
+        token_grad,
+    )
 
 
 def solution(mesh):

time: 215 us -> 212 us (0.986)
  Pallas kernels: 10.1 us -> 6.02 us
  matrix products: 0.86 us -> 3.54 us
    pallas_call x1 -> x0, Pallas kernels: 4.09 us -> none  [weight_grads(): pl.pallas_call(weight_grad_kernel, grid=(slots // step,), in_specs=[pl.Bl...]
    dot_general x0 -> x1, matrix products: none -> 2.69 us  [on_device(): lax.dot_general(own_width.reshape(n_dp * share_rows, width_part), all_del...]
  transfers between devices with their start and end apart: 2 -> 2, of which waited for: 0 -> 0; matrix products, arithmetic and copies ran while one was open for 3% -> 2% of each run, Pallas kernels for 1% -> 1%
where the time goes in v10:
time: 212 us; the launch traced here: 211 us
  blocking collectives  175 us (83%)
  between operations  14.8 us (7%)
  starting transfers between devices  7.09 us (3%)
  Pallas kernels  6.02 us (3%)
  matrix products  3.54 us (2%)
  local copies, waits for them, and re-layouts  3.27 us (2%)
    all_to_all x1, blocking collectives, go_back(): lax.all_to_all(token_sum.astype(jnp.bfloat16), 'zh', split_axis=0, concat...  55.1 us
    all_gather x1, blocking collectives, on_device(): known = lax.all_gather(sent, 'zh', axis=0, tiled=False)  53.4 us
    all_to_all x1, blocking collectives, go_back(): lax.all_to_all(back, near, split_axis=0, concat_axis=0, tiled=True)  18.8 us
    all_to_all x1, blocking collectives, on_device(): lax.all_to_all(by_share, 'dp', split_axis=0, concat_axis=0, tiled=True)  18.2 us
    all_to_all x1, blocking collectives, on_device(): lax.all_to_all(outgoing, near, split_axis=0, concat_axis=0, tiled=True)  16.6 us
    all_to_all x1, blocking collectives, go_back(): lax.all_to_all(slot_grad, 'dp', split_axis=0, concat_axis=0, tiled=True)  13.4 us
    all_to_all x1, starting transfers between devices, on_device(): lax.all_to_all(weights, 'dp', split_axis=0, concat_axis=0, tiled=True)  7.05 us
  transfers between devices with their start and end apart: 2, of which 0 were waited for; matrix products, arithmetic and copies ran while one was open for 2% of the time, Pallas kernels for 1%

profile of v10, /device:TPU:32, one launch (start us, length us, event | category | flops | bytes accessed | tf_op | source)
XLA Modules:
  0.0 211.4 jit_solution(14871001730523991879)
XLA Ops:
  7.2 2.7 %shard_map.84 = bf16[16,128,768]{2,1,0:T(8,128)(2,1)} custom-call(bf16[1,128,384]{2,1,0:T(8,128)(2,1)} %gate_ref.1, bf16[1,128,384]{2,1,0:T(8,128)(2,1)} %up_ref.1), custom_call_target="tpu_custom_call" | custom-call | tf_op jit(solution)/shard_map/pallas_call | solution.py:89
  9.9 0.0 copy-start.5
  9.9 0.0 copy-start.3
  9.9 7.0 %all-to-all-start.3 = ((bf16[16,128,768]{2,1,0:T(8,128)(2,1)}), bf16[16,128,768]{2,1,0:T(8,128)(2,1)S(1)}, u32[]{:S(2)}, u32[]{:S(2)}) async-start(bf16[16,128,768]{2,1,0:T(8,128)(2,1)} %shard_map.84), calls=%async_computation.3 | async-start | bytes 6291456 | tf_op jit(solution)/shard_map/all_to_all | solution.py:111
  17.0 0.0 all-gather.3.cloned.1.call-start
  17.0 0.1 eq.171
  17.1 0.0 copy-done.5
  17.1 0.0 copy-done.3
  17.2 53.4 %all-gather = bf16[1088,128]{1,0:T(8,128)(2,1)S(1)} all-gather(bf16[136,128]{1,0:T(8,128)(2,1)S(1)} %pad_maximum_fusion), channel_id=2, replica_groups=mesh['zh'=8,'zl'=4,'c'=2,'dp'=16] {'zh'}, dimensions={0}, use_global_device_ids=true | all-gather | bytes 313344 | tf_op jit(solution)/shard_map/all_gather | solution.py:116
  70.6 0.0 copy-start
  70.6 0.2 fusion.1
  70.8 1.1 fusion.29
  71.9 0.3 convolution_convert_fusion.1
  72.2 0.8 copy.29
  73.0 0.0 all-to-all-done.3
  73.0 16.6 %all_to_all.30 = bf16[8,8,32,128]{3,2,1,0:T(8,128)(2,1)S(1)} all-to-all(bf16[8,8,32,128]{3,2,1,0:T(8,128)(2,1)} %bitcast.54), channel_id=1, replica_groups=mesh['zh'=8,'zl'=4,'c'=2,'dp'=16] {'zl','c'}, dimensions={0} | all-to-all | bytes 1048576 | tf_op jit(solution)/shard_map/all_to_all | solution.py:143
  89.6 0.0 copy-start.1
  89.6 0.8 copy-done.1
  90.4 18.2 %all_to_all.31.rows_ref = bf16[16,128,128]{2,1,0:T(8,128)(2,1)S(1)} all-to-all(bf16[16,128,128]{2,1,0:T(8,128)(2,1)S(1)} %bitcast.52), channel_id=1, replica_groups=mesh['zh'=8,'zl'=4,'c'=2,'dp'=16] {'dp'}, dimensions={0} | all-to-all | bytes 1048576 | tf_op jit(solution)/shard_map/all_to_all | solution.py:146
  108.7 0.0 copy-done
  108.7 1.3 shard_map.85
  110.0 0.0 all-gather.3.cloned.1.call-update
  110.0 0.5 slice.51
  111.2 89.9 %conditional.1 = (bf16[128,128]{1,0:T(8,128)(2,1)S(1)}) conditional(s32[]{:T(128)} %bitcast.27, () %tuple.16, (bf16[128,768]{1,0:T(8,128)(2,1)}, bf16[2048,768]{1,0:T(8,128)(2,1)S(1)}, bf16[8,256,128]{2,1,0:T(8,128)(2,1)}) %tuple.36), branch_computations={%region_0.1_spmd, %region_1.3_spmd} | conditional | flops 470007808 | bytes 11632678 | solution.py:163
  111.2 0.0 copy-start.2
  111.2 2.0 branch_1_fun.1
  113.2 13.4 %all_to_all.27 = bf16[16,128,128]{2,1,0:T(8,128)(2,1)S(1)} all-to-all(bf16[16,128,128]{2,1,0:T(8,128)(2,1)S(1)} %branch_1_fun.1), channel_id=1, replica_groups=mesh['zh'=8,'zl'=4,'c'=2,'dp'=16] {'dp'}, dimensions={0} | all-to-all | bytes 1048576 | tf_op jit(solution)/shard_map/cond/branch_1_fun/all_to_all | solution.py:151
  126.6 18.8 %all_to_all.28 = bf16[8,8,32,128]{3,2,1,0:T(8,128)(2,1)S(1)} all-to-all(bf16[8,8,32,128]{3,2,1,0:T(8,128)(2,1)S(1)} %bitcast.57), channel_id=1, replica_groups=mesh['zh'=8,'zl'=4,'c'=2,'dp'=16] {'zl','c'}, dimensions={0} | all-to-all | bytes 1048576 | tf_op jit(solution)/shard_map/cond/branch_1_fun/all_to_all | solution.py:153
  145.4 0.0 copy-done.2
  145.4 0.3 fusion
  145.8 55.1 %all_to_all.29 = bf16[8,128,128]{1,2,0:T(8,128)(2,1)S(1)} all-to-all(bf16[8,128,128]{1,2,0:T(8,128)(2,1)S(1)} %fusion), channel_id=1, replica_groups=mesh['zh'=8,'zl'=4,'c'=2,'dp'=16] {'zh'}, dimensions={0} | all-to-all | bytes 524288 | tf_op jit(solution)/shard_map/cond/branch_1_fun/all_to_all | solution.py:158
  201.0 0.1 copy.25
  201.1 0.0 copy-start.4
  201.1 0.0 all-gather.3.cloned.1.call-done
  201.1 2.7 %fusion.31 = f32[128,768]{1,0:T(8,128)S(1)} fusion(bf16[2048,128]{1,0:T(8,128)(2,1)} %bitcast.53, bf16[2048,768]{1,0:T(8,128)(2,1)} %all-gather.3.cloned.1.call-done), kind=kOutput, calls=%fused_computation.43 | convolution fusion | flops 402653184 | bytes 4063232 | tf_op jit(solution)/shard_map/dot_general | solution.py:167
  203.8 0.8 slice_bitcast_fusion
  204.6 0.0 copy-done.4
  (10 shorter events, 0.2 us)
Async XLA Ops:
  9.9 7.2 %copy-start.5 = (s32[128,8]{0,1:T(8,128)S(1)}, s32[128,8]{0,1:T(8,128)}, u32[]{:S(2)}) copy-start(s32[128,8]{0,1:T(8,128)} %param.8) | copy-start | bytes 12292
  9.9 7.2 %copy-start.3 = (bf16[128,128]{1,0:T(8,128)(2,1)S(1)}, bf16[128,128]{1,0:T(8,128)(2,1)}, u32[]{:S(2)}) copy-start(bf16[128,128]{1,0:T(8,128)(2,1)} %param.7) | copy-start | bytes 98308
  9.9 63.1 %all-to-all-start.3 = ((bf16[16,128,768]{2,1,0:T(8,128)(2,1)}), bf16[16,128,768]{2,1,0:T(8,128)(2,1)S(1)}, u32[]{:S(2)}, u32[]{:S(2)}) async-start(bf16[16,128,768]{2,1,0:T(8,128)(2,1)} %shard_map.84), calls=%async_computation.3 | async-start | bytes 6291456 | tf_op jit(solution)/shard_map/all_to_all | solution.py:111
  17.0 184.1 %all-gather.3.cloned.1.call-start = ((), (), s32[]{:S(2)}) async-start(), calls=%async_computation.6 | async-start | bytes 3342336 | tf_op jit(solution)/shard_map/all_gather | solution.py:148
  70.6 38.1 %copy-start = (bf16[1,128,384]{2,1,0:T(8,128)(2,1)S(1)}, bf16[1,128,384]{2,1,0:T(8,128)(2,1)}, u32[]{:S(2)}) copy-start(bf16[1,128,384]{2,1,0:T(8,128)(2,1)} %param.11) | copy-start | bytes 294916
  89.6 0.8 copy-start.1
  111.2 34.2 %copy-start.2 = (bf16[8,256,128]{2,1,0:T(8,128)(2,1)S(1)}, bf16[8,256,128]{2,1,0:T(8,128)(2,1)}, u32[]{:S(2)}) copy-start(bf16[8,256,128]{2,1,0:T(8,128)(2,1)} %get-tuple-element.11) | copy-start | bytes 1572868 | tf_op jit(solution)/shard_map/cond
  201.1 3.5 %copy-start.4 = (bf16[128,128]{1,0:T(8,128)(2,1)}, bf16[128,128]{1,0:T(8,128)(2,1)S(1)}, u32[]{:S(2)}) copy-start(bf16[128,128]{1,0:T(8,128)(2,1)S(1)} %get-tuple-element.32) | copy-start | bytes 98308
Sparse Core Ops, SparseCore 0:
  110.1 76.5 all-gather.2
